TPU v7x, 32 devices: a whole 2x2x4 slice. The times are simulated.
32 devices in a mesh: groups: 2 (over y), chan: 8 (over z, x), pair: 2 (over core).
Axes of the slice: x: 2, y: 2, z: 4, core: 2. Of those that a mesh axis runs over, the one named last changes fastest.
Arguments:
- raw: bfloat16 [1024, 1, 12000], P(('groups', 'chan')), parts along dimension 0, may hold values from -6 to 6
- live_index: int32 [16, 64], P(('groups', 'chan')), parts along dimension 0, may hold values from 0 to 63, each once within a row
- live_count: int32 [16], P('groups'), parts along dimension 0, may hold values from 1 to 64, 256 in all
Outputs:
- correlation: bfloat16 [6, 1024, 512], P('pair', ('groups', 'chan')), parts along dimension 1
There are 2 independent parts, one for each index of `groups`. A program takes and returns all parts, laid end to end along the dimension named above; each array names one. Nothing has to cross between parts.
Inputs may be any that keep to these rules, and one draw needn't show every extreme that they name: `live_index`: each block's row is a permutation of the raw channels of that block. `live_count`: live slots of each block; they sum to 256, and some block fills all 64 slots.
All inputs are finite; a program needn't handle non-finite values.
Results may differ from a plain program's by a relative error of at most 0.001.
The roundings to bfloat16 on the way count: a program that leaves them out, or rounds other values in their place, can miss the bound.
Values may be sent and summed in bfloat16 or wider, within the bound.
No kernel may reach another device: no remote copies, remote signals or barrier semaphores. Data moves between devices by JAX's collectives and lax.ppermute only.
A program may use at most 128 MiB of HBM per device.

v0:
```python
import jax
import jax.numpy as jnp
from jax import lax
from jax.sharding import PartitionSpec as P

S = 12000
NB = 448
NSEG = 1
L = 6
LSTEP = 125
F0 = 60


water_level = 0.1


def lag_weights(lag_ids, bin_ids):
    band_taper = 0.5 - 0.5 * jnp.cos(2.0 * jnp.pi * (bin_ids.astype(jnp.float32) + 0.5) / NB)
    phase_int = (F0 + bin_ids)[None, :] * lag_ids[:, None] % S
    waves = jnp.cos(phase_int.astype(jnp.float32) * (2.0 * jnp.pi / S))
    return band_taper[None, :] * waves / jnp.sqrt(jnp.float32(NSEG * NB))


def spectra_of(picked_rows, bins, samples):
    block_len = samples // 8

    def add_block(block_id, running):
        sample_ids = block_id * block_len + jnp.arange(block_len, dtype=jnp.int32)
        phase_int = sample_ids[:, None] * (F0 + bins)[None, :] % samples
        angles = phase_int.astype(jnp.float32) * (2.0 * jnp.pi / samples)
        dft_table = jnp.concatenate([jnp.cos(angles), -jnp.sin(angles)], axis=1).astype(
            jnp.bfloat16
        )
        sample_blk = lax.dynamic_slice_in_dim(picked_rows, block_id * block_len, block_len, 1)
        return running + jnp.dot(sample_blk, dft_table, preferred_element_type=jnp.float32)

    start_acc = jnp.zeros((picked_rows.shape[0], 2 * bins.shape[0]), jnp.float32)
    return lax.fori_loop(0, 8, add_block, start_acc)


def whiten(spectrum, band_power):
    magnitude = spectrum[:, :, 0] ** 2 + spectrum[:, :, 1] ** 2
    denom = jnp.sqrt(magnitude + water_level * band_power[:, :, None] + 1e-06)
    return (spectrum / denom[:, :, None, :]).astype(jnp.bfloat16)


def correlate(lag_rows, columns):
    product = lax.dot_general(
        lag_rows, columns, (((1,), (1,)), ((), ())), preferred_element_type=jnp.float32
    )
    return product.astype(jnp.bfloat16)


def shards(raw, live_index, live_count):
    slot_count = raw.shape[0]
    seg_count = raw.shape[1]
    samples = raw.shape[2]
    pair_count = lax.axis_size("pair")
    pair_index = lax.axis_index("pair")
    chan_index = lax.axis_index("chan")
    local_bins = NB // pair_count
    lag_share = L // pair_count
    live_slots = live_count[chan_index]
    slot_ids = jnp.arange(slot_count, dtype=jnp.int32)
    chosen = jnp.take(raw, live_index[0], axis=0)
    picked = jnp.where((slot_ids < live_slots)[:, None, None], chosen, jnp.zeros((), raw.dtype))
    picked_rows = picked.reshape(slot_count * seg_count, samples)
    own_bins = pair_index * local_bins + jnp.arange(local_bins, dtype=jnp.int32)
    spectrum = spectra_of(picked_rows, own_bins, samples).reshape(
        slot_count, seg_count, 2, local_bins
    )
    band_power = lax.psum(jnp.sum(spectrum * spectrum, axis=(2, 3)), "pair") / NB
    own_half = whiten(spectrum, band_power)
    own_full = lax.all_gather(own_half, "pair", axis=3, tiled=True)
    own_lags = (pair_index * lag_share + jnp.arange(lag_share, dtype=jnp.int32)) * LSTEP
    weights = lag_weights(own_lags, jnp.arange(NB, dtype=jnp.int32))
    lag_rows = (own_full[None] * weights[:, None, None, None, :]).astype(jnp.bfloat16)
    lag_rows = lag_rows.reshape(lag_share * slot_count, -1)
    own_rows = own_full.reshape(slot_count, -1)
    product = correlate(lag_rows, lax.all_gather(own_rows, "chan", axis=0, tiled=True))
    correlation = product.reshape(lag_share, slot_count, -1)
    return correlation


def solution(mesh):
    return jax.shard_map(
        shards,
        mesh=mesh,
        in_specs=(P(("groups", "chan"), None, None), P(("groups", "chan"), None), P("groups")),
        out_specs=P("pair", ("groups", "chan"), None),
        check_vma=False,
    )
```

profile of v0, /device:TPU:0, one launch (start us, length us, event | category | flops | bytes accessed | tf_op | source)
XLA Modules:
  0.0 118.7 jit_solution(9967840530059940738)
XLA Ops:
  0.0 0.0 copy-start
  0.0 1.4 %dynamic_slice.13 = s32[1]{0:T(128)} dynamic-slice(s32[8]{0:T(128)} %param.7, s32[]{:T(128)S(6)} %select_n.73), dynamic_slice_sizes={1} | dynamic-slice | bytes 12 | tf_op jit(solution)/shard_map/dynamic_slice | solution.py:63
  1.4 1.3 %compare_and_fusion = (pred[64]{0:T(512)(128)(4,1)S(1)}, pred[64]{0:T(512)(128)(4,1)S(1)}) fusion(s32[1,64]{1,0:T(1,128)} %param.6, s32[]{:T(128)} %bitcast), kind=kLoop, calls=%fused_computation.49 | loop fusion | flops 448 | bytes 388 | tf_op jit(solution)/shard_map/jit(_take)/and | solution.py:65
  2.7 0.7 fusion.30
  3.3 0.0 copy-done
  3.3 1.5 %gather_fusion = bf16[64,12000]{1,0:T(8,128)(2,1)S(1)} fusion(bf16[64,12000]{1,0:T(8,128)(2,1)S(1)} %bitcast.21, s32[1024]{0:T(1024)S(1)} %pad_clamp_fusion), kind=kCustom, calls=%fused_computation | custom fusion | bytes 3072256 | tf_op jit(solution)/shard_map/jit(_take)/gather | solution.py:65
  4.9 1.4 %select_select_fusion = bf16[64,12000]{1,0:T(8,128)(2,1)} fusion(bf16[64,12000]{1,0:T(8,128)(2,1)S(1)} %gather_fusion, pred[64]{0:T(512)(128)(4,1)S(1)} %get-tuple-element.147, pred[64]{0:T(512)(128)(4,1)S(1)} %get-tuple-element.148), kind=kLoop, calls=%fused_computation.21 | loop fusion | flops 1536000 | bytes 3072128 | tf_op jit(solution)/shard_map/jit(_where)/select_n | solution.py:66
  6.3 70.3 %while.16 = (s32[]{:T(128)}, f32[64,448]{1,0:T(8,128)S(1)}, bf16[64,12000]{1,0:T(8,128)(2,1)}, s32[]{:T(128)}, s32[]{:T(128)}, /*index=5*/s32[]{:T(128)}, s32[]{:T(128)}, s32[]{:T(128)}) while((s32[]{:T(128)}, f32[64,448]{1,0:T(8,128)S(1)}, bf16[64,12000]{1,0:T(8,128)(2,1)}, s32[]{:T(128)}, s32[]{:T(128)}, /*index=5*/s32[]{:T(128)}, ...), condition=%wide.region_1.2_spmd.clone, body=%wide.region_0.1_spmd.clone.sunk | while | flops 92795296 | bytes 3127929 | solution.py:38
  6.3 7.1 %cosine_convert_fusion.2 = (bf16[1500,224]{1,0:T(8,128)(2,1)S(1)}, bf16[1500,224]{1,0:T(8,128)(2,1)S(1)}) fusion(s32[224]{0:T(256)S(1)} %add_add_fusion.2, s32[1500]{0:T(1024)S(1)} %iota_add_fusion.3), kind=kLoop, calls=%fused_computation.10.clone.1 | loop fusion | flops 4032000 | bytes 1350896 | tf_op jit(solution)/shard_map/convert
  13.4 1.6 %fusion.39 = f32[64,448]{1,0:T(8,128)S(1)} fusion(bf16[1500,224]{1,0:T(8,128)(2,1)S(1)} %get-tuple-element.176, bf16[1500,224]{1,0:T(8,128)(2,1)S(1)} %get-tuple-element.177, bf16[64,12000]{1,0:T(8,128)(2,1)} %get-tuple-element.196, s32[]{:T(128)S(6)} %select_n.112, f32[64,448]{1,0:T(8,128)S(1)} %get-tuple-element.187, pred[]{:T(512)S(6)} %compare.3), kind=kOutput, calls=%fused_computation.15.clone.1 | convolution fusion | flops 88761344 | bytes 1769989 | tf_op jit(solution)/shard_map/while/body/eval_jaxpr/dot_general | solution.py:35
  15.1 7.1 %cosine_convert_fusion.2 = (bf16[1500,224]{1,0:T(8,128)(2,1)S(1)}, bf16[1500,224]{1,0:T(8,128)(2,1)S(1)}) fusion(s32[224]{0:T(256)S(1)} %add_add_fusion.2, s32[1500]{0:T(1024)S(1)} %iota_add_fusion.3), kind=kLoop, calls=%fused_computation.10.clone.1 | loop fusion | flops 4032000 | bytes 1350896 | tf_op jit(solution)/shard_map/convert
  22.2 1.6 %fusion.39 = f32[64,448]{1,0:T(8,128)S(1)} fusion(bf16[1500,224]{1,0:T(8,128)(2,1)S(1)} %get-tuple-element.176, bf16[1500,224]{1,0:T(8,128)(2,1)S(1)} %get-tuple-element.177, bf16[64,12000]{1,0:T(8,128)(2,1)} %get-tuple-element.196, s32[]{:T(128)S(6)} %select_n.112, f32[64,448]{1,0:T(8,128)S(1)} %get-tuple-element.187, pred[]{:T(512)S(6)} %compare.3), kind=kOutput, calls=%fused_computation.15.clone.1 | convolution fusion | flops 88761344 | bytes 1769989 | tf_op jit(solution)/shard_map/while/body/eval_jaxpr/dot_general | solution.py:35
  23.9 7.1 %cosine_convert_fusion.2 = (bf16[1500,224]{1,0:T(8,128)(2,1)S(1)}, bf16[1500,224]{1,0:T(8,128)(2,1)S(1)}) fusion(s32[224]{0:T(256)S(1)} %add_add_fusion.2, s32[1500]{0:T(1024)S(1)} %iota_add_fusion.3), kind=kLoop, calls=%fused_computation.10.clone.1 | loop fusion | flops 4032000 | bytes 1350896 | tf_op jit(solution)/shard_map/convert
  31.0 1.6 %fusion.39 = f32[64,448]{1,0:T(8,128)S(1)} fusion(bf16[1500,224]{1,0:T(8,128)(2,1)S(1)} %get-tuple-element.176, bf16[1500,224]{1,0:T(8,128)(2,1)S(1)} %get-tuple-element.177, bf16[64,12000]{1,0:T(8,128)(2,1)} %get-tuple-element.196, s32[]{:T(128)S(6)} %select_n.112, f32[64,448]{1,0:T(8,128)S(1)} %get-tuple-element.187, pred[]{:T(512)S(6)} %compare.3), kind=kOutput, calls=%fused_computation.15.clone.1 | convolution fusion | flops 88761344 | bytes 1769989 | tf_op jit(solution)/shard_map/while/body/eval_jaxpr/dot_general | solution.py:35
  32.6 7.1 %cosine_convert_fusion.2 = (bf16[1500,224]{1,0:T(8,128)(2,1)S(1)}, bf16[1500,224]{1,0:T(8,128)(2,1)S(1)}) fusion(s32[224]{0:T(256)S(1)} %add_add_fusion.2, s32[1500]{0:T(1024)S(1)} %iota_add_fusion.3), kind=kLoop, calls=%fused_computation.10.clone.1 | loop fusion | flops 4032000 | bytes 1350896 | tf_op jit(solution)/shard_map/convert
  39.8 1.6 %fusion.39 = f32[64,448]{1,0:T(8,128)S(1)} fusion(bf16[1500,224]{1,0:T(8,128)(2,1)S(1)} %get-tuple-element.176, bf16[1500,224]{1,0:T(8,128)(2,1)S(1)} %get-tuple-element.177, bf16[64,12000]{1,0:T(8,128)(2,1)} %get-tuple-element.196, s32[]{:T(128)S(6)} %select_n.112, f32[64,448]{1,0:T(8,128)S(1)} %get-tuple-element.187, pred[]{:T(512)S(6)} %compare.3), kind=kOutput, calls=%fused_computation.15.clone.1 | convolution fusion | flops 88761344 | bytes 1769989 | tf_op jit(solution)/shard_map/while/body/eval_jaxpr/dot_general | solution.py:35
  41.4 7.1 %cosine_convert_fusion.2 = (bf16[1500,224]{1,0:T(8,128)(2,1)S(1)}, bf16[1500,224]{1,0:T(8,128)(2,1)S(1)}) fusion(s32[224]{0:T(256)S(1)} %add_add_fusion.2, s32[1500]{0:T(1024)S(1)} %iota_add_fusion.3), kind=kLoop, calls=%fused_computation.10.clone.1 | loop fusion | flops 4032000 | bytes 1350896 | tf_op jit(solution)/shard_map/convert
  48.5 1.6 %fusion.39 = f32[64,448]{1,0:T(8,128)S(1)} fusion(bf16[1500,224]{1,0:T(8,128)(2,1)S(1)} %get-tuple-element.176, bf16[1500,224]{1,0:T(8,128)(2,1)S(1)} %get-tuple-element.177, bf16[64,12000]{1,0:T(8,128)(2,1)} %get-tuple-element.196, s32[]{:T(128)S(6)} %select_n.112, f32[64,448]{1,0:T(8,128)S(1)} %get-tuple-element.187, pred[]{:T(512)S(6)} %compare.3), kind=kOutput, calls=%fused_computation.15.clone.1 | convolution fusion | flops 88761344 | bytes 1769989 | tf_op jit(solution)/shard_map/while/body/eval_jaxpr/dot_general | solution.py:35
  50.2 7.1 %cosine_convert_fusion.2 = (bf16[1500,224]{1,0:T(8,128)(2,1)S(1)}, bf16[1500,224]{1,0:T(8,128)(2,1)S(1)}) fusion(s32[224]{0:T(256)S(1)} %add_add_fusion.2, s32[1500]{0:T(1024)S(1)} %iota_add_fusion.3), kind=kLoop, calls=%fused_computation.10.clone.1 | loop fusion | flops 4032000 | bytes 1350896 | tf_op jit(solution)/shard_map/convert
  57.3 1.6 %fusion.39 = f32[64,448]{1,0:T(8,128)S(1)} fusion(bf16[1500,224]{1,0:T(8,128)(2,1)S(1)} %get-tuple-element.176, bf16[1500,224]{1,0:T(8,128)(2,1)S(1)} %get-tuple-element.177, bf16[64,12000]{1,0:T(8,128)(2,1)} %get-tuple-element.196, s32[]{:T(128)S(6)} %select_n.112, f32[64,448]{1,0:T(8,128)S(1)} %get-tuple-element.187, pred[]{:T(512)S(6)} %compare.3), kind=kOutput, calls=%fused_computation.15.clone.1 | convolution fusion | flops 88761344 | bytes 1769989 | tf_op jit(solution)/shard_map/while/body/eval_jaxpr/dot_general | solution.py:35
  59.0 7.1 %cosine_convert_fusion.2 = (bf16[1500,224]{1,0:T(8,128)(2,1)S(1)}, bf16[1500,224]{1,0:T(8,128)(2,1)S(1)}) fusion(s32[224]{0:T(256)S(1)} %add_add_fusion.2, s32[1500]{0:T(1024)S(1)} %iota_add_fusion.3), kind=kLoop, calls=%fused_computation.10.clone.1 | loop fusion | flops 4032000 | bytes 1350896 | tf_op jit(solution)/shard_map/convert
  66.1 1.6 %fusion.39 = f32[64,448]{1,0:T(8,128)S(1)} fusion(bf16[1500,224]{1,0:T(8,128)(2,1)S(1)} %get-tuple-element.176, bf16[1500,224]{1,0:T(8,128)(2,1)S(1)} %get-tuple-element.177, bf16[64,12000]{1,0:T(8,128)(2,1)} %get-tuple-element.196, s32[]{:T(128)S(6)} %select_n.112, f32[64,448]{1,0:T(8,128)S(1)} %get-tuple-element.187, pred[]{:T(512)S(6)} %compare.3), kind=kOutput, calls=%fused_computation.15.clone.1 | convolution fusion | flops 88761344 | bytes 1769989 | tf_op jit(solution)/shard_map/while/body/eval_jaxpr/dot_general | solution.py:35
  67.8 7.1 %cosine_convert_fusion.2 = (bf16[1500,224]{1,0:T(8,128)(2,1)S(1)}, bf16[1500,224]{1,0:T(8,128)(2,1)S(1)}) fusion(s32[224]{0:T(256)S(1)} %add_add_fusion.2, s32[1500]{0:T(1024)S(1)} %iota_add_fusion.3), kind=kLoop, calls=%fused_computation.10.clone.1 | loop fusion | flops 4032000 | bytes 1350896 | tf_op jit(solution)/shard_map/convert
  74.9 1.6 %fusion.39 = f32[64,448]{1,0:T(8,128)S(1)} fusion(bf16[1500,224]{1,0:T(8,128)(2,1)S(1)} %get-tuple-element.176, bf16[1500,224]{1,0:T(8,128)(2,1)S(1)} %get-tuple-element.177, bf16[64,12000]{1,0:T(8,128)(2,1)} %get-tuple-element.196, s32[]{:T(128)S(6)} %select_n.112, f32[64,448]{1,0:T(8,128)S(1)} %get-tuple-element.187, pred[]{:T(512)S(6)} %compare.3), kind=kOutput, calls=%fused_computation.15.clone.1 | convolution fusion | flops 88761344 | bytes 1769989 | tf_op jit(solution)/shard_map/while/body/eval_jaxpr/dot_general | solution.py:35
  76.6 0.2 reshape.205
  76.7 0.1 fusion.31
  76.8 0.1 multiply_reduce_fusion
  76.9 2.6 %psum.7 = f32[64,1]{0,1:T(1,128)S(1)} all-reduce(f32[64,1]{0,1:T(1,128)S(1)} %bitcast.22), channel_id=1, replica_groups=mesh['groups'=2,'chan'=8,'pair'=2] {'pair'}, use_global_device_ids=true, to_apply=%region_3.4 | all-reduce | flops 64 | bytes 512 | tf_op jit(solution)/shard_map/psum | solution.py:72
  79.5 0.1 fusion.21
  79.6 0.1 divide_convert_fusion
  79.7 0.1 copy.10
  79.9 2.0 %all_gather.6 = bf16[64,1,2,448]{0,2,1,3:T(2,128)(2,1)S(1)} all-gather(bf16[64,1,2,224]{0,2,1,3:T(2,128)(2,1)S(1)} %copy.10), channel_id=1, replica_groups=mesh['groups'=2,'chan'=8,'pair'=2] {'pair'}, dimensions={3}, use_global_device_ids=true | all-gather | bytes 172032 | tf_op jit(solution)/shard_map/all_gather | solution.py:74
  81.8 0.2 bitcast_convert_fusion
  82.0 0.2 copy.11
  82.3 0.2 fusion.26
  82.4 0.3 multiply_convert_fusion
  82.7 0.3 convert_element_type.72
  83.0 0.2 copy.12
  83.2 0.1 reshape.206
  83.3 34.2 %all_gather.7 = bf16[512,896]{1,0:T(8,128)(2,1)S(1)} all-gather(bf16[64,896]{1,0:T(8,128)(2,1)S(1)} %reshape.206), channel_id=1, replica_groups=mesh['groups'=2,'chan'=8,'pair'=2] {'chan'}, dimensions={0}, use_global_device_ids=true | all-gather | bytes 1032192 | tf_op jit(solution)/shard_map/all_gather | solution.py:80
  117.5 1.1 convolution_convert_fusion
  (22 shorter events, 0.1 us)
Async XLA Ops:
  0.0 3.3 %copy-start = (bf16[64,1,12000]{2,0,1:T(8,128)(2,1)S(1)}, bf16[64,1,12000]{2,0,1:T(8,128)(2,1)}, u32[]{:S(2)}) copy-start(bf16[64,1,12000]{2,0,1:T(8,128)(2,1)} %param.5) | copy-start | bytes 4608004
where the time goes:
time: 119 us
  other arithmetic  61.1 us (51%)
  blocking collectives  38.7 us (33%)
  matrix products  14.2 us (12%)
  local copies, waits for them, and re-layouts  4.09 us (3%)
    another operation x8, other arithmetic  56.7 us
    all_gather x1, blocking collectives, shards(): lax.all_gather(own_rows, 'chan', axis=0, tiled=True)  34.2 us
    dot_general x8, matrix products, add_block(): jnp.dot(sample_blk, dft_table, preferred_element_type=jnp.float32)  13.1 us
    psum x1, blocking collectives, shards(): lax.psum(jnp.sum(spectrum * spectrum, axis=(2, 3)), 'pair') / NB  2.58 us

commit v1 on v0

v1 whole, which is shorter than its diff:
```python
import functools

import jax
import jax.numpy as jnp
import numpy as np
from jax import lax
from jax.experimental import pallas as pl
from jax.experimental.pallas import tpu as pltpu
from jax.sharding import PartitionSpec as P

S = 12000
NB = 448
NSEG = 1
L = 6
LSTEP = 125
F0 = 60

water_level = 0.1

QUARTER = S // 4
CHUNK = 256
CHUNKS = -(-QUARTER // CHUNK)
DEPTH = CHUNKS * CHUNK
GROUP = 4
RES = (0, 2, 1, 3)
PER = NB // 4
LANES = 128
SPARE = LANES - PER
WIDTH = 2 * NB


def bins_of(residue):
    return np.arange(residue, NB, 4)


def quarter_table():
    table = np.zeros((DEPTH, 8 * LANES), np.float32)
    t = np.arange(QUARTER, dtype=np.int64)
    for place, residue in enumerate(RES):
        phase = t[:, None] * (F0 + bins_of(residue))[None, :] % S
        angles = phase.astype(np.float32) * np.float32(2.0 * np.pi / S)
        at = 2 * place * LANES
        table[:QUARTER, at : at + PER] = np.cos(angles.astype(np.float64))
        table[:QUARTER, at + LANES : at + LANES + PER] = -np.sin(angles.astype(np.float64))
    return table.astype(jnp.bfloat16)


def packed_bins():
    pieces = [bins_of(residue) for residue in RES for _ in range(2)]
    columns = []
    for p in range(7):
        columns.append(pieces[p])
        columns.append(pieces[7][p * SPARE : (p + 1) * SPARE])
    return np.concatenate(columns)


def lag_table():
    bins = packed_bins()
    taper = np.float32(0.5) - np.float32(0.5) * np.cos(
        np.float32(2.0 * np.pi) * (bins.astype(np.float32) + np.float32(0.5)) / np.float32(NB)
    )
    phase = (F0 + bins)[None, :] * (np.arange(L) * LSTEP)[:, None] % S
    waves = np.cos(phase.astype(np.float32) * np.float32(2.0 * np.pi / S))
    return (taper[None, :] * waves / np.sqrt(np.float32(NSEG * NB))).astype(np.float32)


def split(value):
    high = value.astype(jnp.bfloat16)
    low = (value - high.astype(jnp.float32)).astype(jnp.bfloat16)
    return high, low


def spectra_kernel(count_ref, index_ref, raw_ref, table_ref, out_ref, x, tail, table, y_even, y_half, y_odd, sems):
    rows = x.shape[0]
    whole = S // LANES * LANES
    x_copy = pltpu.make_async_copy(raw_ref, x, sems.at[0])
    x_copy.start()
    copies = []
    for g in range(CHUNKS // GROUP):
        span = pl.ds(g * GROUP * CHUNK, GROUP * CHUNK)
        copies.append(pltpu.make_async_copy(table_ref.at[span, :], table.at[span, :], sems.at[1 + g]))
        copies[-1].start()
    tail[...] = jnp.zeros_like(tail)
    x_copy.wait()
    tail[:, : S - whole] = x[:, whole:S]

    def window(start):
        base = start // LANES * LANES
        shift = start - base
        parts = []
        for lane in range(base, base + CHUNK + (LANES if shift else 0), LANES):
            if lane + LANES <= S:
                parts.append(x[:, lane : lane + LANES])
            elif lane < S:
                parts.append(tail[...])
            else:
                parts.append(jnp.zeros((rows, LANES), x.dtype))
        value = jnp.concatenate(parts, axis=1).astype(jnp.float32)
        if shift:
            value = pltpu.roll(value, value.shape[1] - shift, axis=1)[:, :CHUNK]
        return value

    even = jnp.zeros((2 * rows, 2 * LANES), jnp.float32)
    half = jnp.zeros((2 * rows, 2 * LANES), jnp.float32)
    odd = jnp.zeros((4 * rows, 4 * LANES), jnp.float32)
    for g in range(CHUNKS // GROUP):
        for c in range(g * GROUP, (g + 1) * GROUP):
            at = c * CHUNK
            x0, x1, x2, x3 = (window(m * QUARTER + at) for m in range(4))
            sum02, sum13 = x0 + x2, x1 + x3
            for target, first, value in (
                (y_even, 0, sum02 + sum13),
                (y_half, 0, sum02 - sum13),
                (y_odd, 0, x0 - x2),
                (y_odd, 2 * rows, x1 - x3),
            ):
                high, low = split(value)
                target[first : first + rows, at : at + CHUNK] = high
                target[first + rows : first + 2 * rows, at : at + CHUNK] = low
        copies[g].wait()
        lo, hi = g * GROUP * CHUNK, (g + 1) * GROUP * CHUNK
        even += jnp.dot(y_even[:, lo:hi], table[lo:hi, : 2 * LANES], preferred_element_type=jnp.float32)
        half += jnp.dot(y_half[:, lo:hi], table[lo:hi, 2 * LANES : 4 * LANES], preferred_element_type=jnp.float32)
        odd += jnp.dot(y_odd[:, lo:hi], table[lo:hi, 4 * LANES :], preferred_element_type=jnp.float32)

    even = even[:rows] + even[rows:]
    half = half[:rows] + half[rows:]
    u = odd[:rows] + odd[rows : 2 * rows]
    v = odd[2 * rows : 3 * rows] + odd[3 * rows :]
    pairs = (
        (even[:, :LANES], even[:, LANES:]),
        (half[:, :LANES], half[:, LANES:]),
        (u[:, :LANES] + v[:, LANES : 2 * LANES], u[:, LANES : 2 * LANES] - v[:, :LANES]),
        (u[:, 2 * LANES : 3 * LANES] - v[:, 3 * LANES :], u[:, 3 * LANES :] + v[:, 2 * LANES : 3 * LANES]),
    )
    power = [re * re + im * im for re, im in pairs]
    band_power = jnp.sum(power[0] + power[1] + power[2] + power[3], axis=1, keepdims=True) / NB
    pieces = []
    for (re, im), own in zip(pairs, power):
        denom = jnp.sqrt(own + water_level * band_power + 1e-06)
        pieces += [re / denom, im / denom]
    lanes = lax.broadcasted_iota(jnp.int32, (rows, LANES), 1)
    packed = []
    for p in range(7):
        moved = pltpu.roll(pieces[7], (PER - p * SPARE) % LANES, axis=1)
        packed.append(jnp.where(lanes < PER, pieces[p], moved))
    whitened = jnp.concatenate(packed, axis=1).astype(jnp.bfloat16)
    source = lax.broadcasted_iota(jnp.int32, (rows, rows), 0)
    slot = lax.broadcasted_iota(jnp.int32, (rows, rows), 1)
    chosen = jnp.logical_and(source == index_ref[...], slot < count_ref[0])
    pick = jnp.where(chosen, 1.0, 0.0).astype(jnp.bfloat16)
    out_ref[...] = lax.dot_general(
        pick, whitened, (((0,), (0,)), ((), ())), preferred_element_type=jnp.float32
    ).astype(jnp.bfloat16)


def spectra(raw_rows, index_row, count, table):
    rows = raw_rows.shape[0]
    return pl.pallas_call(
        spectra_kernel,
        out_shape=jax.ShapeDtypeStruct((rows, WIDTH), jnp.bfloat16),
        in_specs=[
            pl.BlockSpec(memory_space=pltpu.SMEM),
            pl.BlockSpec(memory_space=pltpu.VMEM),
            pl.BlockSpec(memory_space=pl.ANY),
            pl.BlockSpec(memory_space=pl.ANY),
        ],
        out_specs=pl.BlockSpec(memory_space=pltpu.VMEM),
        scratch_shapes=[
            pltpu.VMEM((rows, S), jnp.bfloat16),
            pltpu.VMEM((rows, LANES), jnp.bfloat16),
            pltpu.VMEM((DEPTH, 8 * LANES), jnp.bfloat16),
            pltpu.VMEM((2 * rows, DEPTH), jnp.bfloat16),
            pltpu.VMEM((2 * rows, DEPTH), jnp.bfloat16),
            pltpu.VMEM((4 * rows, DEPTH), jnp.bfloat16),
            pltpu.SemaphoreType.DMA((1 + CHUNKS // GROUP,)),
        ],
        compiler_params=pltpu.CompilerParams(vmem_limit_bytes=40 * 1024 * 1024),
        cost_estimate=pl.CostEstimate(
            flops=2 * DEPTH * rows * 3072, bytes_accessed=DEPTH * 2048 + rows * S * 2, transcendentals=0
        ),
        name="spectra",
    )(count, index_row, raw_rows, table)


def correlate(lag_rows, columns):
    product = lax.dot_general(
        lag_rows, columns, (((1,), (1,)), ((), ())), preferred_element_type=jnp.float32
    )
    return product.astype(jnp.bfloat16)


def shards(table, weights, raw, live_index, live_count):
    slot_count, seg_count, samples = raw.shape
    pair_index = lax.axis_index("pair")
    lag_share = L // lax.axis_size("pair")
    count = lax.dynamic_slice_in_dim(live_count, lax.axis_index("chan"), 1)
    own = spectra(raw.reshape(slot_count * seg_count, samples), live_index, count, table)
    own_weights = lax.dynamic_slice_in_dim(weights, pair_index * lag_share, lag_share, 0)
    lag_rows = (own.astype(jnp.float32)[None] * own_weights[:, None, :]).astype(jnp.bfloat16)
    lag_rows = lag_rows.reshape(lag_share * slot_count, -1)
    product = correlate(lag_rows, lax.all_gather(own, "chan", axis=0, tiled=True))
    return product.reshape(lag_share, slot_count, -1)


def solution(mesh):
    local = functools.partial(shards, jnp.asarray(quarter_table()), jnp.asarray(lag_table()))
    return jax.shard_map(
        local,
        mesh=mesh,
        in_specs=(P(("groups", "chan"), None, None), P(("groups", "chan"), None), P("groups")),
        out_specs=P("pair", ("groups", "chan"), None),
        check_vma=False,
    )
```

time: 119 us -> 46.7 us (0.39)
  other arithmetic: 61.1 us -> 0.06 us
  matrix products: 14.2 us -> 1.14 us
  blocking collectives: 38.7 us -> 34.2 us
  Pallas kernels: 0 us -> 4.17 us
  local copies, waits for them, and re-layouts: 4.09 us -> 6.83 us
    another operation x8 -> x0, other arithmetic: 56.7 us -> none
    dot_general x8 -> x0, matrix products: 13.1 us -> none  [add_block(): jnp.dot(sample_blk, dft_table, preferred_element_type=jnp.float32)]
    unnamed x2 -> x6, local copies, waits for them, and re-layouts: 0.01 us -> 4.83 us
    pallas_call x0 -> x1, Pallas kernels: none -> 4.17 us  [spectra(): pl.pallas_call(spectra_kernel, out_shape=jax.ShapeDtypeStruct((rows, WIDT...]
    psum x1 -> x0, blocking collectives: 2.58 us -> none  [shards(): lax.psum(jnp.sum(spectrum * spectrum, axis=(2, 3)), 'pair') / NB]
    select_n x2 -> x0, other arithmetic: 2.05 us -> none  [the longest x1 1.39 us: shards(): jnp.where((slot_ids < live_slots)[:, None, None], chosen, jnp.zeros((), r...]
    all_gather x2 -> x1, blocking collectives: 36.2 us -> 34.2 us  [shards(): lax.all_gather(own, 'chan', axis=0, tiled=True)]
    gather x1 -> x0, local copies, waits for them, and re-layouts: 1.53 us -> none  [shards(): chosen = jnp.take(raw, live_index[0], axis=0)]
where the time goes in v1:
time: 46.7 us; the launch traced here: 46.4 us
  blocking collectives  34.2 us (73%)
  local copies, waits for them, and re-layouts  6.83 us (15%)
  Pallas kernels  4.17 us (9%)
  matrix products  1.14 us (2%)
    all_gather x1, blocking collectives, shards(): lax.all_gather(own, 'chan', axis=0, tiled=True)  34.2 us
    unnamed x6, local copies, waits for them, and re-layouts  4.83 us
    pallas_call x1, Pallas kernels, spectra(): pl.pallas_call(spectra_kernel, out_shape=jax.ShapeDtypeStruct((rows, WIDT...  4.17 us
    dynamic_slice x1, local copies, waits for them, and re-layouts, shards(): count = lax.dynamic_slice_in_dim(live_count, lax.axis_index('chan'), 1)  1.24 us
    dot_general x1, matrix products, correlate(): lax.dot_general(lag_rows, columns, (((1,), (1,)), ((), ())), preferred_el...  1.14 us

profile of v1, /device:TPU:0, one launch (start us, length us, event | category | flops | bytes accessed | tf_op | source)
XLA Modules:
  0.0 46.4 jit_solution(15589672363750371745)
XLA Ops:
  0.0 1.2 %dynamic_slice.6.count_ref = s32[1]{0:T(128)} dynamic-slice(s32[8]{0:T(128)} %param.7, s32[]{:T(128)S(6)} %select_n.6), dynamic_slice_sizes={1} | dynamic-slice | bytes 12 | tf_op jit(solution)/shard_map/dynamic_slice | solution.py:197
  1.2 0.8 %constant_dynamic-slice_fusion = f32[3,896]{1,0:T(4,128)S(1)} fusion(f32[6,896]{1,0:T(8,128)} %constant.21.clone, s32[]{:T(128)S(6)} %select_n.7), kind=kLoop, calls=%fused_computation.2 | loop fusion | bytes 21508 | tf_op jit(solution)/shard_map/dynamic_slice | solution.py:199
  2.0 0.0 copy-start
  2.0 2.8 %copy-done = bf16[3072,1024]{1,0:T(8,128)(2,1)S(1)} copy-done((bf16[3072,1024]{1,0:T(8,128)(2,1)S(1)}, bf16[3072,1024]{1,0:T(8,128)(2,1)}, u32[]{:S(2)}) %copy-start) | copy-done | bytes 6291480
  4.8 0.0 copy-start.1
  4.8 1.4 %copy-done.1 = bf16[64,1,12000]{2,0,1:T(8,128)(2,1)S(1)} copy-done((bf16[64,1,12000]{2,0,1:T(8,128)(2,1)S(1)}, bf16[64,1,12000]{2,0,1:T(8,128)(2,1)}, u32[]{:S(2)}) %copy-start.1) | copy-done | bytes 1536024
  6.2 0.0 copy-start.2
  6.2 0.7 %copy-done.2 = s32[1,64]{1,0:T(1,128)S(1)} copy-done((s32[1,64]{1,0:T(1,128)S(1)}, s32[1,64]{1,0:T(1,128)}, u32[]{:S(2)}) %copy-start.2) | copy-done | bytes 280
  6.8 4.2 %spectra.1 = bf16[64,896]{1,0:T(8,128)(2,1)S(1)} custom-call(s32[1]{0:T(128)} %dynamic_slice.6.count_ref, s32[1,64]{1,0:T(1,128)S(1)} %copy-done.2, bf16[64,12000]{1,0:T(8,128)(2,1)S(1)} %bitcast.5, bf16[3072,1024]{1,0:T(8,128)(2,1)S(1)} %copy-done), custom_call_target="tpu_custom_call" | custom-call | flops 1207959552 | bytes 7827456 | tf_op jit(solution)/shard_map/spectra/pallas_call | solution.py:159
  11.1 34.2 %all_gather.3 = bf16[512,896]{1,0:T(8,128)(2,1)S(1)} all-gather(bf16[64,896]{1,0:T(8,128)(2,1)S(1)} %spectra.1), channel_id=1, replica_groups=mesh['groups'=2,'chan'=8,'pair'=2] {'chan'}, dimensions={0}, use_global_device_ids=true | all-gather | bytes 1032192 | tf_op jit(solution)/shard_map/all_gather | solution.py:202
  45.3 1.1 %convolution_convert_fusion = bf16[192,512]{1,0:T(8,128)(2,1)} fusion(bf16[192,896]{1,0:T(8,128)(2,1)S(1)} %bitcast.6, bf16[512,896]{1,0:T(8,128)(2,1)S(1)} %all_gather.3), kind=kOutput, calls=%fused_computation | convolution fusion | flops 176259072 | bytes 1458176 | tf_op jit(solution)/shard_map/dot_general | solution.py:187
  (2 shorter events, 0.1 us)
Async XLA Ops:
  2.0 2.8 %copy-start = (bf16[3072,1024]{1,0:T(8,128)(2,1)S(1)}, bf16[3072,1024]{1,0:T(8,128)(2,1)}, u32[]{:S(2)}) copy-start(bf16[3072,1024]{1,0:T(8,128)(2,1)} %constant.20.clone.table_ref) | copy-start | bytes 18874372
  4.8 1.4 %copy-start.1 = (bf16[64,1,12000]{2,0,1:T(8,128)(2,1)S(1)}, bf16[64,1,12000]{2,0,1:T(8,128)(2,1)}, u32[]{:S(2)}) copy-start(bf16[64,1,12000]{2,0,1:T(8,128)(2,1)} %param.5) | copy-start | bytes 4608004
  6.2 0.7 %copy-start.2 = (s32[1,64]{1,0:T(1,128)S(1)}, s32[1,64]{1,0:T(1,128)}, u32[]{:S(2)}) copy-start(s32[1,64]{1,0:T(1,128)} %index_ref.1) | copy-start | bytes 772

commit v2 on v1

--- a/solution.py
+++ b/solution.py
@@ -21,12 +21,13 @@
 CHUNK = 256
 CHUNKS = -(-QUARTER // CHUNK)
 DEPTH = CHUNKS * CHUNK
-GROUP = 4
+GROUP = 2
 RES = (0, 2, 1, 3)
 PER = NB // 4
 LANES = 128
 SPARE = LANES - PER
 WIDTH = 2 * NB
+VMEM_MIB = 60
 
 
 def bins_of(residue):
@@ -70,11 +71,39 @@
     return high, low
 
 
-def spectra_kernel(count_ref, index_ref, raw_ref, table_ref, out_ref, x, tail, table, y_even, y_half, y_odd, sems):
+def spectra_kernel(
+    lag_share,
+    count_ref,
+    index_ref,
+    raw_ref,
+    table_ref,
+    weight_ref,
+    out_ref,
+    first_ref,
+    second_ref,
+    lag_ref,
+    x,
+    tail,
+    table,
+    y_even,
+    y_half,
+    y_odd,
+    counts,
+    index,
+    weights,
+    small_sems,
+    sems,
+):
     rows = x.shape[0]
     whole = S // LANES * LANES
     x_copy = pltpu.make_async_copy(raw_ref, x, sems.at[0])
     x_copy.start()
+    count_copy = pltpu.make_async_copy(count_ref, counts, small_sems.at[0])
+    index_copy = pltpu.make_async_copy(index_ref, index, small_sems.at[1])
+    count_copy.start()
+    index_copy.start()
+    weight_copy = pltpu.make_async_copy(weight_ref.at[lax.axis_index("pair")], weights, small_sems.at[2])
+    weight_copy.start()
     copies = []
     for g in range(CHUNKS // GROUP):
         span = pl.ds(g * GROUP * CHUNK, GROUP * CHUNK)
@@ -145,27 +174,36 @@
         moved = pltpu.roll(pieces[7], (PER - p * SPARE) % LANES, axis=1)
         packed.append(jnp.where(lanes < PER, pieces[p], moved))
     whitened = jnp.concatenate(packed, axis=1).astype(jnp.bfloat16)
+    count_copy.wait()
+    index_copy.wait()
+    count = counts[lax.axis_index("chan")]
     source = lax.broadcasted_iota(jnp.int32, (rows, rows), 0)
     slot = lax.broadcasted_iota(jnp.int32, (rows, rows), 1)
-    chosen = jnp.logical_and(source == index_ref[...], slot < count_ref[0])
+    chosen = jnp.logical_and(source == index[...], slot < count)
     pick = jnp.where(chosen, 1.0, 0.0).astype(jnp.bfloat16)
-    out_ref[...] = lax.dot_general(
-        pick, whitened, (((0,), (0,)), ((), ())), preferred_element_type=jnp.float32
-    ).astype(jnp.bfloat16)
-
-
-def spectra(raw_rows, index_row, count, table):
+    own = lax.dot_general(pick, whitened, (((0,), (0,)), ((), ())), preferred_element_type=jnp.float32)
+    narrow = own.astype(jnp.bfloat16)
+    out_ref[...] = narrow
+    first_ref[...] = narrow[: rows // 2]
+    second_ref[...] = narrow[rows // 2 :]
+    weight_copy.wait()
+    for lag in range(lag_share):
+        lag_ref[lag * rows : (lag + 1) * rows, :] = (own * weights[lag : lag + 1, :]).astype(jnp.bfloat16)
+
+
+def spectra(raw_rows, index_row, live_count, table, weights):
     rows = raw_rows.shape[0]
+    lag_share = weights.shape[1]
     return pl.pallas_call(
-        spectra_kernel,
-        out_shape=jax.ShapeDtypeStruct((rows, WIDTH), jnp.bfloat16),
-        in_specs=[
-            pl.BlockSpec(memory_space=pltpu.SMEM),
-            pl.BlockSpec(memory_space=pltpu.VMEM),
-            pl.BlockSpec(memory_space=pl.ANY),
-            pl.BlockSpec(memory_space=pl.ANY),
+        functools.partial(spectra_kernel, lag_share),
+        out_shape=[
+            jax.ShapeDtypeStruct((rows, WIDTH), jnp.bfloat16),
+            jax.ShapeDtypeStruct((rows // 2, WIDTH), jnp.bfloat16),
+            jax.ShapeDtypeStruct((rows // 2, WIDTH), jnp.bfloat16),
+            jax.ShapeDtypeStruct((lag_share * rows, WIDTH), jnp.bfloat16),
         ],
-        out_specs=pl.BlockSpec(memory_space=pltpu.VMEM),
+        in_specs=[pl.BlockSpec(memory_space=pltpu.HBM)] * 5,
+        out_specs=[pl.BlockSpec(memory_space=pltpu.VMEM)] * 4,
         scratch_shapes=[
             pltpu.VMEM((rows, S), jnp.bfloat16),
             pltpu.VMEM((rows, LANES), jnp.bfloat16),
@@ -173,14 +211,18 @@
             pltpu.VMEM((2 * rows, DEPTH), jnp.bfloat16),
             pltpu.VMEM((2 * rows, DEPTH), jnp.bfloat16),
             pltpu.VMEM((4 * rows, DEPTH), jnp.bfloat16),
+            pltpu.SMEM(live_count.shape, jnp.int32),
+            pltpu.VMEM(index_row.shape, jnp.int32),
+            pltpu.VMEM(weights.shape[1:], jnp.float32),
+            pltpu.SemaphoreType.DMA((3,)),
             pltpu.SemaphoreType.DMA((1 + CHUNKS // GROUP,)),
         ],
-        compiler_params=pltpu.CompilerParams(vmem_limit_bytes=40 * 1024 * 1024),
+        compiler_params=pltpu.CompilerParams(vmem_limit_bytes=VMEM_MIB * 1024 * 1024),
         cost_estimate=pl.CostEstimate(
             flops=2 * DEPTH * rows * 3072, bytes_accessed=DEPTH * 2048 + rows * S * 2, transcendentals=0
         ),
         name="spectra",
-    )(count, index_row, raw_rows, table)
+    )(live_count, index_row, raw_rows, table, weights)
 
 
 def correlate(lag_rows, columns):
@@ -190,17 +232,86 @@
     return product.astype(jnp.bfloat16)
 
 
+def eight_kernel(lags, own, side, near, far, far_swap, near_swap, cross_a, cross_b, cross_swap_a, cross_swap_b, out):
+    me = lax.axis_index("chan")
+    core = lax.axis_index("pair")
+    x, z = me % 2, me // 2
+    rows = own.shape[0]
+    upper = core == 1
+    lag_rows = lags[...]
+    tiles = (
+        ((own[...], side[...]), z),
+        (
+            (
+                jnp.where(upper, near_swap[...], near[...]),
+                jnp.where(upper, near[...], near_swap[...]),
+            ),
+            z ^ 1,
+        ),
+        ((far[...], cross_swap_a[...], cross_swap_b[...]), z ^ (2 + core)),
+        ((far_swap[...], cross_a[...], cross_b[...]), z ^ (3 - core)),
+    )
+    for blocks, plane in tiles:
+        columns = jnp.concatenate(blocks, axis=0)
+        product = lax.dot_general(
+            lag_rows, columns, (((1,), (1,)), ((), ())), preferred_element_type=jnp.float32
+        )
+        product = jnp.where(x == 0, product, pltpu.roll(product, rows, axis=1)).astype(jnp.bfloat16)
+        at = pl.multiple_of(plane * 2 * rows, 2 * rows)
+        for lag in range(out.shape[0]):
+            out[lag, :, pl.ds(at, 2 * rows)] = product[lag * rows : (lag + 1) * rows]
+
+
+def exchange_eight(own, first, second, lags):
+    def split_move(mask1, mask0):
+        pairs = [(2 * c + 1, 2 * (c ^ mask1) + 1) for c in range(8)] + [(2 * c, 2 * (c ^ mask0)) for c in range(8)]
+        return lambda a: lax.ppermute(a, ("chan", "pair"), pairs)
+
+    def forward(a):
+        pairs = [(2 * c + p, 2 * (c ^ 1) + 1 - p) for c in range(8) for p in range(2)]
+        return lax.ppermute(a, ("chan", "pair"), pairs)
+
+    def swap(a):
+        return lax.ppermute(a, "pair", [(0, 1), (1, 0)])
+
+    far_a = split_move(6, 4)(first)
+    far_b = split_move(6, 4)(second)
+    side = split_move(1, 1)(own)
+    near = split_move(3, 2)(own)
+    far_a_ready, side = lax.optimization_barrier((far_a, side))
+    cross_a = forward(far_a_ready)
+    cross_b = forward(far_b)
+    far = jnp.concatenate([far_a, far_b], axis=0)
+    far_swap, near_swap = swap(far), swap(near)
+    cross_swap_a, cross_swap_b = swap(cross_a), swap(cross_b)
+    lag_share, rows = lags.shape[0] // own.shape[0], own.shape[0]
+    return pl.pallas_call(
+        eight_kernel,
+        out_shape=jax.ShapeDtypeStruct((lag_share, rows, 8 * rows), jnp.bfloat16),
+        in_specs=[pl.BlockSpec(memory_space=pltpu.VMEM)] * 11,
+        out_specs=pl.BlockSpec(memory_space=pltpu.VMEM),
+        compiler_params=pltpu.CompilerParams(vmem_limit_bytes=32 * 1024 * 1024),
+        cost_estimate=pl.CostEstimate(
+            flops=2 * lag_share * rows * 8 * rows * WIDTH, bytes_accessed=12 * rows * WIDTH * 2, transcendentals=0
+        ),
+        name="correlate",
+    )(lags, own, side, near, far, far_swap, near_swap, cross_a, cross_b, cross_swap_a, cross_swap_b)
+
+
 def shards(table, weights, raw, live_index, live_count):
     slot_count, seg_count, samples = raw.shape
-    pair_index = lax.axis_index("pair")
-    lag_share = L // lax.axis_size("pair")
-    count = lax.dynamic_slice_in_dim(live_count, lax.axis_index("chan"), 1)
-    own = spectra(raw.reshape(slot_count * seg_count, samples), live_index, count, table)
-    own_weights = lax.dynamic_slice_in_dim(weights, pair_index * lag_share, lag_share, 0)
-    lag_rows = (own.astype(jnp.float32)[None] * own_weights[:, None, :]).astype(jnp.bfloat16)
-    lag_rows = lag_rows.reshape(lag_share * slot_count, -1)
-    product = correlate(lag_rows, lax.all_gather(own, "chan", axis=0, tiled=True))
-    return product.reshape(lag_share, slot_count, -1)
+    pairs = lax.axis_size("pair")
+    own, first, second, lags = spectra(
+        raw.reshape(slot_count * seg_count, samples),
+        live_index,
+        live_count,
+        table,
+        weights.reshape(pairs, L // pairs, WIDTH),
+    )
+    if lax.axis_size("chan") == 8 and pairs == 2 and slot_count == 64:
+        return exchange_eight(own, first, second, lags)
+    product = correlate(lags, lax.all_gather(own, "chan", axis=0, tiled=True))
+    return product.reshape(L // pairs, slot_count, -1)
 
 
 def solution(mesh):

time: 46.7 us -> 27.8 us (0.60)
  blocking collectives: 34.2 us -> 0 us
  starting transfers between devices: 0 us -> 11.2 us
  waiting for transfers between devices: 0 us -> 8.21 us
  local copies, waits for them, and re-layouts: 6.83 us -> 1.89 us
  Pallas kernels: 4.17 us -> 6.32 us
  matrix products: 1.14 us -> 0 us
    all_gather x1 -> x0, blocking collectives: 34.2 us -> none  [shards(): lax.all_gather(own, 'chan', axis=0, tiled=True)]
    ppermute x0 -> x10, starting transfers between devices: none -> 11.2 us  [the longest x4 7.5 us: split_move(): return lambda a: lax.ppermute(a, ('chan', 'pair'), pairs)]
    ppermute x0 -> x10, waiting for transfers between devices: none -> 8.21 us  [the longest x4 5.45 us: split_move(): return lambda a: lax.ppermute(a, ('chan', 'pair'), pairs)]
    unnamed x6 -> x5, local copies, waits for them, and re-layouts: 4.83 us -> 1.88 us
    pallas_call x1 -> x2, Pallas kernels: 4.17 us -> 6.32 us  [the longest x1 5.03 us: spectra(): pl.pallas_call(functools.partial(spectra_kernel, lag_share), out_shape=[j...]
    dynamic_slice x2 -> x0, local copies, waits for them, and re-layouts: 1.99 us -> none  [the longest x1 1.24 us: shards(): count = lax.dynamic_slice_in_dim(live_count, lax.axis_index('chan'), 1)]
    dot_general x1 -> x0, matrix products: 1.14 us -> none  [correlate(): lax.dot_general(lag_rows, columns, (((1,), (1,)), ((), ())), preferred_el...]
  transfers between devices with their start and end apart: 0 -> 10, of which waited for: 0 -> 5; matrix products, arithmetic and copies ran while one was open for 0% -> 0% of each run, Pallas kernels for 0% -> 0%
where the time goes in v2:
time: 27.8 us; the launch traced here: 27.6 us
  starting transfers between devices  11.2 us (40%)
  waiting for transfers between devices  8.21 us (30%)
  Pallas kernels  6.32 us (23%)
  local copies, waits for them, and re-layouts  1.89 us (7%)
    ppermute x4, starting transfers between devices, split_move(): return lambda a: lax.ppermute(a, ('chan', 'pair'), pairs)  7.5 us
    ppermute x4, waiting for transfers between devices, split_move(): return lambda a: lax.ppermute(a, ('chan', 'pair'), pairs)  5.45 us
    pallas_call x1, Pallas kernels, spectra(): pl.pallas_call(functools.partial(spectra_kernel, lag_share), out_shape=[j...  5.03 us
    ppermute x2, starting transfers between devices, forward(): return lax.ppermute(a, ('chan', 'pair'), pairs)  2.19 us
    unnamed x5, local copies, waits for them, and re-layouts  1.88 us
    ppermute x2, waiting for transfers between devices, forward(): return lax.ppermute(a, ('chan', 'pair'), pairs)  1.73 us
    ppermute x4, starting transfers between devices, swap(): return lax.ppermute(a, 'pair', [(0, 1), (1, 0)])  1.48 us
    pallas_call x1, Pallas kernels, exchange_eight(): pl.pallas_call(eight_kernel, out_shape=jax.ShapeDtypeStruct((lag_share, r...  1.29 us
  transfers between devices with their start and end apart: 10, of which 5 were waited for; matrix products, arithmetic and copies ran while one was open for 0% of the time, Pallas kernels for 0%

profile of v2, /device:TPU:0, one launch (start us, length us, event | category | flops | bytes accessed | tf_op | source)
XLA Modules:
  0.0 27.6 jit_solution(5044539134196644874)
XLA Ops:
  0.0 5.0 %spectra.1 = (bf16[64,896]{1,0:T(8,128)(2,1)}, bf16[32,896]{1,0:T(8,128)(2,1)}, bf16[32,896]{1,0:T(8,128)(2,1)}, bf16[192,896]{1,0:T(8,128)(2,1)}) custom-call(s32[8]{0:T(128)} %count_ref.1, s32[1,64]{1,0:T(1,128)} %index_ref.1, bf16[64,12000]{1,0:T(8,128)(2,1)} %bitcast.1, bf16[3072,1024]{1,0:T(8,128)(2,1)} %constant.5.clone.table_ref, ...), custom_call_target="tpu_custom_call" | custom-call | flops 1207959552 | bytes 7827456 | tf_op jit(solution)/shard_map/spectra/pallas_call | solution.py:197
  5.0 4.1 %collective-permute-start = (bf16[32,896]{1,0:T(8,128)(2,1)}, bf16[32,896]{1,0:T(8,128)(2,1)S(1)}, u32[]{:S(2)}, u32[]{:S(2)}) collective-permute-start(bf16[32,896]{1,0:T(8,128)(2,1)} %get-tuple-element.13), channel_id=1, source_target_pairs={{1,13},{3,15},{5,9},{7,11},{9,5},{11,7},{13,1},{15,3},{0,8},{2,10}... | collective-permute-start | bytes 172040 | tf_op jit(solution)/shard_map/ppermute | solution.py:268
  9.1 1.6 %collective-permute-start.2 = (bf16[64,896]{1,0:T(8,128)(2,1)}, bf16[64,896]{1,0:T(8,128)(2,1)S(1)}, u32[]{:S(2)}, u32[]{:S(2)}) collective-permute-start(bf16[64,896]{1,0:T(8,128)(2,1)} %get-tuple-element.12.own), channel_id=1, source_target_pairs={{1,7},{3,5},{5,3},{7,1},{9,15},{11,13},{13,11},{15,9},{0,4},{2,6},... | collective-permute-start | bytes 344072 | tf_op jit(solution)/shard_map/ppermute | solution.py:268
  10.7 1.5 %collective-permute-start.1 = (bf16[64,896]{1,0:T(8,128)(2,1)}, bf16[64,896]{1,0:T(8,128)(2,1)S(1)}, u32[]{:S(2)}, u32[]{:S(2)}) collective-permute-start(bf16[64,896]{1,0:T(8,128)(2,1)} %get-tuple-element.12.own), channel_id=1, source_target_pairs={{1,3},{3,1},{5,7},{7,5},{9,11},{11,9},{13,15},{15,13},{0,2},{2,0},... | collective-permute-start | bytes 344072 | tf_op jit(solution)/shard_map/ppermute | solution.py:268
  12.2 0.3 %collective-permute-start.3 = (bf16[32,896]{1,0:T(8,128)(2,1)}, bf16[32,896]{1,0:T(8,128)(2,1)S(1)}, u32[]{:S(2)}, u32[]{:S(2)}) collective-permute-start(bf16[32,896]{1,0:T(8,128)(2,1)} %get-tuple-element.15), channel_id=1, source_target_pairs={{1,13},{3,15},{5,9},{7,11},{9,5},{11,7},{13,1},{15,3},{0,8},{2,10}... | collective-permute-start | bytes 172040 | tf_op jit(solution)/shard_map/ppermute | solution.py:268
  12.5 0.0 collective-permute-done
  12.6 5.4 %collective-permute-done.3 = bf16[32,896]{1,0:T(8,128)(2,1)S(1)} collective-permute-done((bf16[32,896]{1,0:T(8,128)(2,1)}, bf16[32,896]{1,0:T(8,128)(2,1)S(1)}, u32[]{:S(2)}, u32[]{:S(2)}) %collective-permute-start.3) | collective-permute-done | bytes 57376 | tf_op jit(solution)/shard_map/ppermute | solution.py:268
  18.0 0.1 collective-permute-start.4
  18.1 0.8 %collective-permute-start.7 = (bf16[32,896]{1,0:T(8,128)(2,1)S(1)}, bf16[32,896]{1,0:T(8,128)(2,1)S(1)}, u32[]{:S(2)}, u32[]{:S(2)}) collective-permute-start(bf16[32,896]{1,0:T(8,128)(2,1)S(1)} %collective-permute-done.3), channel_id=1, source_target_pairs={{0,3},{1,2},{2,1},{3,0},{4,7},{5,6},{6,5},{7,4},{8,11},{9,10},{10,... | collective-permute-start | bytes 172040 | tf_op jit(solution)/shard_map/ppermute | solution.py:272
  18.9 0.0 collective-permute-done.1.side
  18.9 0.0 collective-permute-done.2.near
  18.9 0.1 collective-permute-start.5
  19.0 1.4 %collective-permute-start.6 = (bf16[32,896]{1,0:T(8,128)(2,1)S(1)}, bf16[32,896]{1,0:T(8,128)(2,1)S(1)}, u32[]{:S(2)}, u32[]{:S(2)}) collective-permute-start(bf16[32,896]{1,0:T(8,128)(2,1)S(1)} %collective-permute-done), channel_id=1, source_target_pairs={{0,3},{1,2},{2,1},{3,0},{4,7},{5,6},{6,5},{7,4},{8,11},{9,10},{10,... | collective-permute-start | bytes 172040 | tf_op jit(solution)/shard_map/ppermute | solution.py:272
  20.4 1.4 %collective-permute-done.7.cross_b = bf16[32,896]{1,0:T(8,128)(2,1)S(1)} collective-permute-done((bf16[32,896]{1,0:T(8,128)(2,1)S(1)}, bf16[32,896]{1,0:T(8,128)(2,1)S(1)}, u32[]{:S(2)}, u32[]{:S(2)}) %collective-permute-start.7) | collective-permute-done | bytes 57376 | tf_op jit(solution)/shard_map/ppermute | solution.py:272
  21.8 1.1 %collective-permute-start.9 = (bf16[32,896]{1,0:T(8,128)(2,1)S(1)}, bf16[32,896]{1,0:T(8,128)(2,1)S(1)}, u32[]{:S(2)}, u32[]{:S(2)}) collective-permute-start(bf16[32,896]{1,0:T(8,128)(2,1)S(1)} %collective-permute-done.7.cross_b), channel_id=1, source_target_pairs={{0,1},{1,0},{2,3},{3,2},{4,5},{5,4},{6,7},{7,6},{8,9},{9,8},{10,11... | collective-permute-start | bytes 172040 | tf_op jit(solution)/shard_map/ppermute | solution.py:275
  22.9 0.3 %collective-permute-done.6.cross_a = bf16[32,896]{1,0:T(8,128)(2,1)S(1)} collective-permute-done((bf16[32,896]{1,0:T(8,128)(2,1)S(1)}, bf16[32,896]{1,0:T(8,128)(2,1)S(1)}, u32[]{:S(2)}, u32[]{:S(2)}) %collective-permute-start.6) | collective-permute-done | bytes 57376 | tf_op jit(solution)/shard_map/ppermute | solution.py:272
  23.2 0.2 collective-permute-start.8
  23.4 0.3 %collective-permute-done.9.cross_swap_b = bf16[32,896]{1,0:T(8,128)(2,1)S(1)} collective-permute-done((bf16[32,896]{1,0:T(8,128)(2,1)S(1)}, bf16[32,896]{1,0:T(8,128)(2,1)S(1)}, u32[]{:S(2)}, u32[]{:S(2)}) %collective-permute-start.9) | collective-permute-done | bytes 57376 | tf_op jit(solution)/shard_map/ppermute | solution.py:275
  23.8 0.0 collective-permute-done.4.far_swap
  23.8 0.0 collective-permute-done.5.near_swap
  23.8 0.7 %collective-permute-done.8.cross_swap_a = bf16[32,896]{1,0:T(8,128)(2,1)S(1)} collective-permute-done((bf16[32,896]{1,0:T(8,128)(2,1)S(1)}, bf16[32,896]{1,0:T(8,128)(2,1)S(1)}, u32[]{:S(2)}, u32[]{:S(2)}) %collective-permute-start.8) | collective-permute-done | bytes 57376 | tf_op jit(solution)/shard_map/ppermute | solution.py:275
  24.5 0.0 copy-start
  24.5 1.0 %copy-done = bf16[192,896]{1,0:T(8,128)(2,1)S(1)} copy-done((bf16[192,896]{1,0:T(8,128)(2,1)S(1)}, bf16[192,896]{1,0:T(8,128)(2,1)}, u32[]{:S(2)}) %copy-start) | copy-done | bytes 344088
  25.4 0.0 copy-start.1
  25.4 0.9 %copy-done.1 = bf16[64,896]{1,0:T(8,128)(2,1)S(1)} copy-done((bf16[64,896]{1,0:T(8,128)(2,1)S(1)}, bf16[64,896]{1,0:T(8,128)(2,1)}, u32[]{:S(2)}) %copy-start.1) | copy-done | bytes 114712
  26.3 1.3 %correlate.1 = bf16[3,64,512]{2,1,0:T(8,128)(2,1)} custom-call(bf16[192,896]{1,0:T(8,128)(2,1)S(1)} %copy-done, bf16[64,896]{1,0:T(8,128)(2,1)S(1)} %copy-done.1, bf16[64,896]{1,0:T(8,128)(2,1)S(1)} %collective-permute-done.1.side, bf16[64,896]{1,0:T(8,128)(2,1)S(1)} %collective-permute-done.2.near, ...), custom_call_target="tpu_custom_call" | custom-call | flops 176160768 | bytes 1376256 | tf_op jit(solution)/shard_map/correlate/pallas_call | solution.py:288
  (2 shorter events, 0.0 us)
Async XLA Ops:
  5.0 7.5 %collective-permute-start = (bf16[32,896]{1,0:T(8,128)(2,1)}, bf16[32,896]{1,0:T(8,128)(2,1)S(1)}, u32[]{:S(2)}, u32[]{:S(2)}) collective-permute-start(bf16[32,896]{1,0:T(8,128)(2,1)} %get-tuple-element.13), channel_id=1, source_target_pairs={{1,13},{3,15},{5,9},{7,11},{9,5},{11,7},{13,1},{15,3},{0,8},{2,10}... | collective-permute-start | bytes 172040 | tf_op jit(solution)/shard_map/ppermute | solution.py:268
  9.1 9.8 %collective-permute-start.2 = (bf16[64,896]{1,0:T(8,128)(2,1)}, bf16[64,896]{1,0:T(8,128)(2,1)S(1)}, u32[]{:S(2)}, u32[]{:S(2)}) collective-permute-start(bf16[64,896]{1,0:T(8,128)(2,1)} %get-tuple-element.12.own), channel_id=1, source_target_pairs={{1,7},{3,5},{5,3},{7,1},{9,15},{11,13},{13,11},{15,9},{0,4},{2,6},... | collective-permute-start | bytes 344072 | tf_op jit(solution)/shard_map/ppermute | solution.py:268
  10.7 8.2 %collective-permute-start.1 = (bf16[64,896]{1,0:T(8,128)(2,1)}, bf16[64,896]{1,0:T(8,128)(2,1)S(1)}, u32[]{:S(2)}, u32[]{:S(2)}) collective-permute-start(bf16[64,896]{1,0:T(8,128)(2,1)} %get-tuple-element.12.own), channel_id=1, source_target_pairs={{1,3},{3,1},{5,7},{7,5},{9,11},{11,9},{13,15},{15,13},{0,2},{2,0},... | collective-permute-start | bytes 344072 | tf_op jit(solution)/shard_map/ppermute | solution.py:268
  12.2 5.8 %collective-permute-start.3 = (bf16[32,896]{1,0:T(8,128)(2,1)}, bf16[32,896]{1,0:T(8,128)(2,1)S(1)}, u32[]{:S(2)}, u32[]{:S(2)}) collective-permute-start(bf16[32,896]{1,0:T(8,128)(2,1)} %get-tuple-element.15), channel_id=1, source_target_pairs={{1,13},{3,15},{5,9},{7,11},{9,5},{11,7},{13,1},{15,3},{0,8},{2,10}... | collective-permute-start | bytes 172040 | tf_op jit(solution)/shard_map/ppermute | solution.py:268
  18.0 5.8 %collective-permute-start.4 = (bf16[64,896]{1,0:T(8,128)(2,1)S(1)}, bf16[64,896]{1,0:T(8,128)(2,1)S(1)}, u32[]{:S(2)}, u32[]{:S(2)}) collective-permute-start(bf16[64,896]{1,0:T(8,128)(2,1)S(1)} %constant_dynamic-update-slice_fusion.far), channel_id=1, source_target_pairs={{0,1},{1,0},{2,3},{3,2},{4,5},{5,4},{6,7},{7,6},{8,9},{9,8},{10,11... | collective-permute-start | bytes 344072 | tf_op jit(solution)/shard_map/ppermute | solution.py:275
  18.1 3.7 %collective-permute-start.7 = (bf16[32,896]{1,0:T(8,128)(2,1)S(1)}, bf16[32,896]{1,0:T(8,128)(2,1)S(1)}, u32[]{:S(2)}, u32[]{:S(2)}) collective-permute-start(bf16[32,896]{1,0:T(8,128)(2,1)S(1)} %collective-permute-done.3), channel_id=1, source_target_pairs={{0,3},{1,2},{2,1},{3,0},{4,7},{5,6},{6,5},{7,4},{8,11},{9,10},{10,... | collective-permute-start | bytes 172040 | tf_op jit(solution)/shard_map/ppermute | solution.py:272
  18.9 4.9 %collective-permute-start.5 = (bf16[64,896]{1,0:T(8,128)(2,1)S(1)}, bf16[64,896]{1,0:T(8,128)(2,1)S(1)}, u32[]{:S(2)}, u32[]{:S(2)}) collective-permute-start(bf16[64,896]{1,0:T(8,128)(2,1)S(1)} %collective-permute-done.2.near), channel_id=1, source_target_pairs={{0,1},{1,0},{2,3},{3,2},{4,5},{5,4},{6,7},{7,6},{8,9},{9,8},{10,11... | collective-permute-start | bytes 344072 | tf_op jit(solution)/shard_map/ppermute | solution.py:275
  19.0 4.2 %collective-permute-start.6 = (bf16[32,896]{1,0:T(8,128)(2,1)S(1)}, bf16[32,896]{1,0:T(8,128)(2,1)S(1)}, u32[]{:S(2)}, u32[]{:S(2)}) collective-permute-start(bf16[32,896]{1,0:T(8,128)(2,1)S(1)} %collective-permute-done), channel_id=1, source_target_pairs={{0,3},{1,2},{2,1},{3,0},{4,7},{5,6},{6,5},{7,4},{8,11},{9,10},{10,... | collective-permute-start | bytes 172040 | tf_op jit(solution)/shard_map/ppermute | solution.py:272
  21.8 2.0 %collective-permute-start.9 = (bf16[32,896]{1,0:T(8,128)(2,1)S(1)}, bf16[32,896]{1,0:T(8,128)(2,1)S(1)}, u32[]{:S(2)}, u32[]{:S(2)}) collective-permute-start(bf16[32,896]{1,0:T(8,128)(2,1)S(1)} %collective-permute-done.7.cross_b), channel_id=1, source_target_pairs={{0,1},{1,0},{2,3},{3,2},{4,5},{5,4},{6,7},{7,6},{8,9},{9,8},{10,11... | collective-permute-start | bytes 172040 | tf_op jit(solution)/shard_map/ppermute | solution.py:275
  23.2 1.2 %collective-permute-start.8 = (bf16[32,896]{1,0:T(8,128)(2,1)S(1)}, bf16[32,896]{1,0:T(8,128)(2,1)S(1)}, u32[]{:S(2)}, u32[]{:S(2)}) collective-permute-start(bf16[32,896]{1,0:T(8,128)(2,1)S(1)} %collective-permute-done.6.cross_a), channel_id=1, source_target_pairs={{0,1},{1,0},{2,3},{3,2},{4,5},{5,4},{6,7},{7,6},{8,9},{9,8},{10,11... | collective-permute-start | bytes 172040 | tf_op jit(solution)/shard_map/ppermute | solution.py:275
  24.5 1.0 %copy-start = (bf16[192,896]{1,0:T(8,128)(2,1)S(1)}, bf16[192,896]{1,0:T(8,128)(2,1)}, u32[]{:S(2)}) copy-start(bf16[192,896]{1,0:T(8,128)(2,1)} %get-tuple-element.11.lags) | copy-start | bytes 1032196
  25.4 0.9 %copy-start.1 = (bf16[64,896]{1,0:T(8,128)(2,1)S(1)}, bf16[64,896]{1,0:T(8,128)(2,1)}, u32[]{:S(2)}) copy-start(bf16[64,896]{1,0:T(8,128)(2,1)} %get-tuple-element.12.own) | copy-start | bytes 344068

commit v3 on v2

--- a/solution.py
+++ b/solution.py
@@ -27,7 +27,8 @@
 LANES = 128
 SPARE = LANES - PER
 WIDTH = 2 * NB
-VMEM_MIB = 60
+VMEM_KIB = 40 * 1024
+CORR_KIB = 32 * 1024
 
 
 def bins_of(residue):
@@ -197,10 +198,10 @@
     return pl.pallas_call(
         functools.partial(spectra_kernel, lag_share),
         out_shape=[
-            jax.ShapeDtypeStruct((rows, WIDTH), jnp.bfloat16),
-            jax.ShapeDtypeStruct((rows // 2, WIDTH), jnp.bfloat16),
-            jax.ShapeDtypeStruct((rows // 2, WIDTH), jnp.bfloat16),
-            jax.ShapeDtypeStruct((lag_share * rows, WIDTH), jnp.bfloat16),
+            pltpu.VMEM((rows, WIDTH), jnp.bfloat16),
+            pltpu.VMEM((rows // 2, WIDTH), jnp.bfloat16),
+            pltpu.VMEM((rows // 2, WIDTH), jnp.bfloat16),
+            pltpu.VMEM((lag_share * rows, WIDTH), jnp.bfloat16),
         ],
         in_specs=[pl.BlockSpec(memory_space=pltpu.HBM)] * 5,
         out_specs=[pl.BlockSpec(memory_space=pltpu.VMEM)] * 4,
@@ -217,12 +218,12 @@
             pltpu.SemaphoreType.DMA((3,)),
             pltpu.SemaphoreType.DMA((1 + CHUNKS // GROUP,)),
         ],
-        compiler_params=pltpu.CompilerParams(vmem_limit_bytes=VMEM_MIB * 1024 * 1024),
+        compiler_params=pltpu.CompilerParams(vmem_limit_bytes=VMEM_KIB * 1024),
         cost_estimate=pl.CostEstimate(
             flops=2 * DEPTH * rows * 3072, bytes_accessed=DEPTH * 2048 + rows * S * 2, transcendentals=0
         ),
         name="spectra",
-    )(live_count, index_row, raw_rows, table, weights)
+    )(*(pltpu.with_memory_space_constraint(a, pltpu.HBM) for a in (live_count, index_row, raw_rows, table, weights)))
 
 
 def correlate(lag_rows, columns):
@@ -278,8 +279,9 @@
     far_b = split_move(6, 4)(second)
     side = split_move(1, 1)(own)
     near = split_move(3, 2)(own)
-    far_a_ready, side = lax.optimization_barrier((far_a, side))
-    cross_a = forward(far_a_ready)
+    q, near = lax.optimization_barrier((far_a, near))
+    cross_a = forward(q)
+    _, cross_a = lax.optimization_barrier((far_b, cross_a))
     cross_b = forward(far_b)
     far = jnp.concatenate([far_a, far_b], axis=0)
     far_swap, near_swap = swap(far), swap(near)
@@ -290,7 +292,7 @@
         out_shape=jax.ShapeDtypeStruct((lag_share, rows, 8 * rows), jnp.bfloat16),
         in_specs=[pl.BlockSpec(memory_space=pltpu.VMEM)] * 11,
         out_specs=pl.BlockSpec(memory_space=pltpu.VMEM),
-        compiler_params=pltpu.CompilerParams(vmem_limit_bytes=32 * 1024 * 1024),
+        compiler_params=pltpu.CompilerParams(vmem_limit_bytes=CORR_KIB * 1024),
         cost_estimate=pl.CostEstimate(
             flops=2 * lag_share * rows * 8 * rows * WIDTH, bytes_accessed=12 * rows * WIDTH * 2, transcendentals=0
         ),

time: 27.8 us -> 21.7 us (0.78)
  waiting for transfers between devices: 8.21 us -> 5.66 us
  local copies, waits for them, and re-layouts: 1.89 us -> 0.02 us
  starting transfers between devices: 11.2 us -> 10.3 us
  Pallas kernels: 6.32 us -> 5.56 us
    ppermute x4, waiting for transfers between devices: 5.45 us -> 3.56 us  [split_move(): return lambda a: lax.ppermute(a, ('chan', 'pair'), pairs)]
    unnamed x5 -> x1, local copies, waits for them, and re-layouts: 1.88 us -> 0.01 us
    ppermute x2, starting transfers between devices: 2.19 us -> 1.4 us  [forward(): return lax.ppermute(a, ('chan', 'pair'), pairs)]
    pallas_call x1, Pallas kernels: 5.03 us -> 4.28 us  [spectra(): pl.pallas_call(functools.partial(spectra_kernel, lag_share), out_shape=[p...]
    ppermute x2, waiting for transfers between devices: 1.73 us -> 1.22 us  [forward(): return lax.ppermute(a, ('chan', 'pair'), pairs)]
where the time goes in v3:
time: 21.7 us; the launch traced here: 21.6 us
  starting transfers between devices  10.3 us (47%)
  waiting for transfers between devices  5.66 us (26%)
  Pallas kernels  5.56 us (26%)
    ppermute x4, starting transfers between devices, split_move(): return lambda a: lax.ppermute(a, ('chan', 'pair'), pairs)  7.5 us
    pallas_call x1, Pallas kernels, spectra(): pl.pallas_call(functools.partial(spectra_kernel, lag_share), out_shape=[p...  4.28 us
    ppermute x4, waiting for transfers between devices, split_move(): return lambda a: lax.ppermute(a, ('chan', 'pair'), pairs)  3.56 us
    ppermute x4, starting transfers between devices, swap(): return lax.ppermute(a, 'pair', [(0, 1), (1, 0)])  1.42 us
    ppermute x2, starting transfers between devices, forward(): return lax.ppermute(a, ('chan', 'pair'), pairs)  1.4 us
    pallas_call x1, Pallas kernels, exchange_eight(): pl.pallas_call(eight_kernel, out_shape=jax.ShapeDtypeStruct((lag_share, r...  1.29 us
    ppermute x2, waiting for transfers between devices, forward(): return lax.ppermute(a, ('chan', 'pair'), pairs)  1.22 us
    ppermute x4, waiting for transfers between devices, swap(): return lax.ppermute(a, 'pair', [(0, 1), (1, 0)])  0.89 us
  transfers between devices with their start and end apart: 10, of which 5 were waited for; matrix products, arithmetic and copies ran while one was open for 0% of the time, Pallas kernels for 0%

profile of v3, /device:TPU:0, one launch (start us, length us, event | category | flops | bytes accessed | tf_op | source)
XLA Modules:
  0.0 21.6 jit_solution(1559475510581187787)
XLA Ops:
  0.0 4.3 %spectra.1 = (bf16[64,896]{1,0:T(8,128)(2,1)S(1)}, bf16[32,896]{1,0:T(8,128)(2,1)S(1)}, bf16[32,896]{1,0:T(8,128)(2,1)S(1)}, bf16[192,896]{1,0:T(8,128)(2,1)S(1)}) custom-call(s32[8]{0:T(128)} %count_ref.1, s32[1,64]{1,0:T(1,128)} %index_ref.1, bf16[64,12000]{1,0:T(8,128)(2,1)} %bitcast.1, bf16[3072,1024]{1,0:T(8,128)(2,1)} %constant.5.clone.table_ref, ...), custom_call_target="tpu_custom_call" | custom-call | flops 1207959552 | bytes 7827456 | tf_op jit(solution)/shard_map/spectra/pallas_call | solution.py:198
  4.3 4.1 %collective-permute-start.3 = (bf16[32,896]{1,0:T(8,128)(2,1)S(1)}, bf16[32,896]{1,0:T(8,128)(2,1)S(1)}, u32[]{:S(2)}, u32[]{:S(2)}) collective-permute-start(bf16[32,896]{1,0:T(8,128)(2,1)S(1)} %get-tuple-element.16), channel_id=1, source_target_pairs={{1,13},{3,15},{5,9},{7,11},{9,5},{11,7},{13,1},{15,3},{0,8},{2,10}... | collective-permute-start | bytes 172040 | tf_op jit(solution)/shard_map/ppermute | solution.py:269
  8.4 0.1 collective-permute-start.1
  8.5 1.8 %collective-permute-start.2 = (bf16[64,896]{1,0:T(8,128)(2,1)S(1)}, bf16[64,896]{1,0:T(8,128)(2,1)S(1)}, u32[]{:S(2)}, u32[]{:S(2)}) collective-permute-start(bf16[64,896]{1,0:T(8,128)(2,1)S(1)} %get-tuple-element.13.own), channel_id=1, source_target_pairs={{1,7},{3,5},{5,3},{7,1},{9,15},{11,13},{13,11},{15,9},{0,4},{2,6},... | collective-permute-start | bytes 344072 | tf_op jit(solution)/shard_map/ppermute | solution.py:269
  10.3 1.5 %collective-permute-start = (bf16[64,896]{1,0:T(8,128)(2,1)S(1)}, bf16[64,896]{1,0:T(8,128)(2,1)S(1)}, u32[]{:S(2)}, u32[]{:S(2)}) collective-permute-start(bf16[64,896]{1,0:T(8,128)(2,1)S(1)} %get-tuple-element.13.own), channel_id=1, source_target_pairs={{1,3},{3,1},{5,7},{7,5},{9,11},{11,9},{13,15},{15,13},{0,2},{2,0},... | collective-permute-start | bytes 344072 | tf_op jit(solution)/shard_map/ppermute | solution.py:269
  11.8 0.3 %collective-permute-done.3 = bf16[32,896]{1,0:T(8,128)(2,1)S(1)} collective-permute-done((bf16[32,896]{1,0:T(8,128)(2,1)S(1)}, bf16[32,896]{1,0:T(8,128)(2,1)S(1)}, u32[]{:S(2)}, u32[]{:S(2)}) %collective-permute-start.3) | collective-permute-done | bytes 57376 | tf_op jit(solution)/shard_map/ppermute | solution.py:269
  12.1 0.0 collective-permute-start.7
  12.1 2.3 %collective-permute-done.1 = bf16[32,896]{1,0:T(8,128)(2,1)S(1)} collective-permute-done((bf16[32,896]{1,0:T(8,128)(2,1)S(1)}, bf16[32,896]{1,0:T(8,128)(2,1)S(1)}, u32[]{:S(2)}, u32[]{:S(2)}) %collective-permute-start.1) | collective-permute-done | bytes 57376 | tf_op jit(solution)/shard_map/ppermute | solution.py:269
  14.5 0.9 %collective-permute-done.2.near = bf16[64,896]{1,0:T(8,128)(2,1)S(1)} collective-permute-done((bf16[64,896]{1,0:T(8,128)(2,1)S(1)}, bf16[64,896]{1,0:T(8,128)(2,1)S(1)}, u32[]{:S(2)}, u32[]{:S(2)}) %collective-permute-start.2) | collective-permute-done | bytes 114720 | tf_op jit(solution)/shard_map/ppermute | solution.py:269
  15.4 1.4 %collective-permute-start.6 = (bf16[32,896]{1,0:T(8,128)(2,1)S(1)}, bf16[32,896]{1,0:T(8,128)(2,1)S(1)}, u32[]{:S(2)}, u32[]{:S(2)}) collective-permute-start(bf16[32,896]{1,0:T(8,128)(2,1)S(1)} %collective-permute-done.1), channel_id=1, source_target_pairs={{0,3},{1,2},{2,1},{3,0},{4,7},{5,6},{6,5},{7,4},{8,11},{9,10},{10,... | collective-permute-start | bytes 172040 | tf_op jit(solution)/shard_map/ppermute | solution.py:273
  16.8 0.5 %collective-permute-start.4 = (bf16[64,896]{1,0:T(8,128)(2,1)S(1)}, bf16[64,896]{1,0:T(8,128)(2,1)S(1)}, u32[]{:S(2)}, u32[]{:S(2)}) collective-permute-start(bf16[64,896]{1,0:T(8,128)(2,1)S(1)} %constant_dynamic-update-slice_fusion.far), channel_id=1, source_target_pairs={{0,1},{1,0},{2,3},{3,2},{4,5},{5,4},{6,7},{7,6},{8,9},{9,8},{10,11... | collective-permute-start | bytes 344072 | tf_op jit(solution)/shard_map/ppermute | solution.py:276
  17.2 0.1 collective-permute-start.5
  17.3 0.0 collective-permute-done.7.cross_b
  17.3 0.4 %collective-permute-start.9 = (bf16[32,896]{1,0:T(8,128)(2,1)S(1)}, bf16[32,896]{1,0:T(8,128)(2,1)S(1)}, u32[]{:S(2)}, u32[]{:S(2)}) collective-permute-start(bf16[32,896]{1,0:T(8,128)(2,1)S(1)} %collective-permute-done.7.cross_b), channel_id=1, source_target_pairs={{0,1},{1,0},{2,3},{3,2},{4,5},{5,4},{6,7},{7,6},{8,9},{9,8},{10,11... | collective-permute-start | bytes 172040 | tf_op jit(solution)/shard_map/ppermute | solution.py:276
  17.7 1.2 %collective-permute-done.6.cross_a = bf16[32,896]{1,0:T(8,128)(2,1)S(1)} collective-permute-done((bf16[32,896]{1,0:T(8,128)(2,1)S(1)}, bf16[32,896]{1,0:T(8,128)(2,1)S(1)}, u32[]{:S(2)}, u32[]{:S(2)}) %collective-permute-start.6) | collective-permute-done | bytes 57376 | tf_op jit(solution)/shard_map/ppermute | solution.py:273
  19.0 0.4 %collective-permute-start.8 = (bf16[32,896]{1,0:T(8,128)(2,1)S(1)}, bf16[32,896]{1,0:T(8,128)(2,1)S(1)}, u32[]{:S(2)}, u32[]{:S(2)}) collective-permute-start(bf16[32,896]{1,0:T(8,128)(2,1)S(1)} %collective-permute-done.6.cross_a), channel_id=1, source_target_pairs={{0,1},{1,0},{2,3},{3,2},{4,5},{5,4},{6,7},{7,6},{8,9},{9,8},{10,11... | collective-permute-start | bytes 172040 | tf_op jit(solution)/shard_map/ppermute | solution.py:276
  19.4 0.0 collective-permute-done.side
  19.4 0.0 collective-permute-done.9.cross_swap_b
  19.4 0.0 collective-permute-done.4.far_swap
  19.4 0.9 %collective-permute-done.8.cross_swap_a = bf16[32,896]{1,0:T(8,128)(2,1)S(1)} collective-permute-done((bf16[32,896]{1,0:T(8,128)(2,1)S(1)}, bf16[32,896]{1,0:T(8,128)(2,1)S(1)}, u32[]{:S(2)}, u32[]{:S(2)}) %collective-permute-start.8) | collective-permute-done | bytes 57376 | tf_op jit(solution)/shard_map/ppermute | solution.py:276
  20.3 0.0 collective-permute-done.5.near_swap
  20.3 1.3 %correlate.1 = bf16[3,64,512]{2,1,0:T(8,128)(2,1)} custom-call(bf16[192,896]{1,0:T(8,128)(2,1)S(1)} %get-tuple-element.12.lags, bf16[64,896]{1,0:T(8,128)(2,1)S(1)} %get-tuple-element.13.own, bf16[64,896]{1,0:T(8,128)(2,1)S(1)} %collective-permute-done.side, bf16[64,896]{1,0:T(8,128)(2,1)S(1)} %collective-permute-done.2.near, ...), custom_call_target="tpu_custom_call" | custom-call | flops 176160768 | bytes 1376256 | tf_op jit(solution)/shard_map/correlate/pallas_call | solution.py:290
  (2 shorter events, 0.0 us)
Async XLA Ops:
  4.3 7.8 %collective-permute-start.3 = (bf16[32,896]{1,0:T(8,128)(2,1)S(1)}, bf16[32,896]{1,0:T(8,128)(2,1)S(1)}, u32[]{:S(2)}, u32[]{:S(2)}) collective-permute-start(bf16[32,896]{1,0:T(8,128)(2,1)S(1)} %get-tuple-element.16), channel_id=1, source_target_pairs={{1,13},{3,15},{5,9},{7,11},{9,5},{11,7},{13,1},{15,3},{0,8},{2,10}... | collective-permute-start | bytes 172040 | tf_op jit(solution)/shard_map/ppermute | solution.py:269
  8.4 6.1 %collective-permute-start.1 = (bf16[32,896]{1,0:T(8,128)(2,1)S(1)}, bf16[32,896]{1,0:T(8,128)(2,1)S(1)}, u32[]{:S(2)}, u32[]{:S(2)}) collective-permute-start(bf16[32,896]{1,0:T(8,128)(2,1)S(1)} %get-tuple-element.14), channel_id=1, source_target_pairs={{1,13},{3,15},{5,9},{7,11},{9,5},{11,7},{13,1},{15,3},{0,8},{2,10}... | collective-permute-start | bytes 172040 | tf_op jit(solution)/shard_map/ppermute | solution.py:269
  8.5 6.9 %collective-permute-start.2 = (bf16[64,896]{1,0:T(8,128)(2,1)S(1)}, bf16[64,896]{1,0:T(8,128)(2,1)S(1)}, u32[]{:S(2)}, u32[]{:S(2)}) collective-permute-start(bf16[64,896]{1,0:T(8,128)(2,1)S(1)} %get-tuple-element.13.own), channel_id=1, source_target_pairs={{1,7},{3,5},{5,3},{7,1},{9,15},{11,13},{13,11},{15,9},{0,4},{2,6},... | collective-permute-start | bytes 344072 | tf_op jit(solution)/shard_map/ppermute | solution.py:269
  10.3 9.1 %collective-permute-start = (bf16[64,896]{1,0:T(8,128)(2,1)S(1)}, bf16[64,896]{1,0:T(8,128)(2,1)S(1)}, u32[]{:S(2)}, u32[]{:S(2)}) collective-permute-start(bf16[64,896]{1,0:T(8,128)(2,1)S(1)} %get-tuple-element.13.own), channel_id=1, source_target_pairs={{1,3},{3,1},{5,7},{7,5},{9,11},{11,9},{13,15},{15,13},{0,2},{2,0},... | collective-permute-start | bytes 344072 | tf_op jit(solution)/shard_map/ppermute | solution.py:269
  12.1 5.2 %collective-permute-start.7 = (bf16[32,896]{1,0:T(8,128)(2,1)S(1)}, bf16[32,896]{1,0:T(8,128)(2,1)S(1)}, u32[]{:S(2)}, u32[]{:S(2)}) collective-permute-start(bf16[32,896]{1,0:T(8,128)(2,1)S(1)} %collective-permute-done.3), channel_id=1, source_target_pairs={{0,3},{1,2},{2,1},{3,0},{4,7},{5,6},{6,5},{7,4},{8,11},{9,10},{10,... | collective-permute-start | bytes 172040 | tf_op jit(solution)/shard_map/ppermute | solution.py:273
  15.4 3.6 %collective-permute-start.6 = (bf16[32,896]{1,0:T(8,128)(2,1)S(1)}, bf16[32,896]{1,0:T(8,128)(2,1)S(1)}, u32[]{:S(2)}, u32[]{:S(2)}) collective-permute-start(bf16[32,896]{1,0:T(8,128)(2,1)S(1)} %collective-permute-done.1), channel_id=1, source_target_pairs={{0,3},{1,2},{2,1},{3,0},{4,7},{5,6},{6,5},{7,4},{8,11},{9,10},{10,... | collective-permute-start | bytes 172040 | tf_op jit(solution)/shard_map/ppermute | solution.py:273
  16.8 2.6 %collective-permute-start.4 = (bf16[64,896]{1,0:T(8,128)(2,1)S(1)}, bf16[64,896]{1,0:T(8,128)(2,1)S(1)}, u32[]{:S(2)}, u32[]{:S(2)}) collective-permute-start(bf16[64,896]{1,0:T(8,128)(2,1)S(1)} %constant_dynamic-update-slice_fusion.far), channel_id=1, source_target_pairs={{0,1},{1,0},{2,3},{3,2},{4,5},{5,4},{6,7},{7,6},{8,9},{9,8},{10,11... | collective-permute-start | bytes 344072 | tf_op jit(solution)/shard_map/ppermute | solution.py:276
  17.2 3.1 %collective-permute-start.5 = (bf16[64,896]{1,0:T(8,128)(2,1)S(1)}, bf16[64,896]{1,0:T(8,128)(2,1)S(1)}, u32[]{:S(2)}, u32[]{:S(2)}) collective-permute-start(bf16[64,896]{1,0:T(8,128)(2,1)S(1)} %collective-permute-done.2.near), channel_id=1, source_target_pairs={{0,1},{1,0},{2,3},{3,2},{4,5},{5,4},{6,7},{7,6},{8,9},{9,8},{10,11... | collective-permute-start | bytes 344072 | tf_op jit(solution)/shard_map/ppermute | solution.py:276
  17.3 2.1 %collective-permute-start.9 = (bf16[32,896]{1,0:T(8,128)(2,1)S(1)}, bf16[32,896]{1,0:T(8,128)(2,1)S(1)}, u32[]{:S(2)}, u32[]{:S(2)}) collective-permute-start(bf16[32,896]{1,0:T(8,128)(2,1)S(1)} %collective-permute-done.7.cross_b), channel_id=1, source_target_pairs={{0,1},{1,0},{2,3},{3,2},{4,5},{5,4},{6,7},{7,6},{8,9},{9,8},{10,11... | collective-permute-start | bytes 172040 | tf_op jit(solution)/shard_map/ppermute | solution.py:276
  19.0 1.3 %collective-permute-start.8 = (bf16[32,896]{1,0:T(8,128)(2,1)S(1)}, bf16[32,896]{1,0:T(8,128)(2,1)S(1)}, u32[]{:S(2)}, u32[]{:S(2)}) collective-permute-start(bf16[32,896]{1,0:T(8,128)(2,1)S(1)} %collective-permute-done.6.cross_a), channel_id=1, source_target_pairs={{0,1},{1,0},{2,3},{3,2},{4,5},{5,4},{6,7},{7,6},{8,9},{9,8},{10,11... | collective-permute-start | bytes 172040 | tf_op jit(solution)/shard_map/ppermute | solution.py:276

commit v4 on v3

--- a/solution.py
+++ b/solution.py
@@ -21,7 +21,7 @@
 CHUNK = 256
 CHUNKS = -(-QUARTER // CHUNK)
 DEPTH = CHUNKS * CHUNK
-GROUP = 2
+GROUPS = (2, 2, 2, 2, 2, 2)
 RES = (0, 2, 1, 3)
 PER = NB // 4
 LANES = 128
@@ -36,15 +36,15 @@
 
 
 def quarter_table():
-    table = np.zeros((DEPTH, 8 * LANES), np.float32)
+    table = np.zeros((DEPTH, 8 * LANES), np.float64)
     t = np.arange(QUARTER, dtype=np.int64)
+    step = np.float64(np.float32(2.0 * np.pi / S))
     for place, residue in enumerate(RES):
-        phase = t[:, None] * (F0 + bins_of(residue))[None, :] % S
-        angles = phase.astype(np.float32) * np.float32(2.0 * np.pi / S)
+        angles = (t[:, None] * (F0 + bins_of(residue))[None, :] % S) * step
         at = 2 * place * LANES
-        table[:QUARTER, at : at + PER] = np.cos(angles.astype(np.float64))
-        table[:QUARTER, at + LANES : at + LANES + PER] = -np.sin(angles.astype(np.float64))
-    return table.astype(jnp.bfloat16)
+        table[:QUARTER, at : at + PER] = np.cos(angles)
+        table[:QUARTER, at + LANES : at + LANES + PER] = -np.sin(angles)
+    return table.astype(np.float32).astype(jnp.bfloat16)
 
 
 def packed_bins():
@@ -106,8 +106,9 @@
     weight_copy = pltpu.make_async_copy(weight_ref.at[lax.axis_index("pair")], weights, small_sems.at[2])
     weight_copy.start()
     copies = []
-    for g in range(CHUNKS // GROUP):
-        span = pl.ds(g * GROUP * CHUNK, GROUP * CHUNK)
+    ends = np.cumsum(GROUPS)
+    for g, end in enumerate(ends):
+        span = pl.ds(int(end - GROUPS[g]) * CHUNK, GROUPS[g] * CHUNK)
         copies.append(pltpu.make_async_copy(table_ref.at[span, :], table.at[span, :], sems.at[1 + g]))
         copies[-1].start()
     tail[...] = jnp.zeros_like(tail)
@@ -133,8 +134,8 @@
     even = jnp.zeros((2 * rows, 2 * LANES), jnp.float32)
     half = jnp.zeros((2 * rows, 2 * LANES), jnp.float32)
     odd = jnp.zeros((4 * rows, 4 * LANES), jnp.float32)
-    for g in range(CHUNKS // GROUP):
-        for c in range(g * GROUP, (g + 1) * GROUP):
+    for g, end in enumerate(ends):
+        for c in range(int(end) - GROUPS[g], int(end)):
             at = c * CHUNK
             x0, x1, x2, x3 = (window(m * QUARTER + at) for m in range(4))
             sum02, sum13 = x0 + x2, x1 + x3
@@ -148,7 +149,7 @@
                 target[first : first + rows, at : at + CHUNK] = high
                 target[first + rows : first + 2 * rows, at : at + CHUNK] = low
         copies[g].wait()
-        lo, hi = g * GROUP * CHUNK, (g + 1) * GROUP * CHUNK
+        lo, hi = int(end - GROUPS[g]) * CHUNK, int(end) * CHUNK
         even += jnp.dot(y_even[:, lo:hi], table[lo:hi, : 2 * LANES], preferred_element_type=jnp.float32)
         half += jnp.dot(y_half[:, lo:hi], table[lo:hi, 2 * LANES : 4 * LANES], preferred_element_type=jnp.float32)
         odd += jnp.dot(y_odd[:, lo:hi], table[lo:hi, 4 * LANES :], preferred_element_type=jnp.float32)
@@ -216,7 +217,7 @@
             pltpu.VMEM(index_row.shape, jnp.int32),
             pltpu.VMEM(weights.shape[1:], jnp.float32),
             pltpu.SemaphoreType.DMA((3,)),
-            pltpu.SemaphoreType.DMA((1 + CHUNKS // GROUP,)),
+            pltpu.SemaphoreType.DMA((1 + len(GROUPS),)),
         ],
         compiler_params=pltpu.CompilerParams(vmem_limit_bytes=VMEM_KIB * 1024),
         cost_estimate=pl.CostEstimate(
@@ -279,13 +280,15 @@
     far_b = split_move(6, 4)(second)
     side = split_move(1, 1)(own)
     near = split_move(3, 2)(own)
-    q, near = lax.optimization_barrier((far_a, near))
-    cross_a = forward(q)
-    _, cross_a = lax.optimization_barrier((far_b, cross_a))
+    cross_a = forward(far_a)
     cross_b = forward(far_b)
+    cross_a, near, side = lax.optimization_barrier((cross_a, near, side))
+    cross_swap_a = swap(cross_a)
+    cross_b, cross_swap_a = lax.optimization_barrier((cross_b, cross_swap_a))
     far = jnp.concatenate([far_a, far_b], axis=0)
-    far_swap, near_swap = swap(far), swap(near)
-    cross_swap_a, cross_swap_b = swap(cross_a), swap(cross_b)
+    far_swap = swap(far)
+    near_swap = swap(near)
+    cross_swap_b = swap(cross_b)
     lag_share, rows = lags.shape[0] // own.shape[0], own.shape[0]
     return pl.pallas_call(
         eight_kernel,

time: 21.7 us -> 21.4 us (0.986)
  starting transfers between devices: 10.3 us -> 8.84 us
  waiting for transfers between devices: 5.66 us -> 6.8 us
    ppermute x2, waiting for transfers between devices: 1.22 us -> 2.62 us  [forward(): return lax.ppermute(a, ('chan', 'pair'), pairs)]
    ppermute x2, starting transfers between devices: 1.4 us -> 0.46 us  [forward(): return lax.ppermute(a, ('chan', 'pair'), pairs)]
    ppermute x4, waiting for transfers between devices: 3.56 us -> 2.94 us  [split_move(): return lambda a: lax.ppermute(a, ('chan', 'pair'), pairs)]
    ppermute x4, starting transfers between devices: 1.42 us -> 0.88 us  [swap(): return lax.ppermute(a, 'pair', [(0, 1), (1, 0)])]
    ppermute x4, waiting for transfers between devices: 0.89 us -> 1.24 us  [swap(): return lax.ppermute(a, 'pair', [(0, 1), (1, 0)])]
where the time goes in v4:
time: 21.4 us; the launch traced here: 21.2 us
  starting transfers between devices  8.84 us (41%)
  waiting for transfers between devices  6.8 us (32%)
  Pallas kernels  5.56 us (26%)
    ppermute x4, starting transfers between devices, split_move(): return lambda a: lax.ppermute(a, ('chan', 'pair'), pairs)  7.5 us
    pallas_call x1, Pallas kernels, spectra(): pl.pallas_call(functools.partial(spectra_kernel, lag_share), out_shape=[p...  4.28 us
    ppermute x4, waiting for transfers between devices, split_move(): return lambda a: lax.ppermute(a, ('chan', 'pair'), pairs)  2.94 us
    ppermute x2, waiting for transfers between devices, forward(): return lax.ppermute(a, ('chan', 'pair'), pairs)  2.62 us
    pallas_call x1, Pallas kernels, exchange_eight(): pl.pallas_call(eight_kernel, out_shape=jax.ShapeDtypeStruct((lag_share, r...  1.29 us
    ppermute x4, waiting for transfers between devices, swap(): return lax.ppermute(a, 'pair', [(0, 1), (1, 0)])  1.24 us
    ppermute x4, starting transfers between devices, swap(): return lax.ppermute(a, 'pair', [(0, 1), (1, 0)])  0.88 us
    ppermute x2, starting transfers between devices, forward(): return lax.ppermute(a, ('chan', 'pair'), pairs)  0.46 us
  transfers between devices with their start and end apart: 10, of which 5 were waited for; matrix products, arithmetic and copies ran while one was open for 0% of the time, Pallas kernels for 0%

profile of v4, /device:TPU:0, one launch (start us, length us, event | category | flops | bytes accessed | tf_op | source)
XLA Modules:
  0.0 21.2 jit_solution(7746426033756183007)
XLA Ops:
  0.0 4.3 %spectra.1 = (bf16[64,896]{1,0:T(8,128)(2,1)S(1)}, bf16[32,896]{1,0:T(8,128)(2,1)S(1)}, bf16[32,896]{1,0:T(8,128)(2,1)S(1)}, bf16[192,896]{1,0:T(8,128)(2,1)S(1)}) custom-call(s32[8]{0:T(128)} %count_ref.1, s32[1,64]{1,0:T(1,128)} %index_ref.1, bf16[64,12000]{1,0:T(8,128)(2,1)} %bitcast.1, bf16[3072,1024]{1,0:T(8,128)(2,1)} %constant.5.clone.table_ref, ...), custom_call_target="tpu_custom_call" | custom-call | flops 1207959552 | bytes 7827456 | tf_op jit(solution)/shard_map/spectra/pallas_call | solution.py:199
  4.3 4.1 %collective-permute-start = (bf16[32,896]{1,0:T(8,128)(2,1)S(1)}, bf16[32,896]{1,0:T(8,128)(2,1)S(1)}, u32[]{:S(2)}, u32[]{:S(2)}) collective-permute-start(bf16[32,896]{1,0:T(8,128)(2,1)S(1)} %get-tuple-element.16), channel_id=1, source_target_pairs={{1,13},{3,15},{5,9},{7,11},{9,5},{11,7},{13,1},{15,3},{0,8},{2,10}... | collective-permute-start | bytes 172040 | tf_op jit(solution)/shard_map/ppermute | solution.py:270
  8.4 0.1 collective-permute-start.4
  8.5 1.8 %collective-permute-start.3 = (bf16[64,896]{1,0:T(8,128)(2,1)S(1)}, bf16[64,896]{1,0:T(8,128)(2,1)S(1)}, u32[]{:S(2)}, u32[]{:S(2)}) collective-permute-start(bf16[64,896]{1,0:T(8,128)(2,1)S(1)} %get-tuple-element.15.own), channel_id=1, source_target_pairs={{1,3},{3,1},{5,7},{7,5},{9,11},{11,9},{13,15},{15,13},{0,2},{2,0},... | collective-permute-start | bytes 344072 | tf_op jit(solution)/shard_map/ppermute | solution.py:270
  10.2 1.6 %collective-permute-start.2 = (bf16[64,896]{1,0:T(8,128)(2,1)S(1)}, bf16[64,896]{1,0:T(8,128)(2,1)S(1)}, u32[]{:S(2)}, u32[]{:S(2)}) collective-permute-start(bf16[64,896]{1,0:T(8,128)(2,1)S(1)} %get-tuple-element.15.own), channel_id=1, source_target_pairs={{1,7},{3,5},{5,3},{7,1},{9,15},{11,13},{13,11},{15,9},{0,4},{2,6},... | collective-permute-start | bytes 344072 | tf_op jit(solution)/shard_map/ppermute | solution.py:270
  11.8 0.3 %collective-permute-done = bf16[32,896]{1,0:T(8,128)(2,1)S(1)} collective-permute-done((bf16[32,896]{1,0:T(8,128)(2,1)S(1)}, bf16[32,896]{1,0:T(8,128)(2,1)S(1)}, u32[]{:S(2)}, u32[]{:S(2)}) %collective-permute-start) | collective-permute-done | bytes 57376 | tf_op jit(solution)/shard_map/ppermute | solution.py:270
  12.1 0.0 collective-permute-start.1
  12.1 2.6 %collective-permute-done.4 = bf16[32,896]{1,0:T(8,128)(2,1)S(1)} collective-permute-done((bf16[32,896]{1,0:T(8,128)(2,1)S(1)}, bf16[32,896]{1,0:T(8,128)(2,1)S(1)}, u32[]{:S(2)}, u32[]{:S(2)}) %collective-permute-start.4) | collective-permute-done | bytes 57376 | tf_op jit(solution)/shard_map/ppermute | solution.py:270
  14.7 0.5 %collective-permute-start.7 = (bf16[32,896]{1,0:T(8,128)(2,1)S(1)}, bf16[32,896]{1,0:T(8,128)(2,1)S(1)}, u32[]{:S(2)}, u32[]{:S(2)}) collective-permute-start(bf16[32,896]{1,0:T(8,128)(2,1)S(1)} %collective-permute-done.4), channel_id=1, source_target_pairs={{0,3},{1,2},{2,1},{3,0},{4,7},{5,6},{6,5},{7,4},{8,11},{9,10},{10,... | collective-permute-start | bytes 172040 | tf_op jit(solution)/shard_map/ppermute | solution.py:274
  15.2 1.8 %collective-permute-done.1.cross_a = bf16[32,896]{1,0:T(8,128)(2,1)S(1)} collective-permute-done((bf16[32,896]{1,0:T(8,128)(2,1)S(1)}, bf16[32,896]{1,0:T(8,128)(2,1)S(1)}, u32[]{:S(2)}, u32[]{:S(2)}) %collective-permute-start.1) | collective-permute-done | bytes 57376 | tf_op jit(solution)/shard_map/ppermute | solution.py:274
  17.0 0.0 collective-permute-done.3.side
  17.0 0.0 collective-permute-done.2.near
  17.0 0.3 %collective-permute-start.8 = (bf16[32,896]{1,0:T(8,128)(2,1)S(1)}, bf16[32,896]{1,0:T(8,128)(2,1)S(1)}, u32[]{:S(2)}, u32[]{:S(2)}) collective-permute-start(bf16[32,896]{1,0:T(8,128)(2,1)S(1)} %collective-permute-done.1.cross_a), channel_id=1, source_target_pairs={{0,1},{1,0},{2,3},{3,2},{4,5},{5,4},{6,7},{7,6},{8,9},{9,8},{10,11... | collective-permute-start | bytes 172040 | tf_op jit(solution)/shard_map/ppermute | solution.py:277
  17.3 0.3 %collective-permute-start.5 = (bf16[64,896]{1,0:T(8,128)(2,1)S(1)}, bf16[64,896]{1,0:T(8,128)(2,1)S(1)}, u32[]{:S(2)}, u32[]{:S(2)}) collective-permute-start(bf16[64,896]{1,0:T(8,128)(2,1)S(1)} %constant_dynamic-update-slice_fusion.far), channel_id=1, source_target_pairs={{0,1},{1,0},{2,3},{3,2},{4,5},{5,4},{6,7},{7,6},{8,9},{9,8},{10,11... | collective-permute-start | bytes 344072 | tf_op jit(solution)/shard_map/ppermute | solution.py:277
  17.6 0.3 %collective-permute-start.6 = (bf16[64,896]{1,0:T(8,128)(2,1)S(1)}, bf16[64,896]{1,0:T(8,128)(2,1)S(1)}, u32[]{:S(2)}, u32[]{:S(2)}) collective-permute-start(bf16[64,896]{1,0:T(8,128)(2,1)S(1)} %collective-permute-done.2.near), channel_id=1, source_target_pairs={{0,1},{1,0},{2,3},{3,2},{4,5},{5,4},{6,7},{7,6},{8,9},{9,8},{10,11... | collective-permute-start | bytes 344072 | tf_op jit(solution)/shard_map/ppermute | solution.py:277
  17.9 0.8 %collective-permute-done.7.cross_b = bf16[32,896]{1,0:T(8,128)(2,1)S(1)} collective-permute-done((bf16[32,896]{1,0:T(8,128)(2,1)S(1)}, bf16[32,896]{1,0:T(8,128)(2,1)S(1)}, u32[]{:S(2)}, u32[]{:S(2)}) %collective-permute-start.7) | collective-permute-done | bytes 57376 | tf_op jit(solution)/shard_map/ppermute | solution.py:274
  18.7 0.0 collective-permute-done.8.cross_swap_a
  18.7 0.0 collective-permute-start.9
  18.7 0.0 collective-permute-done.5.far_swap
  18.7 1.2 %collective-permute-done.9.cross_swap_b = bf16[32,896]{1,0:T(8,128)(2,1)S(1)} collective-permute-done((bf16[32,896]{1,0:T(8,128)(2,1)S(1)}, bf16[32,896]{1,0:T(8,128)(2,1)S(1)}, u32[]{:S(2)}, u32[]{:S(2)}) %collective-permute-start.9) | collective-permute-done | bytes 57376 | tf_op jit(solution)/shard_map/ppermute | solution.py:277
  20.0 0.0 collective-permute-done.6.near_swap
  20.0 1.3 %correlate.1 = bf16[3,64,512]{2,1,0:T(8,128)(2,1)} custom-call(bf16[192,896]{1,0:T(8,128)(2,1)S(1)} %get-tuple-element.14.lags, bf16[64,896]{1,0:T(8,128)(2,1)S(1)} %get-tuple-element.15.own, bf16[64,896]{1,0:T(8,128)(2,1)S(1)} %collective-permute-done.3.side, bf16[64,896]{1,0:T(8,128)(2,1)S(1)} %collective-permute-done.2.near, ...), custom_call_target="tpu_custom_call" | custom-call | flops 176160768 | bytes 1376256 | tf_op jit(solution)/shard_map/correlate/pallas_call | solution.py:293
  (2 shorter events, 0.0 us)
Async XLA Ops:
  4.3 7.8 %collective-permute-start = (bf16[32,896]{1,0:T(8,128)(2,1)S(1)}, bf16[32,896]{1,0:T(8,128)(2,1)S(1)}, u32[]{:S(2)}, u32[]{:S(2)}) collective-permute-start(bf16[32,896]{1,0:T(8,128)(2,1)S(1)} %get-tuple-element.16), channel_id=1, source_target_pairs={{1,13},{3,15},{5,9},{7,11},{9,5},{11,7},{13,1},{15,3},{0,8},{2,10}... | collective-permute-start | bytes 172040 | tf_op jit(solution)/shard_map/ppermute | solution.py:270
  8.4 6.4 %collective-permute-start.4 = (bf16[32,896]{1,0:T(8,128)(2,1)S(1)}, bf16[32,896]{1,0:T(8,128)(2,1)S(1)}, u32[]{:S(2)}, u32[]{:S(2)}) collective-permute-start(bf16[32,896]{1,0:T(8,128)(2,1)S(1)} %get-tuple-element.19), channel_id=1, source_target_pairs={{1,13},{3,15},{5,9},{7,11},{9,5},{11,7},{13,1},{15,3},{0,8},{2,10}... | collective-permute-start | bytes 172040 | tf_op jit(solution)/shard_map/ppermute | solution.py:270
  8.5 8.5 %collective-permute-start.3 = (bf16[64,896]{1,0:T(8,128)(2,1)S(1)}, bf16[64,896]{1,0:T(8,128)(2,1)S(1)}, u32[]{:S(2)}, u32[]{:S(2)}) collective-permute-start(bf16[64,896]{1,0:T(8,128)(2,1)S(1)} %get-tuple-element.15.own), channel_id=1, source_target_pairs={{1,3},{3,1},{5,7},{7,5},{9,11},{11,9},{13,15},{15,13},{0,2},{2,0},... | collective-permute-start | bytes 344072 | tf_op jit(solution)/shard_map/ppermute | solution.py:270
  10.2 6.8 %collective-permute-start.2 = (bf16[64,896]{1,0:T(8,128)(2,1)S(1)}, bf16[64,896]{1,0:T(8,128)(2,1)S(1)}, u32[]{:S(2)}, u32[]{:S(2)}) collective-permute-start(bf16[64,896]{1,0:T(8,128)(2,1)S(1)} %get-tuple-element.15.own), channel_id=1, source_target_pairs={{1,7},{3,5},{5,3},{7,1},{9,15},{11,13},{13,11},{15,9},{0,4},{2,6},... | collective-permute-start | bytes 344072 | tf_op jit(solution)/shard_map/ppermute | solution.py:270
  12.1 4.9 %collective-permute-start.1 = (bf16[32,896]{1,0:T(8,128)(2,1)S(1)}, bf16[32,896]{1,0:T(8,128)(2,1)S(1)}, u32[]{:S(2)}, u32[]{:S(2)}) collective-permute-start(bf16[32,896]{1,0:T(8,128)(2,1)S(1)} %collective-permute-done), channel_id=1, source_target_pairs={{0,3},{1,2},{2,1},{3,0},{4,7},{5,6},{6,5},{7,4},{8,11},{9,10},{10,... | collective-permute-start | bytes 172040 | tf_op jit(solution)/shard_map/ppermute | solution.py:274
  14.7 4.0 %collective-permute-start.7 = (bf16[32,896]{1,0:T(8,128)(2,1)S(1)}, bf16[32,896]{1,0:T(8,128)(2,1)S(1)}, u32[]{:S(2)}, u32[]{:S(2)}) collective-permute-start(bf16[32,896]{1,0:T(8,128)(2,1)S(1)} %collective-permute-done.4), channel_id=1, source_target_pairs={{0,3},{1,2},{2,1},{3,0},{4,7},{5,6},{6,5},{7,4},{8,11},{9,10},{10,... | collective-permute-start | bytes 172040 | tf_op jit(solution)/shard_map/ppermute | solution.py:274
  17.0 1.7 %collective-permute-start.8 = (bf16[32,896]{1,0:T(8,128)(2,1)S(1)}, bf16[32,896]{1,0:T(8,128)(2,1)S(1)}, u32[]{:S(2)}, u32[]{:S(2)}) collective-permute-start(bf16[32,896]{1,0:T(8,128)(2,1)S(1)} %collective-permute-done.1.cross_a), channel_id=1, source_target_pairs={{0,1},{1,0},{2,3},{3,2},{4,5},{5,4},{6,7},{7,6},{8,9},{9,8},{10,11... | collective-permute-start | bytes 172040 | tf_op jit(solution)/shard_map/ppermute | solution.py:277
  17.3 1.4 %collective-permute-start.5 = (bf16[64,896]{1,0:T(8,128)(2,1)S(1)}, bf16[64,896]{1,0:T(8,128)(2,1)S(1)}, u32[]{:S(2)}, u32[]{:S(2)}) collective-permute-start(bf16[64,896]{1,0:T(8,128)(2,1)S(1)} %constant_dynamic-update-slice_fusion.far), channel_id=1, source_target_pairs={{0,1},{1,0},{2,3},{3,2},{4,5},{5,4},{6,7},{7,6},{8,9},{9,8},{10,11... | collective-permute-start | bytes 344072 | tf_op jit(solution)/shard_map/ppermute | solution.py:277
  17.6 2.4 %collective-permute-start.6 = (bf16[64,896]{1,0:T(8,128)(2,1)S(1)}, bf16[64,896]{1,0:T(8,128)(2,1)S(1)}, u32[]{:S(2)}, u32[]{:S(2)}) collective-permute-start(bf16[64,896]{1,0:T(8,128)(2,1)S(1)} %collective-permute-done.2.near), channel_id=1, source_target_pairs={{0,1},{1,0},{2,3},{3,2},{4,5},{5,4},{6,7},{7,6},{8,9},{9,8},{10,11... | collective-permute-start | bytes 344072 | tf_op jit(solution)/shard_map/ppermute | solution.py:277
  18.7 1.2 %collective-permute-start.9 = (bf16[32,896]{1,0:T(8,128)(2,1)S(1)}, bf16[32,896]{1,0:T(8,128)(2,1)S(1)}, u32[]{:S(2)}, u32[]{:S(2)}) collective-permute-start(bf16[32,896]{1,0:T(8,128)(2,1)S(1)} %collective-permute-done.7.cross_b), channel_id=1, source_target_pairs={{0,1},{1,0},{2,3},{3,2},{4,5},{5,4},{6,7},{7,6},{8,9},{9,8},{10,11... | collective-permute-start | bytes 172040 | tf_op jit(solution)/shard_map/ppermute | solution.py:277

commit v5 on v4

--- a/solution.py
+++ b/solution.py
@@ -168,8 +168,8 @@
     band_power = jnp.sum(power[0] + power[1] + power[2] + power[3], axis=1, keepdims=True) / NB
     pieces = []
     for (re, im), own in zip(pairs, power):
-        denom = jnp.sqrt(own + water_level * band_power + 1e-06)
-        pieces += [re / denom, im / denom]
+        scale = 1.0 / jnp.sqrt(own + water_level * band_power + 1e-06)
+        pieces += [re * scale, im * scale]
     lanes = lax.broadcasted_iota(jnp.int32, (rows, LANES), 1)
     packed = []
     for p in range(7):
@@ -234,34 +234,45 @@
     return product.astype(jnp.bfloat16)
 
 
-def eight_kernel(lags, own, side, near, far, far_swap, near_swap, cross_a, cross_b, cross_swap_a, cross_swap_b, out):
+def put(out, product, plane, rows):
+    at = pl.multiple_of(plane * 2 * rows, 2 * rows)
+    for lag in range(out.shape[0]):
+        out[lag, :, pl.ds(at, 2 * rows)] = product[lag * rows : (lag + 1) * rows]
+
+
+def plane_products(lag_rows, tiles, x, rows):
+    columns = jnp.concatenate([block for blocks in tiles for block in blocks], axis=0)
+    both = lax.dot_general(lag_rows, columns, (((1,), (1,)), ((), ())), preferred_element_type=jnp.float32)
+    products = [both[:, place * 2 * rows : (place + 1) * 2 * rows] for place in range(len(tiles))]
+    return [jnp.where(x == 0, p, pltpu.roll(p, rows, axis=1)).astype(jnp.bfloat16) for p in products]
+
+
+def early_kernel(lags, own, side, near, near_swap, out):
+    x = lax.axis_index("chan") % 2
+    upper = lax.axis_index("pair") == 1
+    nearest = (
+        jnp.where(upper, near_swap[...], near[...]),
+        jnp.where(upper, near[...], near_swap[...]),
+    )
+    tiles = ((own[...], side[...]), nearest)
+    for place, product in enumerate(plane_products(lags[...], tiles, x, own.shape[0])):
+        out[place] = product
+
+
+def late_kernel(lags, early, far, far_swap, cross_a, cross_b, cross_swap_a, cross_swap_b, out):
     me = lax.axis_index("chan")
     core = lax.axis_index("pair")
     x, z = me % 2, me // 2
-    rows = own.shape[0]
-    upper = core == 1
-    lag_rows = lags[...]
+    rows = far.shape[0]
     tiles = (
-        ((own[...], side[...]), z),
-        (
-            (
-                jnp.where(upper, near_swap[...], near[...]),
-                jnp.where(upper, near[...], near_swap[...]),
-            ),
-            z ^ 1,
-        ),
-        ((far[...], cross_swap_a[...], cross_swap_b[...]), z ^ (2 + core)),
-        ((far_swap[...], cross_a[...], cross_b[...]), z ^ (3 - core)),
-    )
-    for blocks, plane in tiles:
-        columns = jnp.concatenate(blocks, axis=0)
-        product = lax.dot_general(
-            lag_rows, columns, (((1,), (1,)), ((), ())), preferred_element_type=jnp.float32
-        )
-        product = jnp.where(x == 0, product, pltpu.roll(product, rows, axis=1)).astype(jnp.bfloat16)
-        at = pl.multiple_of(plane * 2 * rows, 2 * rows)
-        for lag in range(out.shape[0]):
-            out[lag, :, pl.ds(at, 2 * rows)] = product[lag * rows : (lag + 1) * rows]
+        (far[...], cross_swap_a[...], cross_swap_b[...]),
+        (far_swap[...], cross_a[...], cross_b[...]),
+    )
+    put(out, early[0], z, rows)
+    put(out, early[1], z ^ 1, rows)
+    first, second = plane_products(lags[...], tiles, x, rows)
+    put(out, first, z ^ (2 + core), rows)
+    put(out, second, z ^ (3 - core), rows)
 
 
 def exchange_eight(own, first, second, lags):
@@ -290,17 +301,28 @@
     near_swap = swap(near)
     cross_swap_b = swap(cross_b)
     lag_share, rows = lags.shape[0] // own.shape[0], own.shape[0]
-    return pl.pallas_call(
-        eight_kernel,
-        out_shape=jax.ShapeDtypeStruct((lag_share, rows, 8 * rows), jnp.bfloat16),
-        in_specs=[pl.BlockSpec(memory_space=pltpu.VMEM)] * 11,
+    early = pl.pallas_call(
+        early_kernel,
+        out_shape=pltpu.VMEM((2, lag_share * rows, 2 * rows), jnp.bfloat16),
+        in_specs=[pl.BlockSpec(memory_space=pltpu.VMEM)] * 5,
         out_specs=pl.BlockSpec(memory_space=pltpu.VMEM),
         compiler_params=pltpu.CompilerParams(vmem_limit_bytes=CORR_KIB * 1024),
         cost_estimate=pl.CostEstimate(
-            flops=2 * lag_share * rows * 8 * rows * WIDTH, bytes_accessed=12 * rows * WIDTH * 2, transcendentals=0
+            flops=2 * lag_share * rows * 4 * rows * WIDTH, bytes_accessed=8 * rows * WIDTH * 2, transcendentals=0
         ),
-        name="correlate",
-    )(lags, own, side, near, far, far_swap, near_swap, cross_a, cross_b, cross_swap_a, cross_swap_b)
+        name="correlate_early",
+    )(lags, own, side, near, near_swap)
+    return pl.pallas_call(
+        late_kernel,
+        out_shape=jax.ShapeDtypeStruct((lag_share, rows, 8 * rows), jnp.bfloat16),
+        in_specs=[pl.BlockSpec(memory_space=pltpu.VMEM)] * 8,
+        out_specs=pl.BlockSpec(memory_space=pltpu.VMEM),
+        compiler_params=pltpu.CompilerParams(vmem_limit_bytes=CORR_KIB * 1024),
+        cost_estimate=pl.CostEstimate(
+            flops=2 * lag_share * rows * 4 * rows * WIDTH, bytes_accessed=8 * rows * WIDTH * 2, transcendentals=0
+        ),
+        name="correlate_late",
+    )(lags, early, far, far_swap, cross_a, cross_b, cross_swap_a, cross_swap_b)
 
 
 def shards(table, weights, raw, live_index, live_count):

time: 21.4 us -> 21.1 us (0.986)
  waiting for transfers between devices: 6.8 us -> 6.11 us
    ppermute x4, waiting for transfers between devices: 1.24 us -> 0.73 us  [swap(): return lax.ppermute(a, 'pair', [(0, 1), (1, 0)])]
    ppermute x2, starting transfers between devices: 0.46 us -> 0.74 us  [forward(): return lax.ppermute(a, ('chan', 'pair'), pairs)]
    pallas_call x1 -> x2, Pallas kernels: 1.29 us -> 1.47 us  [the longest x1 1.08 us: exchange_eight(): pl.pallas_call(late_kernel, out_shape=jax.ShapeDtypeStruct((lag_share, ro...]
  transfers between devices with their start and end apart: 10 -> 10, of which waited for: 5 -> 6; matrix products, arithmetic and copies ran while one was open for 0% -> 0% of each run, Pallas kernels for 0% -> 2%
where the time goes in v5:
time: 21.1 us; the launch traced here: 21 us
  starting transfers between devices  9.05 us (43%)
  waiting for transfers between devices  6.11 us (29%)
  Pallas kernels  5.74 us (27%)
    ppermute x4, starting transfers between devices, split_move(): return lambda a: lax.ppermute(a, ('chan', 'pair'), pairs)  7.5 us
    pallas_call x1, Pallas kernels, spectra(): pl.pallas_call(functools.partial(spectra_kernel, lag_share), out_shape=[p...  4.28 us
    ppermute x4, waiting for transfers between devices, split_move(): return lambda a: lax.ppermute(a, ('chan', 'pair'), pairs)  2.81 us
    ppermute x2, waiting for transfers between devices, forward(): return lax.ppermute(a, ('chan', 'pair'), pairs)  2.57 us
    pallas_call x1, Pallas kernels, exchange_eight(): pl.pallas_call(late_kernel, out_shape=jax.ShapeDtypeStruct((lag_share, ro...  1.08 us
    ppermute x4, starting transfers between devices, swap(): return lax.ppermute(a, 'pair', [(0, 1), (1, 0)])  0.8 us
    ppermute x2, starting transfers between devices, forward(): return lax.ppermute(a, ('chan', 'pair'), pairs)  0.74 us
    ppermute x4, waiting for transfers between devices, swap(): return lax.ppermute(a, 'pair', [(0, 1), (1, 0)])  0.73 us
  transfers between devices with their start and end apart: 10, of which 6 were waited for; matrix products, arithmetic and copies ran while one was open for 0% of the time, Pallas kernels for 2%

profile of v5, /device:TPU:0, one launch (start us, length us, event | category | flops | bytes accessed | tf_op | source)
XLA Modules:
  0.0 21.0 jit_solution(14484649286577243523)
XLA Ops:
  0.0 4.3 %spectra.1 = (bf16[64,896]{1,0:T(8,128)(2,1)S(1)}, bf16[32,896]{1,0:T(8,128)(2,1)S(1)}, bf16[32,896]{1,0:T(8,128)(2,1)S(1)}, bf16[192,896]{1,0:T(8,128)(2,1)S(1)}) custom-call(s32[8]{0:T(128)} %count_ref.1, s32[1,64]{1,0:T(1,128)} %index_ref.1, bf16[64,12000]{1,0:T(8,128)(2,1)} %bitcast.1, bf16[3072,1024]{1,0:T(8,128)(2,1)} %constant.5.clone.table_ref, ...), custom_call_target="tpu_custom_call" | custom-call | flops 1207959552 | bytes 7827456 | tf_op jit(solution)/shard_map/spectra/pallas_call | solution.py:199
  4.3 4.1 %collective-permute-start = (bf16[32,896]{1,0:T(8,128)(2,1)S(1)}, bf16[32,896]{1,0:T(8,128)(2,1)S(1)}, u32[]{:S(2)}, u32[]{:S(2)}) collective-permute-start(bf16[32,896]{1,0:T(8,128)(2,1)S(1)} %get-tuple-element.16), channel_id=1, source_target_pairs={{1,13},{3,15},{5,9},{7,11},{9,5},{11,7},{13,1},{15,3},{0,8},{2,10}... | collective-permute-start | bytes 172040 | tf_op jit(solution)/shard_map/ppermute | solution.py:281
  8.4 0.1 collective-permute-start.5
  8.5 1.8 %collective-permute-start.2 = (bf16[64,896]{1,0:T(8,128)(2,1)S(1)}, bf16[64,896]{1,0:T(8,128)(2,1)S(1)}, u32[]{:S(2)}, u32[]{:S(2)}) collective-permute-start(bf16[64,896]{1,0:T(8,128)(2,1)S(1)} %get-tuple-element.15.own), channel_id=1, source_target_pairs={{1,7},{3,5},{5,3},{7,1},{9,15},{11,13},{13,11},{15,9},{0,4},{2,6},... | collective-permute-start | bytes 344072 | tf_op jit(solution)/shard_map/ppermute | solution.py:281
  10.3 1.5 %collective-permute-start.3 = (bf16[64,896]{1,0:T(8,128)(2,1)S(1)}, bf16[64,896]{1,0:T(8,128)(2,1)S(1)}, u32[]{:S(2)}, u32[]{:S(2)}) collective-permute-start(bf16[64,896]{1,0:T(8,128)(2,1)S(1)} %get-tuple-element.15.own), channel_id=1, source_target_pairs={{1,3},{3,1},{5,7},{7,5},{9,11},{11,9},{13,15},{15,13},{0,2},{2,0},... | collective-permute-start | bytes 344072 | tf_op jit(solution)/shard_map/ppermute | solution.py:281
  11.8 0.3 %collective-permute-done = bf16[32,896]{1,0:T(8,128)(2,1)S(1)} collective-permute-done((bf16[32,896]{1,0:T(8,128)(2,1)S(1)}, bf16[32,896]{1,0:T(8,128)(2,1)S(1)}, u32[]{:S(2)}, u32[]{:S(2)}) %collective-permute-start) | collective-permute-done | bytes 57376 | tf_op jit(solution)/shard_map/ppermute | solution.py:281
  12.1 0.0 collective-permute-start.1
  12.1 2.3 %collective-permute-done.5 = bf16[32,896]{1,0:T(8,128)(2,1)S(1)} collective-permute-done((bf16[32,896]{1,0:T(8,128)(2,1)S(1)}, bf16[32,896]{1,0:T(8,128)(2,1)S(1)}, u32[]{:S(2)}, u32[]{:S(2)}) %collective-permute-start.5) | collective-permute-done | bytes 57376 | tf_op jit(solution)/shard_map/ppermute | solution.py:281
  14.4 0.7 %collective-permute-start.7 = (bf16[32,896]{1,0:T(8,128)(2,1)S(1)}, bf16[32,896]{1,0:T(8,128)(2,1)S(1)}, u32[]{:S(2)}, u32[]{:S(2)}) collective-permute-start(bf16[32,896]{1,0:T(8,128)(2,1)S(1)} %collective-permute-done.5), channel_id=1, source_target_pairs={{0,3},{1,2},{2,1},{3,0},{4,7},{5,6},{6,5},{7,4},{8,11},{9,10},{10,... | collective-permute-start | bytes 172040 | tf_op jit(solution)/shard_map/ppermute | solution.py:285
  15.2 0.2 collective-permute-done.2.near
  15.4 0.0 collective-permute-done.3.side
  15.4 1.3 %collective-permute-done.1.cross_a = bf16[32,896]{1,0:T(8,128)(2,1)S(1)} collective-permute-done((bf16[32,896]{1,0:T(8,128)(2,1)S(1)}, bf16[32,896]{1,0:T(8,128)(2,1)S(1)}, u32[]{:S(2)}, u32[]{:S(2)}) %collective-permute-start.1) | collective-permute-done | bytes 57376 | tf_op jit(solution)/shard_map/ppermute | solution.py:285
  16.6 0.1 collective-permute-start.4
  16.8 0.4 %collective-permute-start.8 = (bf16[32,896]{1,0:T(8,128)(2,1)S(1)}, bf16[32,896]{1,0:T(8,128)(2,1)S(1)}, u32[]{:S(2)}, u32[]{:S(2)}) collective-permute-start(bf16[32,896]{1,0:T(8,128)(2,1)S(1)} %collective-permute-done.1.cross_a), channel_id=1, source_target_pairs={{0,1},{1,0},{2,3},{3,2},{4,5},{5,4},{6,7},{7,6},{8,9},{9,8},{10,11... | collective-permute-start | bytes 172040 | tf_op jit(solution)/shard_map/ppermute | solution.py:288
  17.2 0.2 collective-permute-start.6
  17.3 1.3 %collective-permute-done.7.cross_b = bf16[32,896]{1,0:T(8,128)(2,1)S(1)} collective-permute-done((bf16[32,896]{1,0:T(8,128)(2,1)S(1)}, bf16[32,896]{1,0:T(8,128)(2,1)S(1)}, u32[]{:S(2)}, u32[]{:S(2)}) %collective-permute-start.7) | collective-permute-done | bytes 57376 | tf_op jit(solution)/shard_map/ppermute | solution.py:285
  18.6 0.0 collective-permute-done.8.cross_swap_a
  18.6 0.1 collective-permute-start.9
  18.7 0.0 collective-permute-done.4.near_swap
  18.7 0.4 %correlate_early.1.early = bf16[2,192,128]{2,1,0:T(8,128)(2,1)S(1)} custom-call(bf16[192,896]{1,0:T(8,128)(2,1)S(1)} %get-tuple-element.14.lags, bf16[64,896]{1,0:T(8,128)(2,1)S(1)} %get-tuple-element.15.own, bf16[64,896]{1,0:T(8,128)(2,1)S(1)} %collective-permute-done.3.side, bf16[64,896]{1,0:T(8,128)(2,1)S(1)} %collective-permute-done.2.near, ...), custom_call_target="tpu_custom_call" | custom-call | flops 88080384 | bytes 917504 | tf_op jit(solution)/shard_map/correlate_early/pallas_call | solution.py:304
  19.1 0.0 collective-permute-done.6.far_swap
  19.2 0.7 %collective-permute-done.9.cross_swap_b = bf16[32,896]{1,0:T(8,128)(2,1)S(1)} collective-permute-done((bf16[32,896]{1,0:T(8,128)(2,1)S(1)}, bf16[32,896]{1,0:T(8,128)(2,1)S(1)}, u32[]{:S(2)}, u32[]{:S(2)}) %collective-permute-start.9) | collective-permute-done | bytes 57376 | tf_op jit(solution)/shard_map/ppermute | solution.py:288
  19.9 1.1 %correlate_late.1 = bf16[3,64,512]{2,1,0:T(8,128)(2,1)} custom-call(bf16[192,896]{1,0:T(8,128)(2,1)S(1)} %get-tuple-element.14.lags, bf16[2,192,128]{2,1,0:T(8,128)(2,1)S(1)} %correlate_early.1.early, bf16[64,896]{1,0:T(8,128)(2,1)S(1)} %constant_dynamic-update-slice_fusion.far, bf16[64,896]{1,0:T(8,128)(2,1)S(1)} %collective-permute-done.6.far_swap, ...), custom_call_target="tpu_custom_call" | custom-call | flops 88080384 | bytes 917504 | tf_op jit(solution)/shard_map/correlate_late/pallas_call | solution.py:315
  (2 shorter events, 0.0 us)
Async XLA Ops:
  4.3 7.8 %collective-permute-start = (bf16[32,896]{1,0:T(8,128)(2,1)S(1)}, bf16[32,896]{1,0:T(8,128)(2,1)S(1)}, u32[]{:S(2)}, u32[]{:S(2)}) collective-permute-start(bf16[32,896]{1,0:T(8,128)(2,1)S(1)} %get-tuple-element.16), channel_id=1, source_target_pairs={{1,13},{3,15},{5,9},{7,11},{9,5},{11,7},{13,1},{15,3},{0,8},{2,10}... | collective-permute-start | bytes 172040 | tf_op jit(solution)/shard_map/ppermute | solution.py:281
  8.4 6.1 %collective-permute-start.5 = (bf16[32,896]{1,0:T(8,128)(2,1)S(1)}, bf16[32,896]{1,0:T(8,128)(2,1)S(1)}, u32[]{:S(2)}, u32[]{:S(2)}) collective-permute-start(bf16[32,896]{1,0:T(8,128)(2,1)S(1)} %get-tuple-element.19), channel_id=1, source_target_pairs={{1,13},{3,15},{5,9},{7,11},{9,5},{11,7},{13,1},{15,3},{0,8},{2,10}... | collective-permute-start | bytes 172040 | tf_op jit(solution)/shard_map/ppermute | solution.py:281
  8.5 6.9 %collective-permute-start.2 = (bf16[64,896]{1,0:T(8,128)(2,1)S(1)}, bf16[64,896]{1,0:T(8,128)(2,1)S(1)}, u32[]{:S(2)}, u32[]{:S(2)}) collective-permute-start(bf16[64,896]{1,0:T(8,128)(2,1)S(1)} %get-tuple-element.15.own), channel_id=1, source_target_pairs={{1,7},{3,5},{5,3},{7,1},{9,15},{11,13},{13,11},{15,9},{0,4},{2,6},... | collective-permute-start | bytes 344072 | tf_op jit(solution)/shard_map/ppermute | solution.py:281
  10.3 5.1 %collective-permute-start.3 = (bf16[64,896]{1,0:T(8,128)(2,1)S(1)}, bf16[64,896]{1,0:T(8,128)(2,1)S(1)}, u32[]{:S(2)}, u32[]{:S(2)}) collective-permute-start(bf16[64,896]{1,0:T(8,128)(2,1)S(1)} %get-tuple-element.15.own), channel_id=1, source_target_pairs={{1,3},{3,1},{5,7},{7,5},{9,11},{11,9},{13,15},{15,13},{0,2},{2,0},... | collective-permute-start | bytes 344072 | tf_op jit(solution)/shard_map/ppermute | solution.py:281
  12.1 4.5 %collective-permute-start.1 = (bf16[32,896]{1,0:T(8,128)(2,1)S(1)}, bf16[32,896]{1,0:T(8,128)(2,1)S(1)}, u32[]{:S(2)}, u32[]{:S(2)}) collective-permute-start(bf16[32,896]{1,0:T(8,128)(2,1)S(1)} %collective-permute-done), channel_id=1, source_target_pairs={{0,3},{1,2},{2,1},{3,0},{4,7},{5,6},{6,5},{7,4},{8,11},{9,10},{10,... | collective-permute-start | bytes 172040 | tf_op jit(solution)/shard_map/ppermute | solution.py:285
  14.4 4.2 %collective-permute-start.7 = (bf16[32,896]{1,0:T(8,128)(2,1)S(1)}, bf16[32,896]{1,0:T(8,128)(2,1)S(1)}, u32[]{:S(2)}, u32[]{:S(2)}) collective-permute-start(bf16[32,896]{1,0:T(8,128)(2,1)S(1)} %collective-permute-done.5), channel_id=1, source_target_pairs={{0,3},{1,2},{2,1},{3,0},{4,7},{5,6},{6,5},{7,4},{8,11},{9,10},{10,... | collective-permute-start | bytes 172040 | tf_op jit(solution)/shard_map/ppermute | solution.py:285
  16.6 2.1 %collective-permute-start.4 = (bf16[64,896]{1,0:T(8,128)(2,1)S(1)}, bf16[64,896]{1,0:T(8,128)(2,1)S(1)}, u32[]{:S(2)}, u32[]{:S(2)}) collective-permute-start(bf16[64,896]{1,0:T(8,128)(2,1)S(1)} %collective-permute-done.2.near), channel_id=1, source_target_pairs={{0,1},{1,0},{2,3},{3,2},{4,5},{5,4},{6,7},{7,6},{8,9},{9,8},{10,11... | collective-permute-start | bytes 344072 | tf_op jit(solution)/shard_map/ppermute | solution.py:288
  16.8 1.9 %collective-permute-start.8 = (bf16[32,896]{1,0:T(8,128)(2,1)S(1)}, bf16[32,896]{1,0:T(8,128)(2,1)S(1)}, u32[]{:S(2)}, u32[]{:S(2)}) collective-permute-start(bf16[32,896]{1,0:T(8,128)(2,1)S(1)} %collective-permute-done.1.cross_a), channel_id=1, source_target_pairs={{0,1},{1,0},{2,3},{3,2},{4,5},{5,4},{6,7},{7,6},{8,9},{9,8},{10,11... | collective-permute-start | bytes 172040 | tf_op jit(solution)/shard_map/ppermute | solution.py:288
  17.2 2.0 %collective-permute-start.6 = (bf16[64,896]{1,0:T(8,128)(2,1)S(1)}, bf16[64,896]{1,0:T(8,128)(2,1)S(1)}, u32[]{:S(2)}, u32[]{:S(2)}) collective-permute-start(bf16[64,896]{1,0:T(8,128)(2,1)S(1)} %constant_dynamic-update-slice_fusion.far), channel_id=1, source_target_pairs={{0,1},{1,0},{2,3},{3,2},{4,5},{5,4},{6,7},{7,6},{8,9},{9,8},{10,11... | collective-permute-start | bytes 344072 | tf_op jit(solution)/shard_map/ppermute | solution.py:288
  18.6 1.2 %collective-permute-start.9 = (bf16[32,896]{1,0:T(8,128)(2,1)S(1)}, bf16[32,896]{1,0:T(8,128)(2,1)S(1)}, u32[]{:S(2)}, u32[]{:S(2)}) collective-permute-start(bf16[32,896]{1,0:T(8,128)(2,1)S(1)} %collective-permute-done.7.cross_b), channel_id=1, source_target_pairs={{0,1},{1,0},{2,3},{3,2},{4,5},{5,4},{6,7},{7,6},{8,9},{9,8},{10,11... | collective-permute-start | bytes 172040 | tf_op jit(solution)/shard_map/ppermute | solution.py:288

commit v6 on v5

--- a/solution.py
+++ b/solution.py
@@ -293,7 +293,6 @@
     near = split_move(3, 2)(own)
     cross_a = forward(far_a)
     cross_b = forward(far_b)
-    cross_a, near, side = lax.optimization_barrier((cross_a, near, side))
     cross_swap_a = swap(cross_a)
     cross_b, cross_swap_a = lax.optimization_barrier((cross_b, cross_swap_a))
     far = jnp.concatenate([far_a, far_b], axis=0)

time: 21.1 us -> 21.1 us (level)
  starting transfers between devices: 9.05 us -> 9.71 us
  waiting for transfers between devices: 6.11 us -> 5.45 us
    ppermute x4, starting transfers between devices: 0.8 us -> 1.46 us  [swap(): return lax.ppermute(a, 'pair', [(0, 1), (1, 0)])]
    ppermute x2, waiting for transfers between devices: 2.57 us -> 1.91 us  [forward(): return lax.ppermute(a, ('chan', 'pair'), pairs)]
where the time goes in v6:
time: 21.1 us; the launch traced here: 21 us
  starting transfers between devices  9.71 us (46%)
  Pallas kernels  5.74 us (27%)
  waiting for transfers between devices  5.45 us (26%)
    ppermute x4, starting transfers between devices, split_move(): return lambda a: lax.ppermute(a, ('chan', 'pair'), pairs)  7.5 us
    pallas_call x1, Pallas kernels, spectra(): pl.pallas_call(functools.partial(spectra_kernel, lag_share), out_shape=[p...  4.28 us
    ppermute x4, waiting for transfers between devices, split_move(): return lambda a: lax.ppermute(a, ('chan', 'pair'), pairs)  2.81 us
    ppermute x2, waiting for transfers between devices, forward(): return lax.ppermute(a, ('chan', 'pair'), pairs)  1.91 us
    ppermute x4, starting transfers between devices, swap(): return lax.ppermute(a, 'pair', [(0, 1), (1, 0)])  1.46 us
    pallas_call x1, Pallas kernels, exchange_eight(): pl.pallas_call(late_kernel, out_shape=jax.ShapeDtypeStruct((lag_share, ro...  1.08 us
    ppermute x2, starting transfers between devices, forward(): return lax.ppermute(a, ('chan', 'pair'), pairs)  0.74 us
    ppermute x4, waiting for transfers between devices, swap(): return lax.ppermute(a, 'pair', [(0, 1), (1, 0)])  0.72 us
  transfers between devices with their start and end apart: 10, of which 6 were waited for; matrix products, arithmetic and copies ran while one was open for 0% of the time, Pallas kernels for 2%

profile of v6, /device:TPU:0, one launch (start us, length us, event | category | flops | bytes accessed | tf_op | source)
XLA Modules:
  0.0 21.0 jit_solution(3067084021492594476)
XLA Ops:
  0.0 4.3 %spectra.1 = (bf16[64,896]{1,0:T(8,128)(2,1)S(1)}, bf16[32,896]{1,0:T(8,128)(2,1)S(1)}, bf16[32,896]{1,0:T(8,128)(2,1)S(1)}, bf16[192,896]{1,0:T(8,128)(2,1)S(1)}) custom-call(s32[8]{0:T(128)} %count_ref.1, s32[1,64]{1,0:T(1,128)} %index_ref.1, bf16[64,12000]{1,0:T(8,128)(2,1)} %bitcast.1, bf16[3072,1024]{1,0:T(8,128)(2,1)} %constant.5.clone.table_ref, ...), custom_call_target="tpu_custom_call" | custom-call | flops 1207959552 | bytes 7827456 | tf_op jit(solution)/shard_map/spectra/pallas_call | solution.py:199
  4.3 4.1 %collective-permute-start.3 = (bf16[32,896]{1,0:T(8,128)(2,1)S(1)}, bf16[32,896]{1,0:T(8,128)(2,1)S(1)}, u32[]{:S(2)}, u32[]{:S(2)}) collective-permute-start(bf16[32,896]{1,0:T(8,128)(2,1)S(1)} %get-tuple-element.13), channel_id=1, source_target_pairs={{1,13},{3,15},{5,9},{7,11},{9,5},{11,7},{13,1},{15,3},{0,8},{2,10}... | collective-permute-start | bytes 172040 | tf_op jit(solution)/shard_map/ppermute | solution.py:281
  8.4 0.1 collective-permute-start.4
  8.5 1.8 %collective-permute-start.1 = (bf16[64,896]{1,0:T(8,128)(2,1)S(1)}, bf16[64,896]{1,0:T(8,128)(2,1)S(1)}, u32[]{:S(2)}, u32[]{:S(2)}) collective-permute-start(bf16[64,896]{1,0:T(8,128)(2,1)S(1)} %get-tuple-element.12.own), channel_id=1, source_target_pairs={{1,7},{3,5},{5,3},{7,1},{9,15},{11,13},{13,11},{15,9},{0,4},{2,6},... | collective-permute-start | bytes 344072 | tf_op jit(solution)/shard_map/ppermute | solution.py:281
  10.3 1.5 %collective-permute-start = (bf16[64,896]{1,0:T(8,128)(2,1)S(1)}, bf16[64,896]{1,0:T(8,128)(2,1)S(1)}, u32[]{:S(2)}, u32[]{:S(2)}) collective-permute-start(bf16[64,896]{1,0:T(8,128)(2,1)S(1)} %get-tuple-element.12.own), channel_id=1, source_target_pairs={{1,3},{3,1},{5,7},{7,5},{9,11},{11,9},{13,15},{15,13},{0,2},{2,0},... | collective-permute-start | bytes 344072 | tf_op jit(solution)/shard_map/ppermute | solution.py:281
  11.8 0.3 %collective-permute-done.3 = bf16[32,896]{1,0:T(8,128)(2,1)S(1)} collective-permute-done((bf16[32,896]{1,0:T(8,128)(2,1)S(1)}, bf16[32,896]{1,0:T(8,128)(2,1)S(1)}, u32[]{:S(2)}, u32[]{:S(2)}) %collective-permute-start.3) | collective-permute-done | bytes 57376 | tf_op jit(solution)/shard_map/ppermute | solution.py:281
  12.1 0.0 collective-permute-start.6
  12.1 2.3 %collective-permute-done.4 = bf16[32,896]{1,0:T(8,128)(2,1)S(1)} collective-permute-done((bf16[32,896]{1,0:T(8,128)(2,1)S(1)}, bf16[32,896]{1,0:T(8,128)(2,1)S(1)}, u32[]{:S(2)}, u32[]{:S(2)}) %collective-permute-start.4) | collective-permute-done | bytes 57376 | tf_op jit(solution)/shard_map/ppermute | solution.py:281
  14.4 0.7 %collective-permute-start.7 = (bf16[32,896]{1,0:T(8,128)(2,1)S(1)}, bf16[32,896]{1,0:T(8,128)(2,1)S(1)}, u32[]{:S(2)}, u32[]{:S(2)}) collective-permute-start(bf16[32,896]{1,0:T(8,128)(2,1)S(1)} %collective-permute-done.4), channel_id=1, source_target_pairs={{0,3},{1,2},{2,1},{3,0},{4,7},{5,6},{6,5},{7,4},{8,11},{9,10},{10,... | collective-permute-start | bytes 172040 | tf_op jit(solution)/shard_map/ppermute | solution.py:285
  15.2 0.2 collective-permute-done.1.near
  15.4 0.8 %collective-permute-start.2 = (bf16[64,896]{1,0:T(8,128)(2,1)S(1)}, bf16[64,896]{1,0:T(8,128)(2,1)S(1)}, u32[]{:S(2)}, u32[]{:S(2)}) collective-permute-start(bf16[64,896]{1,0:T(8,128)(2,1)S(1)} %collective-permute-done.1.near), channel_id=1, source_target_pairs={{0,1},{1,0},{2,3},{3,2},{4,5},{5,4},{6,7},{7,6},{8,9},{9,8},{10,11... | collective-permute-start | bytes 344072 | tf_op jit(solution)/shard_map/ppermute | solution.py:288
  16.1 0.5 %collective-permute-done.6.cross_a = bf16[32,896]{1,0:T(8,128)(2,1)S(1)} collective-permute-done((bf16[32,896]{1,0:T(8,128)(2,1)S(1)}, bf16[32,896]{1,0:T(8,128)(2,1)S(1)}, u32[]{:S(2)}, u32[]{:S(2)}) %collective-permute-start.6) | collective-permute-done | bytes 57376 | tf_op jit(solution)/shard_map/ppermute | solution.py:285
  16.6 0.1 collective-permute-start.8
  16.8 0.5 %collective-permute-start.5 = (bf16[64,896]{1,0:T(8,128)(2,1)S(1)}, bf16[64,896]{1,0:T(8,128)(2,1)S(1)}, u32[]{:S(2)}, u32[]{:S(2)}) collective-permute-start(bf16[64,896]{1,0:T(8,128)(2,1)S(1)} %constant_dynamic-update-slice_fusion.far), channel_id=1, source_target_pairs={{0,1},{1,0},{2,3},{3,2},{4,5},{5,4},{6,7},{7,6},{8,9},{9,8},{10,11... | collective-permute-start | bytes 344072 | tf_op jit(solution)/shard_map/ppermute | solution.py:288
  17.2 1.4 %collective-permute-done.7.cross_b = bf16[32,896]{1,0:T(8,128)(2,1)S(1)} collective-permute-done((bf16[32,896]{1,0:T(8,128)(2,1)S(1)}, bf16[32,896]{1,0:T(8,128)(2,1)S(1)}, u32[]{:S(2)}, u32[]{:S(2)}) %collective-permute-start.7) | collective-permute-done | bytes 57376 | tf_op jit(solution)/shard_map/ppermute | solution.py:285
  18.6 0.0 collective-permute-done.8.cross_swap_a
  18.6 0.1 collective-permute-start.9
  18.7 0.0 collective-permute-done.side
  18.7 0.0 collective-permute-done.2.near_swap
  18.8 0.4 %correlate_early.1.early = bf16[2,192,128]{2,1,0:T(8,128)(2,1)S(1)} custom-call(bf16[192,896]{1,0:T(8,128)(2,1)S(1)} %get-tuple-element.11.lags, bf16[64,896]{1,0:T(8,128)(2,1)S(1)} %get-tuple-element.12.own, bf16[64,896]{1,0:T(8,128)(2,1)S(1)} %collective-permute-done.side, bf16[64,896]{1,0:T(8,128)(2,1)S(1)} %collective-permute-done.1.near, ...), custom_call_target="tpu_custom_call" | custom-call | flops 88080384 | bytes 917504 | tf_op jit(solution)/shard_map/correlate_early/pallas_call | solution.py:303
  19.1 0.0 collective-permute-done.5.far_swap
  19.2 0.7 %collective-permute-done.9.cross_swap_b = bf16[32,896]{1,0:T(8,128)(2,1)S(1)} collective-permute-done((bf16[32,896]{1,0:T(8,128)(2,1)S(1)}, bf16[32,896]{1,0:T(8,128)(2,1)S(1)}, u32[]{:S(2)}, u32[]{:S(2)}) %collective-permute-start.9) | collective-permute-done | bytes 57376 | tf_op jit(solution)/shard_map/ppermute | solution.py:288
  19.9 1.1 %correlate_late.1 = bf16[3,64,512]{2,1,0:T(8,128)(2,1)} custom-call(bf16[192,896]{1,0:T(8,128)(2,1)S(1)} %get-tuple-element.11.lags, bf16[2,192,128]{2,1,0:T(8,128)(2,1)S(1)} %correlate_early.1.early, bf16[64,896]{1,0:T(8,128)(2,1)S(1)} %constant_dynamic-update-slice_fusion.far, bf16[64,896]{1,0:T(8,128)(2,1)S(1)} %collective-permute-done.5.far_swap, ...), custom_call_target="tpu_custom_call" | custom-call | flops 88080384 | bytes 917504 | tf_op jit(solution)/shard_map/correlate_late/pallas_call | solution.py:314
  (2 shorter events, 0.0 us)
Async XLA Ops:
  4.3 7.8 %collective-permute-start.3 = (bf16[32,896]{1,0:T(8,128)(2,1)S(1)}, bf16[32,896]{1,0:T(8,128)(2,1)S(1)}, u32[]{:S(2)}, u32[]{:S(2)}) collective-permute-start(bf16[32,896]{1,0:T(8,128)(2,1)S(1)} %get-tuple-element.13), channel_id=1, source_target_pairs={{1,13},{3,15},{5,9},{7,11},{9,5},{11,7},{13,1},{15,3},{0,8},{2,10}... | collective-permute-start | bytes 172040 | tf_op jit(solution)/shard_map/ppermute | solution.py:281
  8.4 6.1 %collective-permute-start.4 = (bf16[32,896]{1,0:T(8,128)(2,1)S(1)}, bf16[32,896]{1,0:T(8,128)(2,1)S(1)}, u32[]{:S(2)}, u32[]{:S(2)}) collective-permute-start(bf16[32,896]{1,0:T(8,128)(2,1)S(1)} %get-tuple-element.14), channel_id=1, source_target_pairs={{1,13},{3,15},{5,9},{7,11},{9,5},{11,7},{13,1},{15,3},{0,8},{2,10}... | collective-permute-start | bytes 172040 | tf_op jit(solution)/shard_map/ppermute | solution.py:281
  8.5 6.9 %collective-permute-start.1 = (bf16[64,896]{1,0:T(8,128)(2,1)S(1)}, bf16[64,896]{1,0:T(8,128)(2,1)S(1)}, u32[]{:S(2)}, u32[]{:S(2)}) collective-permute-start(bf16[64,896]{1,0:T(8,128)(2,1)S(1)} %get-tuple-element.12.own), channel_id=1, source_target_pairs={{1,7},{3,5},{5,3},{7,1},{9,15},{11,13},{13,11},{15,9},{0,4},{2,6},... | collective-permute-start | bytes 344072 | tf_op jit(solution)/shard_map/ppermute | solution.py:281
  10.3 8.5 %collective-permute-start = (bf16[64,896]{1,0:T(8,128)(2,1)S(1)}, bf16[64,896]{1,0:T(8,128)(2,1)S(1)}, u32[]{:S(2)}, u32[]{:S(2)}) collective-permute-start(bf16[64,896]{1,0:T(8,128)(2,1)S(1)} %get-tuple-element.12.own), channel_id=1, source_target_pairs={{1,3},{3,1},{5,7},{7,5},{9,11},{11,9},{13,15},{15,13},{0,2},{2,0},... | collective-permute-start | bytes 344072 | tf_op jit(solution)/shard_map/ppermute | solution.py:281
  12.1 4.5 %collective-permute-start.6 = (bf16[32,896]{1,0:T(8,128)(2,1)S(1)}, bf16[32,896]{1,0:T(8,128)(2,1)S(1)}, u32[]{:S(2)}, u32[]{:S(2)}) collective-permute-start(bf16[32,896]{1,0:T(8,128)(2,1)S(1)} %collective-permute-done.3), channel_id=1, source_target_pairs={{0,3},{1,2},{2,1},{3,0},{4,7},{5,6},{6,5},{7,4},{8,11},{9,10},{10,... | collective-permute-start | bytes 172040 | tf_op jit(solution)/shard_map/ppermute | solution.py:285
  14.4 4.2 %collective-permute-start.7 = (bf16[32,896]{1,0:T(8,128)(2,1)S(1)}, bf16[32,896]{1,0:T(8,128)(2,1)S(1)}, u32[]{:S(2)}, u32[]{:S(2)}) collective-permute-start(bf16[32,896]{1,0:T(8,128)(2,1)S(1)} %collective-permute-done.4), channel_id=1, source_target_pairs={{0,3},{1,2},{2,1},{3,0},{4,7},{5,6},{6,5},{7,4},{8,11},{9,10},{10,... | collective-permute-start | bytes 172040 | tf_op jit(solution)/shard_map/ppermute | solution.py:285
  15.4 3.4 %collective-permute-start.2 = (bf16[64,896]{1,0:T(8,128)(2,1)S(1)}, bf16[64,896]{1,0:T(8,128)(2,1)S(1)}, u32[]{:S(2)}, u32[]{:S(2)}) collective-permute-start(bf16[64,896]{1,0:T(8,128)(2,1)S(1)} %collective-permute-done.1.near), channel_id=1, source_target_pairs={{0,1},{1,0},{2,3},{3,2},{4,5},{5,4},{6,7},{7,6},{8,9},{9,8},{10,11... | collective-permute-start | bytes 344072 | tf_op jit(solution)/shard_map/ppermute | solution.py:288
  16.6 2.0 %collective-permute-start.8 = (bf16[32,896]{1,0:T(8,128)(2,1)S(1)}, bf16[32,896]{1,0:T(8,128)(2,1)S(1)}, u32[]{:S(2)}, u32[]{:S(2)}) collective-permute-start(bf16[32,896]{1,0:T(8,128)(2,1)S(1)} %collective-permute-done.6.cross_a), channel_id=1, source_target_pairs={{0,1},{1,0},{2,3},{3,2},{4,5},{5,4},{6,7},{7,6},{8,9},{9,8},{10,11... | collective-permute-start | bytes 172040 | tf_op jit(solution)/shard_map/ppermute | solution.py:288
  16.8 2.4 %collective-permute-start.5 = (bf16[64,896]{1,0:T(8,128)(2,1)S(1)}, bf16[64,896]{1,0:T(8,128)(2,1)S(1)}, u32[]{:S(2)}, u32[]{:S(2)}) collective-permute-start(bf16[64,896]{1,0:T(8,128)(2,1)S(1)} %constant_dynamic-update-slice_fusion.far), channel_id=1, source_target_pairs={{0,1},{1,0},{2,3},{3,2},{4,5},{5,4},{6,7},{7,6},{8,9},{9,8},{10,11... | collective-permute-start | bytes 344072 | tf_op jit(solution)/shard_map/ppermute | solution.py:288
  18.6 1.2 %collective-permute-start.9 = (bf16[32,896]{1,0:T(8,128)(2,1)S(1)}, bf16[32,896]{1,0:T(8,128)(2,1)S(1)}, u32[]{:S(2)}, u32[]{:S(2)}) collective-permute-start(bf16[32,896]{1,0:T(8,128)(2,1)S(1)} %collective-permute-done.7.cross_b), channel_id=1, source_target_pairs={{0,1},{1,0},{2,3},{3,2},{4,5},{5,4},{6,7},{7,6},{8,9},{9,8},{10,11... | collective-permute-start | bytes 172040 | tf_op jit(solution)/shard_map/ppermute | solution.py:288

commit v7 on v6

--- a/solution.py
+++ b/solution.py
@@ -280,6 +280,10 @@
         pairs = [(2 * c + 1, 2 * (c ^ mask1) + 1) for c in range(8)] + [(2 * c, 2 * (c ^ mask0)) for c in range(8)]
         return lambda a: lax.ppermute(a, ("chan", "pair"), pairs)
 
+    def cross_move(mask1, mask0):
+        pairs = [(2 * c, 2 * (c ^ mask1) + 1) for c in range(8)] + [(2 * c + 1, 2 * (c ^ mask0)) for c in range(8)]
+        return lambda a: lax.ppermute(a, ("chan", "pair"), pairs)
+
     def forward(a):
         pairs = [(2 * c + p, 2 * (c ^ 1) + 1 - p) for c in range(8) for p in range(2)]
         return lax.ppermute(a, ("chan", "pair"), pairs)
@@ -287,9 +291,9 @@
     def swap(a):
         return lax.ppermute(a, "pair", [(0, 1), (1, 0)])
 
-    far_a = split_move(6, 4)(first)
-    far_b = split_move(6, 4)(second)
-    side = split_move(1, 1)(own)
+    far_a = cross_move(6, 4)(first)
+    far_b = cross_move(6, 4)(second)
+    side = forward(own)
     near = split_move(3, 2)(own)
     cross_a = forward(far_a)
     cross_b = forward(far_b)

time: 21.1 us -> 21.1 us (level)
  starting transfers between devices: 9.71 us -> 10.8 us
  waiting for transfers between devices: 5.45 us -> 4.37 us
    ppermute x4 -> x1, starting transfers between devices: 7.5 us -> 0.01 us  [split_move(): return lambda a: lax.ppermute(a, ('chan', 'pair'), pairs)]
    ppermute x0 -> x2, starting transfers between devices: none -> 5.15 us  [cross_move(): return lambda a: lax.ppermute(a, ('chan', 'pair'), pairs)]
    ppermute x2 -> x3, starting transfers between devices: 0.74 us -> 4.47 us  [forward(): return lax.ppermute(a, ('chan', 'pair'), pairs)]
    ppermute x4 -> x1, waiting for transfers between devices: 2.81 us -> 0.53 us  [split_move(): return lambda a: lax.ppermute(a, ('chan', 'pair'), pairs)]
    ppermute x0 -> x2, waiting for transfers between devices: none -> 1.35 us  [cross_move(): return lambda a: lax.ppermute(a, ('chan', 'pair'), pairs)]
    ppermute x4, starting transfers between devices: 1.46 us -> 1.16 us  [swap(): return lax.ppermute(a, 'pair', [(0, 1), (1, 0)])]
    ppermute x2 -> x3, waiting for transfers between devices: 1.91 us -> 1.76 us  [forward(): return lax.ppermute(a, ('chan', 'pair'), pairs)]
  transfers between devices with their start and end apart: 10 -> 10, of which waited for: 6 -> 5; matrix products, arithmetic and copies ran while one was open for 0% -> 0% of each run, Pallas kernels for 2% -> 2%
where the time goes in v7:
time: 21.1 us; the launch traced here: 20.9 us
  starting transfers between devices  10.8 us (51%)
  Pallas kernels  5.74 us (27%)
  waiting for transfers between devices  4.37 us (21%)
    ppermute x2, starting transfers between devices, cross_move(): return lambda a: lax.ppermute(a, ('chan', 'pair'), pairs)  5.15 us
    ppermute x3, starting transfers between devices, forward(): return lax.ppermute(a, ('chan', 'pair'), pairs)  4.47 us
    pallas_call x1, Pallas kernels, spectra(): pl.pallas_call(functools.partial(spectra_kernel, lag_share), out_shape=[p...  4.28 us
    ppermute x3, waiting for transfers between devices, forward(): return lax.ppermute(a, ('chan', 'pair'), pairs)  1.76 us
    ppermute x2, waiting for transfers between devices, cross_move(): return lambda a: lax.ppermute(a, ('chan', 'pair'), pairs)  1.35 us
    ppermute x4, starting transfers between devices, swap(): return lax.ppermute(a, 'pair', [(0, 1), (1, 0)])  1.16 us
    pallas_call x1, Pallas kernels, exchange_eight(): pl.pallas_call(late_kernel, out_shape=jax.ShapeDtypeStruct((lag_share, ro...  1.07 us
    ppermute x4, waiting for transfers between devices, swap(): return lax.ppermute(a, 'pair', [(0, 1), (1, 0)])  0.72 us
  transfers between devices with their start and end apart: 10, of which 5 were waited for; matrix products, arithmetic and copies ran while one was open for 0% of the time, Pallas kernels for 2%

profile of v7, /device:TPU:0, one launch (start us, length us, event | category | flops | bytes accessed | tf_op | source)
XLA Modules:
  0.0 20.9 jit_solution(5313577241138585498)
XLA Ops:
  0.0 4.3 %spectra.1 = (bf16[64,896]{1,0:T(8,128)(2,1)S(1)}, bf16[32,896]{1,0:T(8,128)(2,1)S(1)}, bf16[32,896]{1,0:T(8,128)(2,1)S(1)}, bf16[192,896]{1,0:T(8,128)(2,1)S(1)}) custom-call(s32[8]{0:T(128)} %count_ref.1, s32[1,64]{1,0:T(1,128)} %index_ref.1, bf16[64,12000]{1,0:T(8,128)(2,1)} %bitcast.1, bf16[3072,1024]{1,0:T(8,128)(2,1)} %constant.5.clone.table_ref, ...), custom_call_target="tpu_custom_call" | custom-call | flops 1207959552 | bytes 7827456 | tf_op jit(solution)/shard_map/spectra/pallas_call | solution.py:199
  4.3 4.5 %collective-permute-start.3 = (bf16[32,896]{1,0:T(8,128)(2,1)S(1)}, bf16[32,896]{1,0:T(8,128)(2,1)S(1)}, u32[]{:S(2)}, u32[]{:S(2)}) collective-permute-start(bf16[32,896]{1,0:T(8,128)(2,1)S(1)} %get-tuple-element.13), channel_id=1, source_target_pairs={{0,13},{2,15},{4,9},{6,11},{8,5},{10,7},{12,1},{14,3},{1,8},{3,10}... | collective-permute-start | bytes 172040 | tf_op jit(solution)/shard_map/ppermute | solution.py:285
  8.8 0.6 %collective-permute-start.4 = (bf16[32,896]{1,0:T(8,128)(2,1)S(1)}, bf16[32,896]{1,0:T(8,128)(2,1)S(1)}, u32[]{:S(2)}, u32[]{:S(2)}) collective-permute-start(bf16[32,896]{1,0:T(8,128)(2,1)S(1)} %get-tuple-element.14), channel_id=1, source_target_pairs={{0,13},{2,15},{4,9},{6,11},{8,5},{10,7},{12,1},{14,3},{1,8},{3,10}... | collective-permute-start | bytes 172040 | tf_op jit(solution)/shard_map/ppermute | solution.py:285
  9.4 0.0 collective-permute-start.1
  9.4 1.5 %collective-permute-start = (bf16[64,896]{1,0:T(8,128)(2,1)S(1)}, bf16[64,896]{1,0:T(8,128)(2,1)S(1)}, u32[]{:S(2)}, u32[]{:S(2)}) collective-permute-start(bf16[64,896]{1,0:T(8,128)(2,1)S(1)} %get-tuple-element.12.own), channel_id=1, source_target_pairs={{0,3},{1,2},{2,1},{3,0},{4,7},{5,6},{6,5},{7,4},{8,11},{9,10},{10,... | collective-permute-start | bytes 344072 | tf_op jit(solution)/shard_map/ppermute | solution.py:289
  10.9 0.0 collective-permute-done.3
  10.9 2.2 %collective-permute-start.6 = (bf16[32,896]{1,0:T(8,128)(2,1)S(1)}, bf16[32,896]{1,0:T(8,128)(2,1)S(1)}, u32[]{:S(2)}, u32[]{:S(2)}) collective-permute-start(bf16[32,896]{1,0:T(8,128)(2,1)S(1)} %collective-permute-done.3), channel_id=1, source_target_pairs={{0,3},{1,2},{2,1},{3,0},{4,7},{5,6},{6,5},{7,4},{8,11},{9,10},{10,... | collective-permute-start | bytes 172040 | tf_op jit(solution)/shard_map/ppermute | solution.py:289
  13.2 1.3 %collective-permute-done.4 = bf16[32,896]{1,0:T(8,128)(2,1)S(1)} collective-permute-done((bf16[32,896]{1,0:T(8,128)(2,1)S(1)}, bf16[32,896]{1,0:T(8,128)(2,1)S(1)}, u32[]{:S(2)}, u32[]{:S(2)}) %collective-permute-start.4) | collective-permute-done | bytes 57376 | tf_op jit(solution)/shard_map/ppermute | solution.py:285
  14.5 0.7 %collective-permute-start.7 = (bf16[32,896]{1,0:T(8,128)(2,1)S(1)}, bf16[32,896]{1,0:T(8,128)(2,1)S(1)}, u32[]{:S(2)}, u32[]{:S(2)}) collective-permute-start(bf16[32,896]{1,0:T(8,128)(2,1)S(1)} %collective-permute-done.4), channel_id=1, source_target_pairs={{0,3},{1,2},{2,1},{3,0},{4,7},{5,6},{6,5},{7,4},{8,11},{9,10},{10,... | collective-permute-start | bytes 172040 | tf_op jit(solution)/shard_map/ppermute | solution.py:289
  15.3 0.5 %collective-permute-done.1.near = bf16[64,896]{1,0:T(8,128)(2,1)S(1)} collective-permute-done((bf16[64,896]{1,0:T(8,128)(2,1)S(1)}, bf16[64,896]{1,0:T(8,128)(2,1)S(1)}, u32[]{:S(2)}, u32[]{:S(2)}) %collective-permute-start.1) | collective-permute-done | bytes 114720 | tf_op jit(solution)/shard_map/ppermute | solution.py:281
  15.8 0.5 %collective-permute-start.2 = (bf16[64,896]{1,0:T(8,128)(2,1)S(1)}, bf16[64,896]{1,0:T(8,128)(2,1)S(1)}, u32[]{:S(2)}, u32[]{:S(2)}) collective-permute-start(bf16[64,896]{1,0:T(8,128)(2,1)S(1)} %collective-permute-done.1.near), channel_id=1, source_target_pairs={{0,1},{1,0},{2,3},{3,2},{4,5},{5,4},{6,7},{7,6},{8,9},{9,8},{10,11... | collective-permute-start | bytes 344072 | tf_op jit(solution)/shard_map/ppermute | solution.py:292
  16.3 0.3 %collective-permute-done.6.cross_a = bf16[32,896]{1,0:T(8,128)(2,1)S(1)} collective-permute-done((bf16[32,896]{1,0:T(8,128)(2,1)S(1)}, bf16[32,896]{1,0:T(8,128)(2,1)S(1)}, u32[]{:S(2)}, u32[]{:S(2)}) %collective-permute-start.6) | collective-permute-done | bytes 57376 | tf_op jit(solution)/shard_map/ppermute | solution.py:289
  16.6 0.4 %collective-permute-start.8 = (bf16[32,896]{1,0:T(8,128)(2,1)S(1)}, bf16[32,896]{1,0:T(8,128)(2,1)S(1)}, u32[]{:S(2)}, u32[]{:S(2)}) collective-permute-start(bf16[32,896]{1,0:T(8,128)(2,1)S(1)} %collective-permute-done.6.cross_a), channel_id=1, source_target_pairs={{0,1},{1,0},{2,3},{3,2},{4,5},{5,4},{6,7},{7,6},{8,9},{9,8},{10,11... | collective-permute-start | bytes 172040 | tf_op jit(solution)/shard_map/ppermute | solution.py:292
  17.0 0.2 collective-permute-start.5
  17.2 1.4 %collective-permute-done.7.cross_b = bf16[32,896]{1,0:T(8,128)(2,1)S(1)} collective-permute-done((bf16[32,896]{1,0:T(8,128)(2,1)S(1)}, bf16[32,896]{1,0:T(8,128)(2,1)S(1)}, u32[]{:S(2)}, u32[]{:S(2)}) %collective-permute-start.7) | collective-permute-done | bytes 57376 | tf_op jit(solution)/shard_map/ppermute | solution.py:289
  18.6 0.0 collective-permute-done.8.cross_swap_a
  18.6 0.1 collective-permute-start.9
  18.7 0.0 collective-permute-done.side
  18.7 0.0 collective-permute-done.2.near_swap
  18.7 0.4 %correlate_early.1.early = bf16[2,192,128]{2,1,0:T(8,128)(2,1)S(1)} custom-call(bf16[192,896]{1,0:T(8,128)(2,1)S(1)} %get-tuple-element.11.lags, bf16[64,896]{1,0:T(8,128)(2,1)S(1)} %get-tuple-element.12.own, bf16[64,896]{1,0:T(8,128)(2,1)S(1)} %collective-permute-done.side, bf16[64,896]{1,0:T(8,128)(2,1)S(1)} %collective-permute-done.1.near, ...), custom_call_target="tpu_custom_call" | custom-call | flops 88080384 | bytes 917504 | tf_op jit(solution)/shard_map/correlate_early/pallas_call | solution.py:307
  19.1 0.0 collective-permute-done.5.far_swap
  19.1 0.7 %collective-permute-done.9.cross_swap_b = bf16[32,896]{1,0:T(8,128)(2,1)S(1)} collective-permute-done((bf16[32,896]{1,0:T(8,128)(2,1)S(1)}, bf16[32,896]{1,0:T(8,128)(2,1)S(1)}, u32[]{:S(2)}, u32[]{:S(2)}) %collective-permute-start.9) | collective-permute-done | bytes 57376 | tf_op jit(solution)/shard_map/ppermute | solution.py:292
  19.9 1.1 %correlate_late.1 = bf16[3,64,512]{2,1,0:T(8,128)(2,1)} custom-call(bf16[192,896]{1,0:T(8,128)(2,1)S(1)} %get-tuple-element.11.lags, bf16[2,192,128]{2,1,0:T(8,128)(2,1)S(1)} %correlate_early.1.early, bf16[64,896]{1,0:T(8,128)(2,1)S(1)} %constant_dynamic-update-slice_fusion.far, bf16[64,896]{1,0:T(8,128)(2,1)S(1)} %collective-permute-done.5.far_swap, ...), custom_call_target="tpu_custom_call" | custom-call | flops 88080384 | bytes 917504 | tf_op jit(solution)/shard_map/correlate_late/pallas_call | solution.py:318
  (2 shorter events, 0.0 us)
Async XLA Ops:
  4.3 6.6 %collective-permute-start.3 = (bf16[32,896]{1,0:T(8,128)(2,1)S(1)}, bf16[32,896]{1,0:T(8,128)(2,1)S(1)}, u32[]{:S(2)}, u32[]{:S(2)}) collective-permute-start(bf16[32,896]{1,0:T(8,128)(2,1)S(1)} %get-tuple-element.13), channel_id=1, source_target_pairs={{0,13},{2,15},{4,9},{6,11},{8,5},{10,7},{12,1},{14,3},{1,8},{3,10}... | collective-permute-start | bytes 172040 | tf_op jit(solution)/shard_map/ppermute | solution.py:285
  8.8 5.7 %collective-permute-start.4 = (bf16[32,896]{1,0:T(8,128)(2,1)S(1)}, bf16[32,896]{1,0:T(8,128)(2,1)S(1)}, u32[]{:S(2)}, u32[]{:S(2)}) collective-permute-start(bf16[32,896]{1,0:T(8,128)(2,1)S(1)} %get-tuple-element.14), channel_id=1, source_target_pairs={{0,13},{2,15},{4,9},{6,11},{8,5},{10,7},{12,1},{14,3},{1,8},{3,10}... | collective-permute-start | bytes 172040 | tf_op jit(solution)/shard_map/ppermute | solution.py:285
  9.4 6.4 %collective-permute-start.1 = (bf16[64,896]{1,0:T(8,128)(2,1)S(1)}, bf16[64,896]{1,0:T(8,128)(2,1)S(1)}, u32[]{:S(2)}, u32[]{:S(2)}) collective-permute-start(bf16[64,896]{1,0:T(8,128)(2,1)S(1)} %get-tuple-element.12.own), channel_id=1, source_target_pairs={{1,7},{3,5},{5,3},{7,1},{9,15},{11,13},{13,11},{15,9},{0,4},{2,6},... | collective-permute-start | bytes 344072 | tf_op jit(solution)/shard_map/ppermute | solution.py:281
  9.4 9.3 %collective-permute-start = (bf16[64,896]{1,0:T(8,128)(2,1)S(1)}, bf16[64,896]{1,0:T(8,128)(2,1)S(1)}, u32[]{:S(2)}, u32[]{:S(2)}) collective-permute-start(bf16[64,896]{1,0:T(8,128)(2,1)S(1)} %get-tuple-element.12.own), channel_id=1, source_target_pairs={{0,3},{1,2},{2,1},{3,0},{4,7},{5,6},{6,5},{7,4},{8,11},{9,10},{10,... | collective-permute-start | bytes 344072 | tf_op jit(solution)/shard_map/ppermute | solution.py:289
  10.9 5.7 %collective-permute-start.6 = (bf16[32,896]{1,0:T(8,128)(2,1)S(1)}, bf16[32,896]{1,0:T(8,128)(2,1)S(1)}, u32[]{:S(2)}, u32[]{:S(2)}) collective-permute-start(bf16[32,896]{1,0:T(8,128)(2,1)S(1)} %collective-permute-done.3), channel_id=1, source_target_pairs={{0,3},{1,2},{2,1},{3,0},{4,7},{5,6},{6,5},{7,4},{8,11},{9,10},{10,... | collective-permute-start | bytes 172040 | tf_op jit(solution)/shard_map/ppermute | solution.py:289
  14.5 4.1 %collective-permute-start.7 = (bf16[32,896]{1,0:T(8,128)(2,1)S(1)}, bf16[32,896]{1,0:T(8,128)(2,1)S(1)}, u32[]{:S(2)}, u32[]{:S(2)}) collective-permute-start(bf16[32,896]{1,0:T(8,128)(2,1)S(1)} %collective-permute-done.4), channel_id=1, source_target_pairs={{0,3},{1,2},{2,1},{3,0},{4,7},{5,6},{6,5},{7,4},{8,11},{9,10},{10,... | collective-permute-start | bytes 172040 | tf_op jit(solution)/shard_map/ppermute | solution.py:289
  15.8 2.9 %collective-permute-start.2 = (bf16[64,896]{1,0:T(8,128)(2,1)S(1)}, bf16[64,896]{1,0:T(8,128)(2,1)S(1)}, u32[]{:S(2)}, u32[]{:S(2)}) collective-permute-start(bf16[64,896]{1,0:T(8,128)(2,1)S(1)} %collective-permute-done.1.near), channel_id=1, source_target_pairs={{0,1},{1,0},{2,3},{3,2},{4,5},{5,4},{6,7},{7,6},{8,9},{9,8},{10,11... | collective-permute-start | bytes 344072 | tf_op jit(solution)/shard_map/ppermute | solution.py:292
  16.6 2.0 %collective-permute-start.8 = (bf16[32,896]{1,0:T(8,128)(2,1)S(1)}, bf16[32,896]{1,0:T(8,128)(2,1)S(1)}, u32[]{:S(2)}, u32[]{:S(2)}) collective-permute-start(bf16[32,896]{1,0:T(8,128)(2,1)S(1)} %collective-permute-done.6.cross_a), channel_id=1, source_target_pairs={{0,1},{1,0},{2,3},{3,2},{4,5},{5,4},{6,7},{7,6},{8,9},{9,8},{10,11... | collective-permute-start | bytes 172040 | tf_op jit(solution)/shard_map/ppermute | solution.py:292
  17.0 2.1 %collective-permute-start.5 = (bf16[64,896]{1,0:T(8,128)(2,1)S(1)}, bf16[64,896]{1,0:T(8,128)(2,1)S(1)}, u32[]{:S(2)}, u32[]{:S(2)}) collective-permute-start(bf16[64,896]{1,0:T(8,128)(2,1)S(1)} %constant_dynamic-update-slice_fusion.far), channel_id=1, source_target_pairs={{0,1},{1,0},{2,3},{3,2},{4,5},{5,4},{6,7},{7,6},{8,9},{9,8},{10,11... | collective-permute-start | bytes 344072 | tf_op jit(solution)/shard_map/ppermute | solution.py:292
  18.6 1.2 %collective-permute-start.9 = (bf16[32,896]{1,0:T(8,128)(2,1)S(1)}, bf16[32,896]{1,0:T(8,128)(2,1)S(1)}, u32[]{:S(2)}, u32[]{:S(2)}) collective-permute-start(bf16[32,896]{1,0:T(8,128)(2,1)S(1)} %collective-permute-done.7.cross_b), channel_id=1, source_target_pairs={{0,1},{1,0},{2,3},{3,2},{4,5},{5,4},{6,7},{7,6},{8,9},{9,8},{10,11... | collective-permute-start | bytes 172040 | tf_op jit(solution)/shard_map/ppermute | solution.py:292

commit v8 on v7

--- a/solution.py
+++ b/solution.py
@@ -73,7 +73,6 @@
 
 
 def spectra_kernel(
-    lag_share,
     count_ref,
     index_ref,
     raw_ref,
@@ -82,7 +81,7 @@
     out_ref,
     first_ref,
     second_ref,
-    lag_ref,
+    weights,
     x,
     tail,
     table,
@@ -91,7 +90,6 @@
     y_odd,
     counts,
     index,
-    weights,
     small_sems,
     sems,
 ):
@@ -189,20 +187,18 @@
     first_ref[...] = narrow[: rows // 2]
     second_ref[...] = narrow[rows // 2 :]
     weight_copy.wait()
-    for lag in range(lag_share):
-        lag_ref[lag * rows : (lag + 1) * rows, :] = (own * weights[lag : lag + 1, :]).astype(jnp.bfloat16)
 
 
 def spectra(raw_rows, index_row, live_count, table, weights):
     rows = raw_rows.shape[0]
     lag_share = weights.shape[1]
     return pl.pallas_call(
-        functools.partial(spectra_kernel, lag_share),
+        spectra_kernel,
         out_shape=[
             pltpu.VMEM((rows, WIDTH), jnp.bfloat16),
             pltpu.VMEM((rows // 2, WIDTH), jnp.bfloat16),
             pltpu.VMEM((rows // 2, WIDTH), jnp.bfloat16),
-            pltpu.VMEM((lag_share * rows, WIDTH), jnp.bfloat16),
+            pltpu.VMEM((lag_share, WIDTH), jnp.float32),
         ],
         in_specs=[pl.BlockSpec(memory_space=pltpu.HBM)] * 5,
         out_specs=[pl.BlockSpec(memory_space=pltpu.VMEM)] * 4,
@@ -215,7 +211,6 @@
             pltpu.VMEM((4 * rows, DEPTH), jnp.bfloat16),
             pltpu.SMEM(live_count.shape, jnp.int32),
             pltpu.VMEM(index_row.shape, jnp.int32),
-            pltpu.VMEM(weights.shape[1:], jnp.float32),
             pltpu.SemaphoreType.DMA((3,)),
             pltpu.SemaphoreType.DMA((1 + len(GROUPS),)),
         ],
@@ -247,7 +242,11 @@
     return [jnp.where(x == 0, p, pltpu.roll(p, rows, axis=1)).astype(jnp.bfloat16) for p in products]
 
 
-def early_kernel(lags, own, side, near, near_swap, out):
+def early_kernel(weights, own, side, near, near_swap, out, lags):
+    rows = own.shape[0]
+    wide = own[...].astype(jnp.float32)
+    for lag in range(weights.shape[0]):
+        lags[lag * rows : (lag + 1) * rows, :] = (wide * weights[lag : lag + 1, :]).astype(jnp.bfloat16)
     x = lax.axis_index("chan") % 2
     upper = lax.axis_index("pair") == 1
     nearest = (
@@ -275,7 +274,7 @@
     put(out, second, z ^ (3 - core), rows)
 
 
-def exchange_eight(own, first, second, lags):
+def exchange_eight(own, first, second, own_weights):
     def split_move(mask1, mask0):
         pairs = [(2 * c + 1, 2 * (c ^ mask1) + 1) for c in range(8)] + [(2 * c, 2 * (c ^ mask0)) for c in range(8)]
         return lambda a: lax.ppermute(a, ("chan", "pair"), pairs)
@@ -303,18 +302,21 @@
     far_swap = swap(far)
     near_swap = swap(near)
     cross_swap_b = swap(cross_b)
-    lag_share, rows = lags.shape[0] // own.shape[0], own.shape[0]
-    early = pl.pallas_call(
+    lag_share, rows = own_weights.shape[0], own.shape[0]
+    early, lags = pl.pallas_call(
         early_kernel,
-        out_shape=pltpu.VMEM((2, lag_share * rows, 2 * rows), jnp.bfloat16),
+        out_shape=[
+            pltpu.VMEM((2, lag_share * rows, 2 * rows), jnp.bfloat16),
+            pltpu.VMEM((lag_share * rows, WIDTH), jnp.bfloat16),
+        ],
         in_specs=[pl.BlockSpec(memory_space=pltpu.VMEM)] * 5,
-        out_specs=pl.BlockSpec(memory_space=pltpu.VMEM),
+        out_specs=[pl.BlockSpec(memory_space=pltpu.VMEM)] * 2,
         compiler_params=pltpu.CompilerParams(vmem_limit_bytes=CORR_KIB * 1024),
         cost_estimate=pl.CostEstimate(
             flops=2 * lag_share * rows * 4 * rows * WIDTH, bytes_accessed=8 * rows * WIDTH * 2, transcendentals=0
         ),
         name="correlate_early",
-    )(lags, own, side, near, near_swap)
+    )(own_weights, own, side, near, near_swap)
     return pl.pallas_call(
         late_kernel,
         out_shape=jax.ShapeDtypeStruct((lag_share, rows, 8 * rows), jnp.bfloat16),
@@ -331,7 +333,7 @@
 def shards(table, weights, raw, live_index, live_count):
     slot_count, seg_count, samples = raw.shape
     pairs = lax.axis_size("pair")
-    own, first, second, lags = spectra(
+    own, first, second, own_weights = spectra(
         raw.reshape(slot_count * seg_count, samples),
         live_index,
         live_count,
@@ -339,7 +341,8 @@
         weights.reshape(pairs, L // pairs, WIDTH),
     )
     if lax.axis_size("chan") == 8 and pairs == 2 and slot_count == 64:
-        return exchange_eight(own, first, second, lags)
+        return exchange_eight(own, first, second, own_weights)
+    lags = (own.astype(jnp.float32)[None] * own_weights[:, None, :]).astype(jnp.bfloat16).reshape(-1, WIDTH)
     product = correlate(lags, lax.all_gather(own, "chan", axis=0, tiled=True))
     return product.reshape(L // pairs, slot_count, -1)
 

time: 21.1 us -> 21 us (level)
  no operation moved by 1% of the time
where the time goes in v8:
time: 21 us; the launch traced here: 20.9 us
  starting transfers between devices  10.8 us (51%)
  Pallas kernels  5.71 us (27%)
  waiting for transfers between devices  4.36 us (21%)
    ppermute x2, starting transfers between devices, cross_move(): return lambda a: lax.ppermute(a, ('chan', 'pair'), pairs)  5.15 us
    ppermute x3, starting transfers between devices, forward(): return lax.ppermute(a, ('chan', 'pair'), pairs)  4.47 us
    pallas_call x1, Pallas kernels, spectra(): pl.pallas_call(spectra_kernel, out_shape=[pltpu.VMEM((rows, WIDTH), jnp.b...  4.24 us
    ppermute x3, waiting for transfers between devices, forward(): return lax.ppermute(a, ('chan', 'pair'), pairs)  1.77 us
    ppermute x2, waiting for transfers between devices, cross_move(): return lambda a: lax.ppermute(a, ('chan', 'pair'), pairs)  1.34 us
    ppermute x4, starting transfers between devices, swap(): return lax.ppermute(a, 'pair', [(0, 1), (1, 0)])  1.16 us
    pallas_call x1, Pallas kernels, exchange_eight(): pl.pallas_call(late_kernel, out_shape=jax.ShapeDtypeStruct((lag_share, ro...  1.08 us
    ppermute x4, waiting for transfers between devices, swap(): return lax.ppermute(a, 'pair', [(0, 1), (1, 0)])  0.71 us
  transfers between devices with their start and end apart: 10, of which 5 were waited for; matrix products, arithmetic and copies ran while one was open for 0% of the time, Pallas kernels for 2%

profile of v8, /device:TPU:0, one launch (start us, length us, event | category | flops | bytes accessed | tf_op | source)
XLA Modules:
  0.0 20.9 jit_solution(17102841114021948236)
XLA Ops:
  0.0 4.2 %spectra.1 = (bf16[64,896]{1,0:T(8,128)(2,1)S(1)}, bf16[32,896]{1,0:T(8,128)(2,1)S(1)}, bf16[32,896]{1,0:T(8,128)(2,1)S(1)}, f32[3,896]{1,0:T(4,128)S(1)}) custom-call(s32[8]{0:T(128)} %count_ref.1, s32[1,64]{1,0:T(1,128)} %index_ref.1, bf16[64,12000]{1,0:T(8,128)(2,1)} %bitcast.1, bf16[3072,1024]{1,0:T(8,128)(2,1)} %constant.5.clone.table_ref, ...), custom_call_target="tpu_custom_call" | custom-call | flops 1207959552 | bytes 7827456 | tf_op jit(solution)/shard_map/spectra/pallas_call | solution.py:195
  4.2 4.5 %collective-permute-start.3 = (bf16[32,896]{1,0:T(8,128)(2,1)S(1)}, bf16[32,896]{1,0:T(8,128)(2,1)S(1)}, u32[]{:S(2)}, u32[]{:S(2)}) collective-permute-start(bf16[32,896]{1,0:T(8,128)(2,1)S(1)} %get-tuple-element.17), channel_id=1, source_target_pairs={{0,13},{2,15},{4,9},{6,11},{8,5},{10,7},{12,1},{14,3},{1,8},{3,10}... | collective-permute-start | bytes 172040 | tf_op jit(solution)/shard_map/ppermute | solution.py:284
  8.8 0.6 %collective-permute-start.4 = (bf16[32,896]{1,0:T(8,128)(2,1)S(1)}, bf16[32,896]{1,0:T(8,128)(2,1)S(1)}, u32[]{:S(2)}, u32[]{:S(2)}) collective-permute-start(bf16[32,896]{1,0:T(8,128)(2,1)S(1)} %get-tuple-element.18), channel_id=1, source_target_pairs={{0,13},{2,15},{4,9},{6,11},{8,5},{10,7},{12,1},{14,3},{1,8},{3,10}... | collective-permute-start | bytes 172040 | tf_op jit(solution)/shard_map/ppermute | solution.py:284
  9.4 0.0 collective-permute-start.1
  9.4 1.5 %collective-permute-start = (bf16[64,896]{1,0:T(8,128)(2,1)S(1)}, bf16[64,896]{1,0:T(8,128)(2,1)S(1)}, u32[]{:S(2)}, u32[]{:S(2)}) collective-permute-start(bf16[64,896]{1,0:T(8,128)(2,1)S(1)} %get-tuple-element.14.own), channel_id=1, source_target_pairs={{0,3},{1,2},{2,1},{3,0},{4,7},{5,6},{6,5},{7,4},{8,11},{9,10},{10,... | collective-permute-start | bytes 344072 | tf_op jit(solution)/shard_map/ppermute | solution.py:288
  10.9 0.0 collective-permute-done.3
  10.9 2.3 %collective-permute-start.6 = (bf16[32,896]{1,0:T(8,128)(2,1)S(1)}, bf16[32,896]{1,0:T(8,128)(2,1)S(1)}, u32[]{:S(2)}, u32[]{:S(2)}) collective-permute-start(bf16[32,896]{1,0:T(8,128)(2,1)S(1)} %collective-permute-done.3), channel_id=1, source_target_pairs={{0,3},{1,2},{2,1},{3,0},{4,7},{5,6},{6,5},{7,4},{8,11},{9,10},{10,... | collective-permute-start | bytes 172040 | tf_op jit(solution)/shard_map/ppermute | solution.py:288
  13.1 1.3 %collective-permute-done.4 = bf16[32,896]{1,0:T(8,128)(2,1)S(1)} collective-permute-done((bf16[32,896]{1,0:T(8,128)(2,1)S(1)}, bf16[32,896]{1,0:T(8,128)(2,1)S(1)}, u32[]{:S(2)}, u32[]{:S(2)}) %collective-permute-start.4) | collective-permute-done | bytes 57376 | tf_op jit(solution)/shard_map/ppermute | solution.py:284
  14.5 0.7 %collective-permute-start.7 = (bf16[32,896]{1,0:T(8,128)(2,1)S(1)}, bf16[32,896]{1,0:T(8,128)(2,1)S(1)}, u32[]{:S(2)}, u32[]{:S(2)}) collective-permute-start(bf16[32,896]{1,0:T(8,128)(2,1)S(1)} %collective-permute-done.4), channel_id=1, source_target_pairs={{0,3},{1,2},{2,1},{3,0},{4,7},{5,6},{6,5},{7,4},{8,11},{9,10},{10,... | collective-permute-start | bytes 172040 | tf_op jit(solution)/shard_map/ppermute | solution.py:288
  15.2 0.5 %collective-permute-done.1.near = bf16[64,896]{1,0:T(8,128)(2,1)S(1)} collective-permute-done((bf16[64,896]{1,0:T(8,128)(2,1)S(1)}, bf16[64,896]{1,0:T(8,128)(2,1)S(1)}, u32[]{:S(2)}, u32[]{:S(2)}) %collective-permute-start.1) | collective-permute-done | bytes 114720 | tf_op jit(solution)/shard_map/ppermute | solution.py:280
  15.8 0.5 %collective-permute-start.2 = (bf16[64,896]{1,0:T(8,128)(2,1)S(1)}, bf16[64,896]{1,0:T(8,128)(2,1)S(1)}, u32[]{:S(2)}, u32[]{:S(2)}) collective-permute-start(bf16[64,896]{1,0:T(8,128)(2,1)S(1)} %collective-permute-done.1.near), channel_id=1, source_target_pairs={{0,1},{1,0},{2,3},{3,2},{4,5},{5,4},{6,7},{7,6},{8,9},{9,8},{10,11... | collective-permute-start | bytes 344072 | tf_op jit(solution)/shard_map/ppermute | solution.py:291
  16.2 0.3 %collective-permute-done.6.cross_a = bf16[32,896]{1,0:T(8,128)(2,1)S(1)} collective-permute-done((bf16[32,896]{1,0:T(8,128)(2,1)S(1)}, bf16[32,896]{1,0:T(8,128)(2,1)S(1)}, u32[]{:S(2)}, u32[]{:S(2)}) %collective-permute-start.6) | collective-permute-done | bytes 57376 | tf_op jit(solution)/shard_map/ppermute | solution.py:288
  16.5 0.4 %collective-permute-start.8 = (bf16[32,896]{1,0:T(8,128)(2,1)S(1)}, bf16[32,896]{1,0:T(8,128)(2,1)S(1)}, u32[]{:S(2)}, u32[]{:S(2)}) collective-permute-start(bf16[32,896]{1,0:T(8,128)(2,1)S(1)} %collective-permute-done.6.cross_a), channel_id=1, source_target_pairs={{0,1},{1,0},{2,3},{3,2},{4,5},{5,4},{6,7},{7,6},{8,9},{9,8},{10,11... | collective-permute-start | bytes 172040 | tf_op jit(solution)/shard_map/ppermute | solution.py:291
  16.9 0.2 collective-permute-start.5
  17.1 1.5 %collective-permute-done.7.cross_b = bf16[32,896]{1,0:T(8,128)(2,1)S(1)} collective-permute-done((bf16[32,896]{1,0:T(8,128)(2,1)S(1)}, bf16[32,896]{1,0:T(8,128)(2,1)S(1)}, u32[]{:S(2)}, u32[]{:S(2)}) %collective-permute-start.7) | collective-permute-done | bytes 57376 | tf_op jit(solution)/shard_map/ppermute | solution.py:288
  18.6 0.0 collective-permute-done.8.cross_swap_a
  18.6 0.1 collective-permute-start.9
  18.7 0.0 collective-permute-done.side
  18.7 0.0 collective-permute-done.2.near_swap
  18.7 0.4 %correlate_early.1 = (bf16[2,192,128]{2,1,0:T(8,128)(2,1)S(1)}, bf16[192,896]{1,0:T(8,128)(2,1)S(1)}) custom-call(f32[3,896]{1,0:T(4,128)S(1)} %get-tuple-element.13.weights, bf16[64,896]{1,0:T(8,128)(2,1)S(1)} %get-tuple-element.14.own, bf16[64,896]{1,0:T(8,128)(2,1)S(1)} %collective-permute-done.side, bf16[64,896]{1,0:T(8,128)(2,1)S(1)} %collective-permute-done.1.near, ...), custom_call_target="tpu_custom_call" | custom-call | flops 88080384 | bytes 917504 | tf_op jit(solution)/shard_map/correlate_early/pallas_call | solution.py:306
  19.1 0.0 collective-permute-done.5.far_swap
  19.1 0.7 %collective-permute-done.9.cross_swap_b = bf16[32,896]{1,0:T(8,128)(2,1)S(1)} collective-permute-done((bf16[32,896]{1,0:T(8,128)(2,1)S(1)}, bf16[32,896]{1,0:T(8,128)(2,1)S(1)}, u32[]{:S(2)}, u32[]{:S(2)}) %collective-permute-start.9) | collective-permute-done | bytes 57376 | tf_op jit(solution)/shard_map/ppermute | solution.py:291
  19.8 1.1 %correlate_late.1 = bf16[3,64,512]{2,1,0:T(8,128)(2,1)} custom-call(bf16[192,896]{1,0:T(8,128)(2,1)S(1)} %get-tuple-element.15.lags, bf16[2,192,128]{2,1,0:T(8,128)(2,1)S(1)} %get-tuple-element.16.early, bf16[64,896]{1,0:T(8,128)(2,1)S(1)} %constant_dynamic-update-slice_fusion.far, bf16[64,896]{1,0:T(8,128)(2,1)S(1)} %collective-permute-done.5.far_swap, ...), custom_call_target="tpu_custom_call" | custom-call | flops 88080384 | bytes 917504 | tf_op jit(solution)/shard_map/correlate_late/pallas_call | solution.py:320
  (2 shorter events, 0.0 us)
Async XLA Ops:
  4.2 6.6 %collective-permute-start.3 = (bf16[32,896]{1,0:T(8,128)(2,1)S(1)}, bf16[32,896]{1,0:T(8,128)(2,1)S(1)}, u32[]{:S(2)}, u32[]{:S(2)}) collective-permute-start(bf16[32,896]{1,0:T(8,128)(2,1)S(1)} %get-tuple-element.17), channel_id=1, source_target_pairs={{0,13},{2,15},{4,9},{6,11},{8,5},{10,7},{12,1},{14,3},{1,8},{3,10}... | collective-permute-start | bytes 172040 | tf_op jit(solution)/shard_map/ppermute | solution.py:284
  8.8 5.7 %collective-permute-start.4 = (bf16[32,896]{1,0:T(8,128)(2,1)S(1)}, bf16[32,896]{1,0:T(8,128)(2,1)S(1)}, u32[]{:S(2)}, u32[]{:S(2)}) collective-permute-start(bf16[32,896]{1,0:T(8,128)(2,1)S(1)} %get-tuple-element.18), channel_id=1, source_target_pairs={{0,13},{2,15},{4,9},{6,11},{8,5},{10,7},{12,1},{14,3},{1,8},{3,10}... | collective-permute-start | bytes 172040 | tf_op jit(solution)/shard_map/ppermute | solution.py:284
  9.4 6.4 %collective-permute-start.1 = (bf16[64,896]{1,0:T(8,128)(2,1)S(1)}, bf16[64,896]{1,0:T(8,128)(2,1)S(1)}, u32[]{:S(2)}, u32[]{:S(2)}) collective-permute-start(bf16[64,896]{1,0:T(8,128)(2,1)S(1)} %get-tuple-element.14.own), channel_id=1, source_target_pairs={{1,7},{3,5},{5,3},{7,1},{9,15},{11,13},{13,11},{15,9},{0,4},{2,6},... | collective-permute-start | bytes 344072 | tf_op jit(solution)/shard_map/ppermute | solution.py:280
  9.4 9.3 %collective-permute-start = (bf16[64,896]{1,0:T(8,128)(2,1)S(1)}, bf16[64,896]{1,0:T(8,128)(2,1)S(1)}, u32[]{:S(2)}, u32[]{:S(2)}) collective-permute-start(bf16[64,896]{1,0:T(8,128)(2,1)S(1)} %get-tuple-element.14.own), channel_id=1, source_target_pairs={{0,3},{1,2},{2,1},{3,0},{4,7},{5,6},{6,5},{7,4},{8,11},{9,10},{10,... | collective-permute-start | bytes 344072 | tf_op jit(solution)/shard_map/ppermute | solution.py:288
  10.9 5.7 %collective-permute-start.6 = (bf16[32,896]{1,0:T(8,128)(2,1)S(1)}, bf16[32,896]{1,0:T(8,128)(2,1)S(1)}, u32[]{:S(2)}, u32[]{:S(2)}) collective-permute-start(bf16[32,896]{1,0:T(8,128)(2,1)S(1)} %collective-permute-done.3), channel_id=1, source_target_pairs={{0,3},{1,2},{2,1},{3,0},{4,7},{5,6},{6,5},{7,4},{8,11},{9,10},{10,... | collective-permute-start | bytes 172040 | tf_op jit(solution)/shard_map/ppermute | solution.py:288
  14.5 4.1 %collective-permute-start.7 = (bf16[32,896]{1,0:T(8,128)(2,1)S(1)}, bf16[32,896]{1,0:T(8,128)(2,1)S(1)}, u32[]{:S(2)}, u32[]{:S(2)}) collective-permute-start(bf16[32,896]{1,0:T(8,128)(2,1)S(1)} %collective-permute-done.4), channel_id=1, source_target_pairs={{0,3},{1,2},{2,1},{3,0},{4,7},{5,6},{6,5},{7,4},{8,11},{9,10},{10,... | collective-permute-start | bytes 172040 | tf_op jit(solution)/shard_map/ppermute | solution.py:288
  15.8 3.0 %collective-permute-start.2 = (bf16[64,896]{1,0:T(8,128)(2,1)S(1)}, bf16[64,896]{1,0:T(8,128)(2,1)S(1)}, u32[]{:S(2)}, u32[]{:S(2)}) collective-permute-start(bf16[64,896]{1,0:T(8,128)(2,1)S(1)} %collective-permute-done.1.near), channel_id=1, source_target_pairs={{0,1},{1,0},{2,3},{3,2},{4,5},{5,4},{6,7},{7,6},{8,9},{9,8},{10,11... | collective-permute-start | bytes 344072 | tf_op jit(solution)/shard_map/ppermute | solution.py:291
  16.5 2.0 %collective-permute-start.8 = (bf16[32,896]{1,0:T(8,128)(2,1)S(1)}, bf16[32,896]{1,0:T(8,128)(2,1)S(1)}, u32[]{:S(2)}, u32[]{:S(2)}) collective-permute-start(bf16[32,896]{1,0:T(8,128)(2,1)S(1)} %collective-permute-done.6.cross_a), channel_id=1, source_target_pairs={{0,1},{1,0},{2,3},{3,2},{4,5},{5,4},{6,7},{7,6},{8,9},{9,8},{10,11... | collective-permute-start | bytes 172040 | tf_op jit(solution)/shard_map/ppermute | solution.py:291
  16.9 2.2 %collective-permute-start.5 = (bf16[64,896]{1,0:T(8,128)(2,1)S(1)}, bf16[64,896]{1,0:T(8,128)(2,1)S(1)}, u32[]{:S(2)}, u32[]{:S(2)}) collective-permute-start(bf16[64,896]{1,0:T(8,128)(2,1)S(1)} %constant_dynamic-update-slice_fusion.far), channel_id=1, source_target_pairs={{0,1},{1,0},{2,3},{3,2},{4,5},{5,4},{6,7},{7,6},{8,9},{9,8},{10,11... | collective-permute-start | bytes 344072 | tf_op jit(solution)/shard_map/ppermute | solution.py:291
  18.6 1.2 %collective-permute-start.9 = (bf16[32,896]{1,0:T(8,128)(2,1)S(1)}, bf16[32,896]{1,0:T(8,128)(2,1)S(1)}, u32[]{:S(2)}, u32[]{:S(2)}) collective-permute-start(bf16[32,896]{1,0:T(8,128)(2,1)S(1)} %collective-permute-done.7.cross_b), channel_id=1, source_target_pairs={{0,1},{1,0},{2,3},{3,2},{4,5},{5,4},{6,7},{7,6},{8,9},{9,8},{10,11... | collective-permute-start | bytes 172040 | tf_op jit(solution)/shard_map/ppermute | solution.py:291
